TPU v7x, 128 devices: a whole 4x4x4 slice. The times are simulated.
128 devices in a mesh: wide: 32 (over x, y, core), narrow: 4 (over z).
Axes of the slice: x: 4, y: 4, z: 4, core: 2. Of those that a mesh axis runs over, the one named last changes fastest.
Arguments:
- volume: bfloat16 [16, 2048, 512], P(None, 'wide', 'narrow'), may hold values from -24 to 24
- log_weights: float32 [6], replicated, may hold values from -2 to 2
- means: float32 [6, 48], replicated, may hold values from -2 to 2
- prec_factor: float32 [6, 48, 48], replicated, may hold values from -0.06 to 0.25, as said below
Outputs:
- responsibility: float32 [6, 16, 2048, 512], P(None, None, 'wide', 'narrow')
- new_weights: float32 [6], replicated
- new_means: float32 [6, 48], replicated
- new_cov: float32 [6, 48, 48], replicated
Inputs may be any that keep to these rules, and one draw needn't show every extreme that they name: `prec_factor`: lower triangular with a positive diagonal.
All inputs are finite; a program needn't handle non-finite values.
Results may differ from a plain program's by a relative error of at most 0.00045.
The roundings to bfloat16 on the way count: a program that leaves them out, or rounds other values in their place, can miss the bound.
Values may be sent and summed in bfloat16 or wider, within the bound.
No kernel may reach another device: no remote copies, remote signals or barrier semaphores. Data moves between devices by JAX's collectives and lax.ppermute only.
A program may use at most 128 MiB of HBM per device.

v0:
```python
import math

import jax
import jax.numpy as jnp
from jax import lax
from jax.sharding import PartitionSpec as P

BASE_TAPS = ((1.0, 4.0, 6.0, 4.0, 1.0), (-1.0, -2.0, 0.0, 2.0, 1.0), (1.0, 0.0, -2.0, 0.0, 1.0))
TAP_NORMS = (70.0, 10.0, 6.0)
DILATIONS = (1, 2, 4, 8)
ORDER_TRIPLES = (
    (0, 0, 0),
    (0, 1, 0),
    (0, 0, 1),
    (1, 0, 0),
    (0, 2, 0),
    (0, 0, 2),
    (2, 0, 0),
    (0, 1, 1),
    (1, 1, 0),
    (1, 0, 1),
    (1, 1, 1),
    (0, 2, 2),
)
margin_cells = 16
block_rows = 4


def padded_2(cells, sides, width):
    for axis, dim in sides:
        count = lax.axis_size(axis)
        ends = count - 1
        head = lax.slice_in_dim(cells, 0, width, axis=dim)
        tail = lax.slice_in_dim(cells, cells.shape[dim] - width, cells.shape[dim], axis=dim)
        cells = jnp.concatenate(
            [
                lax.ppermute(tail, axis, [(i, (i + 1) % count) for i in range(ends)]),
                cells,
                lax.ppermute(head, axis, [((i + 1) % count, i) for i in range(ends)]),
            ],
            axis=dim,
        )
    return cells


def filter_axis(padded, axis_number, deriv_order, dilation, length):
    summed = None
    for tap_index in range(5):
        coefficient = BASE_TAPS[deriv_order][tap_index] / math.sqrt(TAP_NORMS[deriv_order])
        row_start = margin_cells + (tap_index - 2) * dilation
        sliced = lax.slice_in_dim(padded, row_start, row_start + length, axis=axis_number).astype(
            jnp.float32
        )
        summed = sliced * coefficient if summed is None else summed + sliced * coefficient
    return summed


def across_columns(padded, length):
    return jnp.stack(
        [
            filter_axis(padded, 2, deriv_order, dilation, length)
            for dilation in DILATIONS
            for deriv_order in range(3)
        ]
    )


def block_features(window, block_size):
    planes = window.shape[1]
    outputs = []
    for scale_index in range(len(DILATIONS)):
        dilation = DILATIONS[scale_index]
        filtered_pairs = {}
        for triple in ORDER_TRIPLES:
            pair_key = (triple[1], triple[2])
            if pair_key not in filtered_pairs:
                filtered_pairs[pair_key] = filter_axis(
                    window[3 * scale_index + triple[2]], 1, triple[1], dilation, block_size
                )
            deep_pad = jnp.pad(
                filtered_pairs[pair_key], ((margin_cells, margin_cells), (0, 0), (0, 0))
            )
            outputs.append(filter_axis(deep_pad, 0, triple[0], dilation, planes))
    stacked = jnp.stack(outputs).astype(jnp.bfloat16)
    return stacked.reshape(stacked.shape[0], -1)


def expectation(features, lowered_stack, offsets, log_prior):
    proj = jnp.dot(lowered_stack, features, preferred_element_type=jnp.float32)
    centred = proj - offsets[:, None]
    distance = jnp.sum(
        (centred * centred).reshape(log_prior.shape[0], features.shape[0], -1), axis=1
    )
    scores = log_prior[:, None] - 0.5 * distance
    return jax.nn.softmax(scores, axis=0)


def moments(features, resp_block):
    comp_count = resp_block.shape[0]
    feat_count = features.shape[0]
    block_counts = jnp.sum(resp_block, axis=1)
    weighted = (resp_block[:, None, :] * features[None].astype(jnp.float32)).astype(jnp.bfloat16)
    weighted = weighted.reshape(comp_count * feat_count, -1)
    block_first = jnp.sum(weighted.astype(jnp.float32), axis=1).reshape(comp_count, feat_count)
    block_second = lax.dot_general(
        weighted, features, (((1,), (1,)), ((), ())), preferred_element_type=jnp.float32
    )
    return (block_counts, block_first, block_second.reshape(comp_count, feat_count, feat_count))


def parameters(log_weights, means, prec_factor):
    comp_count, feat_count = means.shape
    lowered = prec_factor.astype(jnp.bfloat16)
    lowered_stack = jnp.transpose(lowered, (0, 2, 1)).reshape(comp_count * feat_count, feat_count)
    offsets = jnp.einsum(
        "kij,ki->kj", lowered.astype(jnp.float32), means, precision=lax.Precision.HIGHEST
    ).reshape(-1)
    log_diag = jnp.sum(jnp.log(jnp.diagonal(prec_factor, axis1=1, axis2=2)), axis=1)
    log_prior = (
        jax.nn.log_softmax(log_weights) + log_diag - 0.5 * feat_count * math.log(2.0 * math.pi)
    )
    return (lowered_stack, offsets, log_prior)


def finalize(counts, first, second):
    new_weights = counts / jnp.sum(counts)
    new_means = first / counts[:, None]
    new_cov = second / counts[:, None, None] - new_means[:, :, None] * new_means[:, None, :]
    return (new_weights, new_means, new_cov)


def shards(volume, log_weights, means, prec_factor):
    planes, row_count, column_count = volume.shape
    comp_count, feat_count = means.shape
    lowered_stack, offsets, log_prior = parameters(log_weights, means, prec_factor)
    padded_cols = padded_2(volume, (("narrow", 2),), 16)
    across = across_columns(padded_cols, column_count)
    rows_pad = padded_2(across, (("wide", 2),), 16)

    def one_block(block_index, loop_state):
        resp_all, counts, first, second = loop_state
        row_start = block_index * block_rows
        window = lax.dynamic_slice_in_dim(rows_pad, row_start, block_rows + 2 * margin_cells, 2)
        features = block_features(window, block_rows)
        resp_block = expectation(features, lowered_stack, offsets, log_prior)
        block_counts, block_first, block_second = moments(features, resp_block)
        resp_all = lax.dynamic_update_slice_in_dim(
            resp_all, resp_block.reshape(comp_count, planes, block_rows, column_count), row_start, 2
        )
        return (resp_all, counts + block_counts, first + block_first, second + block_second)

    initial = (
        jnp.zeros((comp_count, planes, row_count, column_count), jnp.float32),
        jnp.zeros((comp_count,), jnp.float32),
        jnp.zeros((comp_count, feat_count), jnp.float32),
        jnp.zeros((comp_count, feat_count, feat_count), jnp.float32),
    )
    responsibility, counts, first, second = lax.fori_loop(
        0, row_count // block_rows, one_block, initial
    )
    total_counts, total_first, total_second = lax.psum((counts, first, second), ("wide", "narrow"))
    new_weights, new_means, new_cov = finalize(total_counts, total_first, total_second)
    return (responsibility, new_weights, new_means, new_cov)


def solution(mesh):
    in_specs = (P(None, "wide", "narrow"), P(), P(), P())
    out_specs = (P(None, None, "wide", "narrow"), P(), P(), P())
    return jax.shard_map(shards, mesh=mesh, in_specs=in_specs, out_specs=out_specs, check_vma=False)
```

profile of v0, /device:TPU:0, one launch (start us, length us, event | category | flops | bytes accessed | tf_op | source)
XLA Modules:
  0.0 710.1 jit_solution(10271138397837898796)
XLA Ops:
  37.5 7.7 %pad_maximum_fusion = f32[12,16,96,128]{3,2,1,0:T(8,128)} fusion(f32[12,16,16,128]{3,2,1,0:T(8,128)S(1)} %collective-permute-done.3, f32[12,16,64,128]{3,2,1,0:T(8,128)} %copy-done.2, f32[12,16,16,128]{3,2,1,0:T(8,128)S(1)} %collective-permute-done.2), kind=kLoop, calls=%fused_computation.289 | loop fusion | flops 4718592 | bytes 18874368 | tf_op jit(solution)/shard_map/concatenate | solution.py:35
  47.3 575.3 %while.24 = (s32[]{:T(128)}, f32[6,16,64,128]{3,2,1,0:T(8,128)}, f32[6]{0:T(128)}, f32[6,48]{1,0:T(8,128)S(1)}, f32[6,48,48]{2,1,0:T(8,128)}, /*index=5*/f32[6]{...) while((s32[]{:T(128)}, f32[6,16,64,128]{3,2,1,0:T(8,128)}, ...), condition=%wide.wide.region_9.10_spmd.clone, body=%wide.wide.region_3.9_spmd.clone.sunk | while | flops 480947520 | bytes 43939432 | solution.py:158
  68.2 5.9 fusion.236
  74.1 4.6 reduce_sum.113
  104.2 5.9 fusion.236
  110.2 4.6 reduce_sum.113
  140.2 5.9 fusion.236
  146.1 4.6 reduce_sum.113
  176.2 5.9 fusion.236
  182.1 4.6 reduce_sum.113
  212.2 5.9 fusion.236
  218.1 4.6 reduce_sum.113
  248.2 5.9 fusion.236
  254.1 4.6 reduce_sum.113
  284.2 5.9 fusion.236
  290.1 4.6 reduce_sum.113
  320.1 5.9 fusion.236
  326.1 4.6 reduce_sum.113
  356.1 5.9 fusion.236
  362.0 4.6 reduce_sum.113
  392.1 5.9 fusion.236
  398.0 4.6 reduce_sum.113
  428.1 5.9 fusion.236
  434.0 4.6 reduce_sum.113
  464.1 5.9 fusion.236
  470.0 4.6 reduce_sum.113
  500.1 5.9 fusion.236
  506.0 4.6 reduce_sum.113
  536.0 5.9 fusion.236
  571.8 5.9 fusion.236
  607.5 5.9 fusion.236
  622.6 84.8 %all-reduce.28 = (f32[6]{0:T(128)S(1)}, f32[6,48]{1,0:T(8,128)S(1)}, f32[6,48,48]{2,1,0:T(8,128)S(1)}) all-reduce(f32[6]{0:T(128)} %get-tuple-element.279, f32[6,48]{1,0:T(8,128)S(1)} %get-tuple-element.280, f32[6,48,48]{2,1,0:T(8,128)} %get-tuple-element.281), channel_id=1, replica_groups=mesh['wide'=32,'narrow'=4] {'wide','narrow'}, use_global_device_ids=true, to_apply=%region_10.11 | all-reduce | flops 14118 | bytes 112944 | tf_op jit(solution)/shard_map/psum | solution.py:161
  (1597 shorter events, 454.6 us)
Async XLA Ops:
  0.6 33.0 %copy-start = (f32[6,48]{1,0:T(8,128)S(1)}, f32[6,48]{1,0:T(8,128)}, u32[]{:S(2)}) copy-start(f32[6,48]{1,0:T(8,128)} %param.8) | copy-start | bytes 3460
  0.6 17.7 %copy-start.1 = (bf16[16,64,128]{2,1,0:T(8,128)(2,1)S(1)}, bf16[16,64,128]{2,1,0:T(8,128)(2,1)}, u32[]{:S(2)}) copy-start(bf16[16,64,128]{2,1,0:T(8,128)(2,1)} %param.6) | copy-start | bytes 786436
  1.9 10.2 %collective-permute-start.1 = (bf16[16,64,16]{2,1,0:T(8,128)(2,1)S(1)}, bf16[16,64,16]{2,1,0:T(8,128)(2,1)S(1)}, u32[]{:S(2)}, u32[]{:S(2)}) collective-permute-start(bf16[16,64,16]{2,1,0:T(8,128)(2,1)S(1)} %get-tuple-element.449), channel_id=1, source_target_pairs={{1,0},{2,1},{3,2},{5,4},{6,5},{7,6},{9,8},{10,9},{11,10},{13,12},{... | collective-permute-start | bytes 98312 | tf_op jit(solution)/shard_map/ppermute | solution.py:39
  3.2 10.1 %collective-permute-start = (bf16[16,64,16]{2,1,0:T(8,128)(2,1)S(1)}, bf16[16,64,16]{2,1,0:T(8,128)(2,1)S(1)}, u32[]{:S(2)}, u32[]{:S(2)}) collective-permute-start(bf16[16,64,16]{2,1,0:T(8,128)(2,1)S(1)} %get-tuple-element.448), channel_id=1, source_target_pairs={{0,1},{1,2},{2,3},{4,5},{5,6},{6,7},{8,9},{9,10},{10,11},{12,13},{... | collective-permute-start | bytes 98312 | tf_op jit(solution)/shard_map/ppermute | solution.py:37
  20.7 8.8 %copy-start.10 = (f32[6]{0:T(128)S(1)}, f32[6]{0:T(128)}, u32[]{:S(2)}) copy-start(f32[6]{0:T(128)} %param.7) | copy-start | bytes 76
  20.7 11.5 %copy-start.3 = (f32[6,48,48]{2,1,0:T(8,128)S(1)}, f32[6,48,48]{2,1,0:T(8,128)}, u32[]{:S(2)}) copy-start(f32[6,48,48]{2,1,0:T(8,128)} %param.9) | copy-start | bytes 165892
  26.8 10.7 %collective-permute-start.2 = (f32[12,16,16,128]{3,2,1,0:T(8,128)}, f32[12,16,16,128]{3,2,1,0:T(8,128)S(1)}, u32[]{:S(2)}, u32[]{:S(2)}) collective-permute-start(f32[12,16,16,128]{3,2,1,0:T(8,128)} %get-tuple-element.446), channel_id=1, source_target_pairs={{0,4},{4,8},{8,12},{12,16},{16,20},{20,24},{24,28},{28,32},{32,36}... | collective-permute-start | bytes 4718600 | tf_op jit(solution)/shard_map/ppermute | solution.py:37
  28.2 9.3 %collective-permute-start.3 = (f32[12,16,16,128]{3,2,1,0:T(8,128)}, f32[12,16,16,128]{3,2,1,0:T(8,128)S(1)}, u32[]{:S(2)}, u32[]{:S(2)}) collective-permute-start(f32[12,16,16,128]{3,2,1,0:T(8,128)} %get-tuple-element.447), channel_id=1, source_target_pairs={{4,0},{8,4},{12,8},{16,12},{20,16},{24,20},{28,24},{32,28},{36,32}... | collective-permute-start | bytes 4718600 | tf_op jit(solution)/shard_map/ppermute | solution.py:39
  74.1 5.3 copy-start.4
  110.2 5.3 copy-start.4
  146.1 5.3 copy-start.4
  150.7 4.0 copy-start.7
  182.1 5.3 copy-start.4
  186.7 4.0 copy-start.7
  218.1 5.3 copy-start.4
  222.7 4.0 copy-start.7
  254.1 5.3 copy-start.4
  258.7 4.0 copy-start.7
  290.1 5.3 copy-start.4
  294.7 4.0 copy-start.7
  326.1 5.3 copy-start.4
  330.6 4.0 copy-start.7
  362.0 5.3 copy-start.4
  366.6 4.0 copy-start.7
  398.0 5.3 copy-start.4
  402.6 4.0 copy-start.7
  434.0 5.3 copy-start.4
  470.0 5.3 copy-start.4
  506.0 5.3 copy-start.4
  542.0 5.3 copy-start.4
  577.7 5.3 copy-start.4
  613.4 5.3 copy-start.4
  (43 other events, 78.6 us)
where the time goes:
time: 723 us; the launch traced here: 710 us
  other arithmetic  280 us (39%)
  local copies, waits for them, and re-layouts  206 us (28%)
  matrix products  117 us (16%)
  blocking collectives  84.8 us (12%)
  starting transfers between devices  8.52 us (1%)
    another operation x784, local copies, waits for them, and re-layouts, block_features(): stacked = jnp.stack(outputs).astype(jnp.bfloat16)  125 us
    dot_general x16, matrix products, expectation(): proj = jnp.dot(lowered_stack, features, preferred_element_type=jnp.float32)  94.6 us
    psum x1, blocking collectives, shards(): lax.psum((counts, first, second), ('wide', 'narrow'))  84.8 us
    another operation x256, other arithmetic  81.4 us
    reduce_sum x16, other arithmetic, expectation(): jnp.sum((centred * centred).reshape(log_prior.shape[0], features.shape[0]...  73.3 us
    add x192, other arithmetic, filter_axis(): summed + sliced * coefficient  66.4 us
    squeeze x16, local copies, waits for them, and re-layouts, block_features(): window[3 * scale_index + triple[2]]  55.2 us
    dot_general x16, matrix products, moments(): lax.dot_general(weighted, features, (((1,), (1,)), ((), ())), preferred_e...  22.6 us
  transfers between devices with their start and end apart: 4, of which 2 were waited for; matrix products, arithmetic and copies ran while one was open for 1% of the time, Pallas kernels for 0%

commit v1 on v0

v1 whole, which is shorter than its diff:
```python
import math

import jax
import jax.numpy as jnp
import numpy as np
from jax import lax
from jax.experimental import pallas as pl
from jax.experimental.pallas import tpu as pltpu
from jax.sharding import PartitionSpec as P

BASE_TAPS = ((1.0, 4.0, 6.0, 4.0, 1.0), (-1.0, -2.0, 0.0, 2.0, 1.0), (1.0, 0.0, -2.0, 0.0, 1.0))
TAP_NORMS = (70.0, 10.0, 6.0)
DILATIONS = (1, 2, 4, 8)
ORDER_TRIPLES = (
    (0, 0, 0),
    (0, 1, 0),
    (0, 0, 1),
    (1, 0, 0),
    (0, 2, 0),
    (0, 0, 2),
    (2, 0, 0),
    (0, 1, 1),
    (1, 1, 0),
    (1, 0, 1),
    (1, 1, 1),
    (0, 2, 2),
)
SHIFTS = (-16, -8, -4, -2, -1, 0, 1, 2, 4, 8, 16)
MARGIN = 16
PLANES, ROWS, COLS = 16, 64, 128
COMP, FEAT = 6, 48
DEEP = 4 * FEAT + 16


def filter_matrix():
    out = np.zeros((4, PLANES, 16, 5, 5, PLANES), np.float32)
    for s, d in enumerate(DILATIONS):
        base = 4 * (s % 2)
        for j, (oz, ox, oy) in enumerate(ORDER_TRIPLES):
            plane_taps = np.outer(BASE_TAPS[ox], BASE_TAPS[oy])
            for c in range(5):
                for z in range(PLANES):
                    src = z + (c - 2) * d
                    if 0 <= src < PLANES:
                        out[s, z, base + j, :, :, src] += BASE_TAPS[oz][c] * plane_taps
    return out.reshape(4, PLANES * 16, 25 * PLANES)


def feature_scale():
    rows = [1.0 / math.sqrt(TAP_NORMS[a] * TAP_NORMS[b] * TAP_NORMS[c]) for a, b, c in ORDER_TRIPLES]
    return np.tile(np.array(rows * 4, np.float32)[:, None], (1, COLS))


def kernel(
    vol_ref, filt_ref, scale_ref, lhs_ref, prior_ref, resp_ref, sec_ref, cnt_ref, shifted, feats
):
    octet = pl.program_id(0)
    one_tile = jnp.where(lax.broadcasted_iota(jnp.int32, (16, COLS), 0) < 3, 1.0, 0.0)
    one_tile = one_tile.astype(jnp.bfloat16)

    @pl.when(octet == 0)
    def _():
        def one_row(x, carry):
            row = vol_ref[x]
            for n, shift in enumerate(SHIFTS):
                shifted[n, x] = row[:, MARGIN + shift : MARGIN + shift + COLS]
            return carry

        lax.fori_loop(0, ROWS + 2 * MARGIN, one_row, 0)
        sec_ref[...] = jnp.zeros_like(sec_ref)
        cnt_ref[...] = jnp.zeros_like(cnt_ref)

    def one_pair(pair, carry):
        x = octet * 8 + pair * 2
        blocks = []
        for s, d in enumerate(DILATIONS):
            sides = []
            for e in range(2):
                tiles = [
                    shifted[SHIFTS.index((b - 2) * d), x + e + MARGIN + (a - 2) * d]
                    for a in range(5)
                    for b in range(5)
                ]
                sides.append(jnp.concatenate(tiles, axis=0))
            rhs = jnp.concatenate(sides, axis=1)
            out = jnp.dot(filt_ref[s], rhs, preferred_element_type=jnp.float32)
            blocks.append(out.reshape(PLANES, 16, 2 * COLS))
        a, b, c, d = blocks
        rows = [a[:, :8], a[:, 8:] + b[:, :8], b[:, 8:], c[:, :8], c[:, 8:] + d[:, :8], d[:, 8:]]
        whole = jnp.concatenate(rows, axis=1)
        for e in range(2):
            part = whole[:, :, e * COLS : (e + 1) * COLS] * scale_ref[...][None]
            feats[pair * 2 + e] = part.astype(jnp.bfloat16)
        return carry

    lax.fori_loop(0, 4, one_pair, 0)

    def one_plane(z, carry):
        quads = []
        for q in range(2):
            quads.append(
                jnp.concatenate([feats[4 * q + i, z] for i in range(4)] + [one_tile], axis=0)
            )
        rhs = jnp.concatenate(quads, axis=1)
        scores = []
        for g in range(3):
            proj = jnp.dot(
                lhs_ref[g * 8 * FEAT : (g + 1) * 8 * FEAT], rhs, preferred_element_type=jnp.float32
            )
            proj = proj.reshape(FEAT, 8, 2 * COLS)
            distance = jnp.sum(proj * proj, axis=0)
            prior = prior_ref[g]
            scores.append(jnp.concatenate([prior, prior], axis=1) - 0.5 * distance)
        top = jnp.maximum(jnp.maximum(scores[0], scores[1]), scores[2])
        top = jnp.maximum(top, pltpu.roll(top, 4, 0))
        powers = [jnp.exp(s - top) for s in scores]
        total = powers[0] + powers[1] + powers[2]
        total = total + pltpu.roll(total, 4, 0)
        inverse = 1.0 / total
        for g in range(3):
            r = powers[g] * inverse
            left, right = r[:, :COLS], r[:, COLS:]
            for h in range(2):
                tile = jnp.concatenate(
                    [left[4 * h : 4 * h + 4], right[4 * h : 4 * h + 4]], axis=0
                )
                resp_ref[2 * g + h, z] = tile
                cnt_ref[2 * g + h] += tile
        features, weighted = [], []
        for i in range(8):
            f = feats[i, z]
            f32 = f.astype(jnp.float32)
            features.append(jnp.concatenate([f, one_tile], axis=0))
            weighted.append(
                jnp.concatenate(
                    [(resp_ref[k, z, i : i + 1] * f32).astype(jnp.bfloat16) for k in range(COMP)],
                    axis=0,
                )
            )
        f_all = jnp.concatenate(features, axis=1)
        w_all = jnp.concatenate(weighted, axis=1)
        sec_ref[...] += lax.dot_general(
            f_all, w_all, (((1,), (1,)), ((), ())), preferred_element_type=jnp.float32
        )
        return carry

    lax.fori_loop(0, PLANES, one_plane, 0)


def local_step(padded, lhs, prior):
    filt = jnp.asarray(filter_matrix(), jnp.bfloat16)
    scale = jnp.asarray(feature_scale())
    full = lambda *shape: pl.BlockSpec(shape, lambda o: (0,) * len(shape))
    return pl.pallas_call(
        kernel,
        grid=(ROWS // 8,),
        in_specs=[
            full(*padded.shape),
            full(*filt.shape),
            full(*scale.shape),
            full(*lhs.shape),
            full(*prior.shape),
        ],
        out_specs=[
            pl.BlockSpec((COMP, PLANES, 8, COLS), lambda o: (0, 0, o, 0)),
            full(FEAT + 16, COMP * FEAT),
            full(COMP, 8, COLS),
        ],
        out_shape=[
            jax.ShapeDtypeStruct((COMP, PLANES, ROWS, COLS), jnp.float32),
            jax.ShapeDtypeStruct((FEAT + 16, COMP * FEAT), jnp.float32),
            jax.ShapeDtypeStruct((COMP, 8, COLS), jnp.float32),
        ],
        scratch_shapes=[
            pltpu.VMEM((len(SHIFTS), ROWS + 2 * MARGIN, PLANES, COLS), jnp.bfloat16),
            pltpu.VMEM((8, PLANES, FEAT, COLS), jnp.bfloat16),
        ],
        compiler_params=pltpu.CompilerParams(
            dimension_semantics=("arbitrary",), vmem_limit_bytes=50 * 2**20
        ),
        name="mixture_step",
    )(padded, filt, scale, lhs, prior)


def parameters(log_weights, means, prec_factor):
    lowered = prec_factor.astype(jnp.bfloat16)
    offsets = jnp.einsum(
        "kij,ki->kj", lowered.astype(jnp.float32), means, precision=lax.Precision.HIGHEST
    )
    log_diag = jnp.sum(jnp.log(jnp.diagonal(prec_factor, axis1=1, axis2=2)), axis=1)
    log_prior = jax.nn.log_softmax(log_weights) + log_diag - 0.5 * FEAT * math.log(2.0 * math.pi)
    columns = jnp.transpose(lowered.reshape(3, 2, FEAT, FEAT), (0, 3, 1, 2))
    eye = jnp.eye(4, dtype=jnp.bfloat16)
    stacked = columns[:, :, :, None, None, :] * eye[None, None, None, :, :, None]
    stacked = stacked.reshape(COMP * FEAT * 4, 4 * FEAT)
    rest = -jnp.transpose(offsets.reshape(3, 2, FEAT), (0, 2, 1))
    terms = []
    for _ in range(3):
        term = lax.reduce_precision(rest, 8, 7)
        terms.append(term)
        rest = rest - term
    tail = jnp.stack(terms + [jnp.zeros_like(rest)] * 13, axis=-1).astype(jnp.bfloat16)
    tail = jnp.broadcast_to(tail[:, :, :, None, :], (3, FEAT, 2, 4, 16)).reshape(-1, 16)
    lhs = jnp.concatenate([stacked, tail], axis=1)
    prior = jnp.broadcast_to(log_prior.reshape(3, 2, 1, 1), (3, 2, 4, COLS)).reshape(3, 8, COLS)
    return lhs, prior


def padded_2(cells, axis, dim, width):
    count = lax.axis_size(axis)
    ends = count - 1
    head = lax.slice_in_dim(cells, 0, width, axis=dim)
    tail = lax.slice_in_dim(cells, cells.shape[dim] - width, cells.shape[dim], axis=dim)
    before = lax.ppermute(tail, axis, [(i, i + 1) for i in range(ends)])
    after = lax.ppermute(head, axis, [(i + 1, i) for i in range(ends)])
    return jnp.concatenate([before, cells, after], axis=dim)


def wide_perm(move):
    perm = []
    for i in range(32):
        x, y, c = move(i // 8, (i // 2) % 4, i % 2)
        perm.append((i, (x * 4 + y) * 2 + c))
    return perm


def device_sum(part):
    part = part + lax.ppermute(part, "wide", wide_perm(lambda x, y, c: (x, y, 1 - c)))
    narrow = [
        lax.ppermute(part, "narrow", [(i, (i + d) % 4) for i in range(4)]) for d in (1, 2, 3)
    ]
    part = ((part + narrow[0]) + (narrow[1] + narrow[2]))
    for axis in range(2):
        got = []
        for d in (1, 2, 3):
            if axis == 0:
                perm = wide_perm(lambda x, y, c: (x, (y + d) % 4, c))
            else:
                perm = wide_perm(lambda x, y, c: ((x + d) % 4, y, c))
            got.append(lax.ppermute(part, "wide", perm))
        part = (part + got[0]) + (got[1] + got[2])
    return part


def shards(volume, log_weights, means, prec_factor):
    lhs, prior = parameters(log_weights, means, prec_factor)
    cells = padded_2(volume, "narrow", 2, MARGIN)
    cells = padded_2(cells, "wide", 1, MARGIN)
    cells = jnp.transpose(cells, (1, 0, 2))
    cells = jnp.pad(cells, ((0, 0), (0, 0), (0, 96)))
    responsibility, sec, cnt = local_step(cells, lhs, prior)
    counts = jnp.sum(cnt, axis=(1, 2))
    flat = jnp.concatenate([sec[: FEAT + 1].reshape(-1), counts, jnp.zeros((218,), jnp.float32)])
    flat = device_sum(flat.reshape(112, 128)).reshape(-1)
    size = FEAT * COMP * FEAT
    second = jnp.transpose(flat[:size].reshape(FEAT, COMP, FEAT), (1, 2, 0))
    first = flat[size : size + COMP * FEAT].reshape(COMP, FEAT)
    counts = flat[size + COMP * FEAT : size + COMP * FEAT + COMP]
    new_weights = counts / jnp.sum(counts)
    new_means = first / counts[:, None]
    new_cov = second / counts[:, None, None] - new_means[:, :, None] * new_means[:, None, :]
    return (responsibility, new_weights, new_means, new_cov)


def solution(mesh):
    in_specs = (P(None, "wide", "narrow"), P(), P(), P())
    out_specs = (P(None, None, "wide", "narrow"), P(), P(), P())
    return jax.shard_map(shards, mesh=mesh, in_specs=in_specs, out_specs=out_specs, check_vma=False)
```

time: 723 us -> 184 us (0.25); the launches traced: 710 us -> 183 us
  other arithmetic: 280 us -> 6.12 us
  local copies, waits for them, and re-layouts: 206 us -> 10 us
  Pallas kernels: 0 us -> 122 us
  matrix products: 117 us -> 0.16 us
  blocking collectives: 84.8 us -> 0 us
  starting transfers between devices: 8.52 us -> 30.5 us
  waiting for transfers between devices: 4.45 us -> 13 us
    another operation x784 -> x7, local copies, waits for them, and re-layouts: 125 us -> 1.79 us  [parameters(): jnp.stack(terms + [jnp.zeros_like(rest)] * 13, axis=-1).astype(jnp.bfloat16)]
    pallas_call x0 -> x1, Pallas kernels: none -> 122 us  [local_step(): pl.pallas_call(kernel, grid=(ROWS // 8,), in_specs=[full(*padded.shape),...]
    dot_general x32 -> x0, matrix products: 117 us -> none  [the longest x16 94.6 us: expectation(): proj = jnp.dot(lowered_stack, features, preferred_element_type=jnp.float32)]
    reduce_sum x65 -> x1, other arithmetic: 94.1 us -> 0.13 us  [shards(): counts = jnp.sum(cnt, axis=(1, 2))]
    psum x1 -> x0, blocking collectives: 84.8 us -> none  [shards(): lax.psum((counts, first, second), ('wide', 'narrow'))]
    another operation x257 -> x1, other arithmetic: 81.8 us -> 0.02 us  [parameters(): jnp.stack(terms + [jnp.zeros_like(rest)] * 13, axis=-1).astype(jnp.bfloat16)]
    add x224 -> x4, other arithmetic: 66.7 us -> 0.06 us  [the longest x2 0.03 us: device_sum(): part = part + got[0] + (got[1] + got[2])]
    squeeze x16 -> x0, local copies, waits for them, and re-layouts: 55.2 us -> none  [block_features(): window[3 * scale_index + triple[2]]]
  transfers between devices with their start and end apart: 4 -> 14, of which waited for: 2 -> 7; matrix products, arithmetic and copies ran while one was open for 1% -> 5% of each run, Pallas kernels for 0% -> 0%
where the time goes in v1:
time: 184 us; the launch traced here: 183 us
  Pallas kernels  122 us (66%)
  starting transfers between devices  30.5 us (17%)
  waiting for transfers between devices  13 us (7%)
  local copies, waits for them, and re-layouts  10 us (5%)
  other arithmetic  6.12 us (3%)
    pallas_call x1, Pallas kernels, local_step(): pl.pallas_call(kernel, grid=(ROWS // 8,), in_specs=[full(*padded.shape),...  122 us
    ppermute x6, starting transfers between devices, device_sum(): got.append(lax.ppermute(part, 'wide', perm))  11.7 us
    ppermute x3, starting transfers between devices, device_sum(): lax.ppermute(part, 'narrow', [(i, (i + d) % 4) for i in range(4)])  7.24 us
    ppermute x6, waiting for transfers between devices, device_sum(): got.append(lax.ppermute(part, 'wide', perm))  6.29 us
    ppermute x2, starting transfers between devices, padded_2(): before = lax.ppermute(tail, axis, [(i, i + 1) for i in range(ends)])  5.37 us
  transfers between devices with their start and end apart: 14, of which 7 were waited for; matrix products, arithmetic and copies ran while one was open for 5% of the time, Pallas kernels for 0%

profile of v1, /device:TPU:0, one launch (start us, length us, event | category | flops | bytes accessed | tf_op | source)
XLA Modules:
  0.0 182.9 jit_solution(5962758994345268017)
XLA Ops:
  0.7 1.2 copy.38
  1.8 0.9 fusion.8
  2.7 3.9 %collective-permute-start = (bf16[16,64,16]{2,0,1:T(8,128)(2,1)}, bf16[16,64,16]{2,0,1:T(8,128)(2,1)S(1)}, u32[]{:S(2)}, u32[]{:S(2)}) collective-permute-start(bf16[16,64,16]{2,0,1:T(8,128)(2,1)} %get-tuple-element.24), channel_id=1, source_target_pairs={{0,1},{1,2},{2,3},{4,5},{5,6},{6,7},{8,9},{9,10},{10,11},{12,13},{... | collective-permute-start | bytes 98312 | tf_op jit(solution)/shard_map/ppermute | solution.py:214
  6.6 1.3 collective-permute-start.1
  7.9 1.5 copy.45
  10.7 0.6 mul.33
  11.4 2.1 %gather_fusion = f32[48,6]{1,0:T(8,128)S(1)} fusion(f32[6,48,48]{0,2,1:T(8,128)} %copy.45, s32[48]{0:T(128)S(1)} %or_bitcast_fusion), kind=kCustom, calls=%fused_computation | custom fusion | bytes 2688 | tf_op jit(solution)/shard_map/jit(diagonal)/gather | solution.py:190
  13.6 1.2 stack.23
  15.2 0.6 reduce_max.10
  15.8 1.2 exponential_reduce_fusion
  17.9 1.5 collective-permute-start.2
  19.4 1.3 collective-permute-start.3
  20.7 0.7 add_add_fusion.3
  21.6 2.7 %collective-permute-done.3 = bf16[16,16,160]{2,0,1:T(8,128)(2,1)S(1)} collective-permute-done((bf16[16,16,160]{2,0,1:T(8,128)(2,1)S(1)}, bf16[16,16,160]{2,0,1:T(8,128)(2,1)S(1)}, u32[]{:S(2)}, u32[]{:S(2)}) %collective-permute-start.3) | collective-permute-done | bytes 81952 | tf_op jit(solution)/shard_map/ppermute | solution.py:215
  24.9 121.6 %mixture_step.1 = (f32[6,16,64,128]{3,2,1,0:T(8,128)}, f32[64,288]{1,0:T(8,128)S(1)}, f32[6,8,128]{2,1,0:T(8,128)S(1)}) custom-call(bf16[96,16,256]{2,1,0:T(8,128)(2,1)S(1)} %pad.4.vol_ref, bf16[4,256,400]{2,1,0:T(8,128)(2,1)S(1)} %copy-done.1, f32[48,128]{1,0:T(8,128)S(1)} %copy-done.2, bf16[1152,208]{1,0:T(8,128)(2,1)S(1)} %pad_maximum_fusion.lhs_ref, ...), custom_call_target="tpu_custom_call" | custom-call | tf_op jit(solution)/shard_map/mixture_step/pallas_call | solution.py:154
  146.8 3.6 %collective-permute-start.4 = (f32[112,128]{1,0:T(8,128)S(1)}, f32[112,128]{1,0:T(8,128)S(1)}, u32[]{:S(2)}, u32[]{:S(2)}) collective-permute-start(f32[112,128]{1,0:T(8,128)S(1)} %bitcast.41), channel_id=1, source_target_pairs={{0,4},{4,0},{8,12},{12,8},{16,20},{20,16},{24,28},{28,24},{32,36},... | collective-permute-start | bytes 172040 | tf_op jit(solution)/shard_map/ppermute | solution.py:228
  150.3 0.9 collective-permute-done.4
  151.2 2.7 %collective-permute-start.5 = (f32[112,128]{1,0:T(8,128)S(1)}, f32[112,128]{1,0:T(8,128)S(1)}, u32[]{:S(2)}, u32[]{:S(2)}) collective-permute-start(f32[112,128]{1,0:T(8,128)S(1)} %bitcast_add_fusion), channel_id=1, source_target_pairs={{0,1},{1,2},{2,3},{3,0},{4,5},{5,6},{6,7},{7,4},{8,9},{9,10},{10,1... | collective-permute-start | bytes 172040 | tf_op jit(solution)/shard_map/ppermute | solution.py:230
  153.9 3.6 %collective-permute-start.6 = (f32[112,128]{1,0:T(8,128)S(1)}, f32[112,128]{1,0:T(8,128)S(1)}, u32[]{:S(2)}, u32[]{:S(2)}) collective-permute-start(f32[112,128]{1,0:T(8,128)S(1)} %bitcast_add_fusion), channel_id=1, source_target_pairs={{0,2},{1,3},{2,0},{3,1},{4,6},{5,7},{6,4},{7,5},{8,10},{9,11},{10,... | collective-permute-start | bytes 172040 | tf_op jit(solution)/shard_map/ppermute | solution.py:230
  157.5 1.0 collective-permute-start.7
  158.5 2.4 %collective-permute-done.6 = f32[112,128]{1,0:T(8,128)S(1)} collective-permute-done((f32[112,128]{1,0:T(8,128)S(1)}, f32[112,128]{1,0:T(8,128)S(1)}, u32[]{:S(2)}, u32[]{:S(2)}) %collective-permute-start.6) | collective-permute-done | bytes 57376 | tf_op jit(solution)/shard_map/ppermute | solution.py:230
  160.9 0.7 collective-permute-done.7
  161.7 4.8 %collective-permute-start.10 = (f32[112,128]{1,0:T(8,128)S(1)}, f32[112,128]{1,0:T(8,128)S(1)}, u32[]{:S(2)}, u32[]{:S(2)}) collective-permute-start(f32[112,128]{1,0:T(8,128)S(1)} %add_add_fusion.2), channel_id=1, source_target_pairs={{0,24},{4,28},{8,0},{12,4},{16,8},{20,12},{24,16},{28,20},{32,56},... | collective-permute-start | bytes 172040 | tf_op jit(solution)/shard_map/ppermute | solution.py:240
  166.4 1.5 collective-permute-start.9
  168.3 4.2 %collective-permute-done.8 = f32[112,128]{1,0:T(8,128)S(1)} collective-permute-done((f32[112,128]{1,0:T(8,128)S(1)}, f32[112,128]{1,0:T(8,128)S(1)}, u32[]{:S(2)}, u32[]{:S(2)}) %collective-permute-start.8) | collective-permute-done | bytes 57376 | tf_op jit(solution)/shard_map/ppermute | solution.py:240
  172.5 1.6 collective-permute-start.11
  174.0 1.3 collective-permute-start.12
  175.3 2.5 %collective-permute-start.13 = (f32[112,128]{1,0:T(8,128)S(1)}, f32[112,128]{1,0:T(8,128)S(1)}, u32[]{:S(2)}, u32[]{:S(2)}) collective-permute-start(f32[112,128]{1,0:T(8,128)S(1)} %add_add_fusion.1), channel_id=1, source_target_pairs={{0,96},{4,100},{8,104},{12,108},{16,112},{20,116},{24,120},{28,124... | collective-permute-start | bytes 172040 | tf_op jit(solution)/shard_map/ppermute | solution.py:240
  177.9 1.8 collective-permute-done.12
  179.7 0.7 fusion.9
  180.9 0.8 copy.47
  181.7 1.2 broadcast_divide_fusion.1
  (61 shorter events, 4.0 us)
Async XLA Ops:
  0.6 8.8 %copy-start = (f32[6,48]{1,0:T(8,128)S(1)}, f32[6,48]{1,0:T(8,128)}, u32[]{:S(2)}) copy-start(f32[6,48]{1,0:T(8,128)} %param.8) | copy-start | bytes 3460
  0.6 7.3 %copy-start.3 = (f32[6,48,48]{2,1,0:T(8,128)S(1)}, f32[6,48,48]{2,1,0:T(8,128)}, u32[]{:S(2)}) copy-start(f32[6,48,48]{2,1,0:T(8,128)} %param.9) | copy-start | bytes 165892
  2.7 15.1 %collective-permute-start = (bf16[16,64,16]{2,0,1:T(8,128)(2,1)}, bf16[16,64,16]{2,0,1:T(8,128)(2,1)S(1)}, u32[]{:S(2)}, u32[]{:S(2)}) collective-permute-start(bf16[16,64,16]{2,0,1:T(8,128)(2,1)} %get-tuple-element.24), channel_id=1, source_target_pairs={{0,1},{1,2},{2,3},{4,5},{5,6},{6,7},{8,9},{9,10},{10,11},{12,13},{... | collective-permute-start | bytes 98312 | tf_op jit(solution)/shard_map/ppermute | solution.py:214
  6.6 11.1 %collective-permute-start.1 = (bf16[16,64,16]{2,0,1:T(8,128)(2,1)S(1)}, bf16[16,64,16]{2,0,1:T(8,128)(2,1)S(1)}, u32[]{:S(2)}, u32[]{:S(2)}) collective-permute-start(bf16[16,64,16]{2,0,1:T(8,128)(2,1)S(1)} %get-tuple-element.25), channel_id=1, source_target_pairs={{1,0},{2,1},{3,2},{5,4},{6,5},{7,6},{9,8},{10,9},{11,10},{13,12},{... | collective-permute-start | bytes 98312 | tf_op jit(solution)/shard_map/ppermute | solution.py:215
  11.3 3.8 %copy-start.5 = (f32[6]{0:T(128)S(1)}, f32[6]{0:T(128)}, u32[]{:S(2)}) copy-start(f32[6]{0:T(128)} %param.7) | copy-start | bytes 76
  17.9 3.7 %collective-permute-start.2 = (bf16[16,16,160]{2,0,1:T(8,128)(2,1)S(1)}, bf16[16,16,160]{2,0,1:T(8,128)(2,1)S(1)}, u32[]{:S(2)}, u32[]{:S(2)}) collective-permute-start(bf16[16,16,160]{2,0,1:T(8,128)(2,1)S(1)} %get-tuple-element.22), channel_id=1, source_target_pairs={{0,4},{4,8},{8,12},{12,16},{16,20},{20,24},{24,28},{28,32},{32,36}... | collective-permute-start | bytes 245768 | tf_op jit(solution)/shard_map/ppermute | solution.py:214
  19.4 4.9 %collective-permute-start.3 = (bf16[16,16,160]{2,0,1:T(8,128)(2,1)S(1)}, bf16[16,16,160]{2,0,1:T(8,128)(2,1)S(1)}, u32[]{:S(2)}, u32[]{:S(2)}) collective-permute-start(bf16[16,16,160]{2,0,1:T(8,128)(2,1)S(1)} %get-tuple-element.23), channel_id=1, source_target_pairs={{4,0},{8,4},{12,8},{16,12},{20,16},{24,20},{28,24},{32,28},{36,32}... | collective-permute-start | bytes 245768 | tf_op jit(solution)/shard_map/ppermute | solution.py:215
  21.6 3.3 %copy-start.1 = (bf16[4,256,400]{2,1,0:T(8,128)(2,1)S(1)}, bf16[4,256,400]{2,1,0:T(8,128)(2,1)}, u32[]{:S(2)}) copy-start(bf16[4,256,400]{2,1,0:T(8,128)(2,1)} %constant.27.clone.filt_ref) | copy-start | bytes 2457604
  21.6 3.3 %copy-start.2 = (f32[48,128]{1,0:T(8,128)S(1)}, f32[48,128]{1,0:T(8,128)}, u32[]{:S(2)}) copy-start(f32[48,128]{1,0:T(8,128)} %constant.28.clone.scale_ref) | copy-start | bytes 73732
  146.8 4.4 %collective-permute-start.4 = (f32[112,128]{1,0:T(8,128)S(1)}, f32[112,128]{1,0:T(8,128)S(1)}, u32[]{:S(2)}, u32[]{:S(2)}) collective-permute-start(f32[112,128]{1,0:T(8,128)S(1)} %bitcast.41), channel_id=1, source_target_pairs={{0,4},{4,0},{8,12},{12,8},{16,20},{20,16},{24,28},{28,24},{32,36},... | collective-permute-start | bytes 172040 | tf_op jit(solution)/shard_map/ppermute | solution.py:228
  151.2 7.3 %collective-permute-start.5 = (f32[112,128]{1,0:T(8,128)S(1)}, f32[112,128]{1,0:T(8,128)S(1)}, u32[]{:S(2)}, u32[]{:S(2)}) collective-permute-start(f32[112,128]{1,0:T(8,128)S(1)} %bitcast_add_fusion), channel_id=1, source_target_pairs={{0,1},{1,2},{2,3},{3,0},{4,5},{5,6},{6,7},{7,4},{8,9},{9,10},{10,1... | collective-permute-start | bytes 172040 | tf_op jit(solution)/shard_map/ppermute | solution.py:230
  153.9 7.0 %collective-permute-start.6 = (f32[112,128]{1,0:T(8,128)S(1)}, f32[112,128]{1,0:T(8,128)S(1)}, u32[]{:S(2)}, u32[]{:S(2)}) collective-permute-start(f32[112,128]{1,0:T(8,128)S(1)} %bitcast_add_fusion), channel_id=1, source_target_pairs={{0,2},{1,3},{2,0},{3,1},{4,6},{5,7},{6,4},{7,5},{8,10},{9,11},{10,... | collective-permute-start | bytes 172040 | tf_op jit(solution)/shard_map/ppermute | solution.py:230
  157.5 4.2 %collective-permute-start.7 = (f32[112,128]{1,0:T(8,128)S(1)}, f32[112,128]{1,0:T(8,128)S(1)}, u32[]{:S(2)}, u32[]{:S(2)}) collective-permute-start(f32[112,128]{1,0:T(8,128)S(1)} %bitcast_add_fusion), channel_id=1, source_target_pairs={{0,3},{1,0},{2,1},{3,2},{4,7},{5,4},{6,5},{7,6},{8,11},{9,8},{10,9... | collective-permute-start | bytes 172040 | tf_op jit(solution)/shard_map/ppermute | solution.py:230
  161.7 6.6 %collective-permute-start.10 = (f32[112,128]{1,0:T(8,128)S(1)}, f32[112,128]{1,0:T(8,128)S(1)}, u32[]{:S(2)}, u32[]{:S(2)}) collective-permute-start(f32[112,128]{1,0:T(8,128)S(1)} %add_add_fusion.2), channel_id=1, source_target_pairs={{0,24},{4,28},{8,0},{12,4},{16,8},{20,12},{24,16},{28,20},{32,56},... | collective-permute-start | bytes 172040 | tf_op jit(solution)/shard_map/ppermute | solution.py:240
  166.4 6.0 %collective-permute-start.8 = (f32[112,128]{1,0:T(8,128)S(1)}, f32[112,128]{1,0:T(8,128)S(1)}, u32[]{:S(2)}, u32[]{:S(2)}) collective-permute-start(f32[112,128]{1,0:T(8,128)S(1)} %add_add_fusion.2), channel_id=1, source_target_pairs={{0,8},{4,12},{8,16},{12,20},{16,24},{20,28},{24,0},{28,4},{32,40},... | collective-permute-start | bytes 172040 | tf_op jit(solution)/shard_map/ppermute | solution.py:240
  166.4 6.0 %collective-permute-start.9 = (f32[112,128]{1,0:T(8,128)S(1)}, f32[112,128]{1,0:T(8,128)S(1)}, u32[]{:S(2)}, u32[]{:S(2)}) collective-permute-start(f32[112,128]{1,0:T(8,128)S(1)} %add_add_fusion.2), channel_id=1, source_target_pairs={{0,16},{4,20},{8,24},{12,28},{16,0},{20,4},{24,8},{28,12},{32,48},... | collective-permute-start | bytes 172040 | tf_op jit(solution)/shard_map/ppermute | solution.py:240
  172.5 5.5 %collective-permute-start.11 = (f32[112,128]{1,0:T(8,128)S(1)}, f32[112,128]{1,0:T(8,128)S(1)}, u32[]{:S(2)}, u32[]{:S(2)}) collective-permute-start(f32[112,128]{1,0:T(8,128)S(1)} %add_add_fusion.1), channel_id=1, source_target_pairs={{0,32},{4,36},{8,40},{12,44},{16,48},{20,52},{24,56},{28,60},{32,6... | collective-permute-start | bytes 172040 | tf_op jit(solution)/shard_map/ppermute | solution.py:240
  174.0 5.7 %collective-permute-start.12 = (f32[112,128]{1,0:T(8,128)S(1)}, f32[112,128]{1,0:T(8,128)S(1)}, u32[]{:S(2)}, u32[]{:S(2)}) collective-permute-start(f32[112,128]{1,0:T(8,128)S(1)} %add_add_fusion.1), channel_id=1, source_target_pairs={{0,64},{4,68},{8,72},{12,76},{16,80},{20,84},{24,88},{28,92},{32,9... | collective-permute-start | bytes 172040 | tf_op jit(solution)/shard_map/ppermute | solution.py:240
  175.3 4.4 %collective-permute-start.13 = (f32[112,128]{1,0:T(8,128)S(1)}, f32[112,128]{1,0:T(8,128)S(1)}, u32[]{:S(2)}, u32[]{:S(2)}) collective-permute-start(f32[112,128]{1,0:T(8,128)S(1)} %add_add_fusion.1), channel_id=1, source_target_pairs={{0,96},{4,100},{8,104},{12,108},{16,112},{20,116},{24,120},{28,124... | collective-permute-start | bytes 172040 | tf_op jit(solution)/shard_map/ppermute | solution.py:240
  180.7 2.2 %copy-start.4 = (f32[6,48]{1,0:T(8,128)}, f32[6,48]{1,0:T(8,128)S(1)}, u32[]{:S(2)}) copy-start(f32[6,48]{1,0:T(8,128)S(1)} %broadcast_divide_fusion) | copy-start | bytes 3460

commit v2 on v1

--- a/solution.py
+++ b/solution.py
@@ -51,8 +51,26 @@
     return np.tile(np.array(rows * 4, np.float32)[:, None], (1, COLS))
 
 
+def interleave_matrix():
+    out = np.zeros((FEAT, 8, 8, FEAT), np.float32)
+    for j in range(FEAT):
+        for c in range(8):
+            out[j, c, c, j] = 1.0
+    return out.reshape(8 * FEAT, 8 * FEAT)
+
+
 def kernel(
-    vol_ref, filt_ref, scale_ref, lhs_ref, prior_ref, resp_ref, sec_ref, cnt_ref, shifted, feats
+    vol_ref,
+    filt_ref,
+    scale_ref,
+    lhs_ref,
+    prior_ref,
+    resp_ref,
+    moment_ref,
+    shifted,
+    feats,
+    sec_ref,
+    cnt_ref,
 ):
     octet = pl.program_id(0)
     one_tile = jnp.where(lax.broadcasted_iota(jnp.int32, (16, COLS), 0) < 3, 1.0, 0.0)
@@ -66,7 +84,7 @@
                 shifted[n, x] = row[:, MARGIN + shift : MARGIN + shift + COLS]
             return carry
 
-        lax.fori_loop(0, ROWS + 2 * MARGIN, one_row, 0)
+        lax.fori_loop(0, ROWS + 2 * MARGIN, one_row, 0, unroll=16)
         sec_ref[...] = jnp.zeros_like(sec_ref)
         cnt_ref[...] = jnp.zeros_like(cnt_ref)
 
@@ -93,9 +111,9 @@
             feats[pair * 2 + e] = part.astype(jnp.bfloat16)
         return carry
 
-    lax.fori_loop(0, 4, one_pair, 0)
-
-    def one_plane(z, carry):
+    lax.fori_loop(0, 4, one_pair, 0, unroll=4)
+
+    def expect(z):
         quads = []
         for q in range(2):
             quads.append(
@@ -126,25 +144,133 @@
                 )
                 resp_ref[2 * g + h, z] = tile
                 cnt_ref[2 * g + h] += tile
+
+    def moment(z):
         features, weighted = [], []
+        tiles = [resp_ref[k, z] for k in range(COMP)]
         for i in range(8):
             f = feats[i, z]
             f32 = f.astype(jnp.float32)
             features.append(jnp.concatenate([f, one_tile], axis=0))
             weighted.append(
                 jnp.concatenate(
-                    [(resp_ref[k, z, i : i + 1] * f32).astype(jnp.bfloat16) for k in range(COMP)],
+                    [(tiles[k][i : i + 1] * f32).astype(jnp.bfloat16) for k in range(COMP)],
                     axis=0,
                 )
             )
         f_all = jnp.concatenate(features, axis=1)
         w_all = jnp.concatenate(weighted, axis=1)
         sec_ref[...] += lax.dot_general(
-            f_all, w_all, (((1,), (1,)), ((), ())), preferred_element_type=jnp.float32
+            w_all, f_all, (((1,), (1,)), ((), ())), preferred_element_type=jnp.float32
         )
+
+    def expect_step(z, carry):
+        expect(z)
         return carry
 
-    lax.fori_loop(0, PLANES, one_plane, 0)
+    def moment_step(z, carry):
+        moment(z)
+        return carry
+
+    lax.fori_loop(0, PLANES, expect_step, 0, unroll=16)
+    lax.fori_loop(0, PLANES, moment_step, 0, unroll=16)
+
+    @pl.when(octet == pl.num_programs(0) - 1)
+    def _():
+        lane = lax.broadcasted_iota(jnp.int32, (FEAT, 128), 1)
+        for m in range(3):
+            first, second = [sec_ref[k * FEAT : (k + 1) * FEAT] for k in (2 * m, 2 * m + 1)]
+            both = jnp.concatenate([first, second], axis=1)
+            both = jnp.where(lane == FEAT + 1, jnp.sum(cnt_ref[2 * m]), both)
+            both = jnp.where(lane == 64 + FEAT + 1, jnp.sum(cnt_ref[2 * m + 1]), both)
+            moment_ref[m * FEAT : (m + 1) * FEAT] = both
+
+
+def prepare_kernel(weight_ref, mean_ref, factor_ref, order_ref, lhs_ref, prior_ref):
+    logits = weight_ref[...]
+    top = jnp.max(logits, axis=1, keepdims=True)
+    log_total = jnp.log(jnp.sum(jnp.exp(logits - top), axis=1, keepdims=True)) + top
+    on_diagonal = lax.broadcasted_iota(jnp.int32, (FEAT, FEAT), 0) == lax.broadcasted_iota(
+        jnp.int32, (FEAT, FEAT), 1
+    )
+    lane = lax.broadcasted_iota(jnp.int32, (FEAT, 256), 1)
+    half = lax.broadcasted_iota(jnp.int32, (8, COLS), 0) < 4
+    order = order_ref[...]
+    for g in range(3):
+        rows, priors = [], []
+        for h in range(2):
+            k = 2 * g + h
+            factor = factor_ref[k]
+            log_diag = jnp.sum(jnp.where(on_diagonal, jnp.log(jnp.where(on_diagonal, factor, 1.0)), 0.0))
+            prior = logits[:, k : k + 1] - log_total + log_diag - 0.5 * FEAT * math.log(2.0 * math.pi)
+            priors.append(jnp.broadcast_to(prior, (8, COLS)))
+            columns = factor.astype(jnp.bfloat16).astype(jnp.float32).T
+            offset = jnp.sum(columns * mean_ref[k : k + 1], axis=1, keepdims=True)
+            rest = -offset
+            tail = jnp.zeros((FEAT, 256), jnp.float32)
+            for t in range(3):
+                term = rest.astype(jnp.bfloat16).astype(jnp.float32)
+                tail = jnp.where(lane == 4 * FEAT + t, term, tail)
+                rest = rest - term
+            wide = jnp.concatenate([columns, jnp.zeros((FEAT, 256 - FEAT), jnp.float32)], axis=1)
+            for x in range(4):
+                moved = wide if x == 0 else pltpu.roll(wide, x * FEAT, 1)
+                rows.append((moved + tail).astype(jnp.bfloat16))
+        block = jnp.dot(order, jnp.concatenate(rows, axis=0), preferred_element_type=jnp.float32)
+        lhs_ref[g * 8 * FEAT : (g + 1) * 8 * FEAT] = block[:, :DEEP].astype(jnp.bfloat16)
+        prior_ref[g] = jnp.where(half, priors[0], priors[1])
+
+
+def vmem_specs(count):
+    return [pl.BlockSpec(memory_space=pltpu.VMEM)] * count
+
+
+def prepare(log_weights, means, prec_factor):
+    order = jnp.asarray(interleave_matrix(), jnp.bfloat16)
+    return pl.pallas_call(
+        prepare_kernel,
+        in_specs=vmem_specs(4),
+        out_specs=vmem_specs(2),
+        out_shape=[
+            jax.ShapeDtypeStruct((COMP * FEAT * 4, DEEP), jnp.bfloat16),
+            jax.ShapeDtypeStruct((3, 8, COLS), jnp.float32),
+        ],
+        cost_estimate=pl.CostEstimate(flops=10**8, bytes_accessed=2 * 10**6, transcendentals=2 * 10**4),
+        name="prepare",
+    )(log_weights.reshape(1, COMP), means, prec_factor, order)
+
+
+def finish_kernel(moment_ref, weight_ref, mean_ref, cov_ref):
+    on_diagonal = lax.broadcasted_iota(jnp.int32, (FEAT, FEAT), 0) == lax.broadcasted_iota(
+        jnp.int32, (FEAT, FEAT), 1
+    )
+    lane = lax.broadcasted_iota(jnp.int32, (1, COMP), 1)
+    counts = jnp.zeros((1, COMP), jnp.float32)
+    for k in range(COMP):
+        both = moment_ref[k // 2 * FEAT : (k // 2 + 1) * FEAT]
+        block = both[:, k % 2 * 64 : k % 2 * 64 + 64]
+        count = block[:1, FEAT + 1 : FEAT + 2]
+        column = block[:, FEAT : FEAT + 1] / count
+        row = jnp.sum(jnp.where(on_diagonal, column, 0.0), axis=0, keepdims=True)
+        cov_ref[k] = block[:, :FEAT] / count - column * row
+        mean_ref[k : k + 1] = row
+        counts = jnp.where(lane == k, count, counts)
+    weight_ref[...] = counts / jnp.sum(counts, axis=1, keepdims=True)
+
+
+def finish(moments):
+    new_weights, new_means, new_cov = pl.pallas_call(
+        finish_kernel,
+        in_specs=vmem_specs(1),
+        out_specs=vmem_specs(3),
+        out_shape=[
+            jax.ShapeDtypeStruct((1, COMP), jnp.float32),
+            jax.ShapeDtypeStruct((COMP, FEAT), jnp.float32),
+            jax.ShapeDtypeStruct((COMP, FEAT, FEAT), jnp.float32),
+        ],
+        name="finish",
+    )(moments)
+    return new_weights.reshape(COMP), new_means, new_cov
 
 
 def local_step(padded, lhs, prior):
@@ -163,47 +289,23 @@
         ],
         out_specs=[
             pl.BlockSpec((COMP, PLANES, 8, COLS), lambda o: (0, 0, o, 0)),
-            full(FEAT + 16, COMP * FEAT),
-            full(COMP, 8, COLS),
+            full(3 * FEAT, 128),
         ],
         out_shape=[
             jax.ShapeDtypeStruct((COMP, PLANES, ROWS, COLS), jnp.float32),
-            jax.ShapeDtypeStruct((FEAT + 16, COMP * FEAT), jnp.float32),
-            jax.ShapeDtypeStruct((COMP, 8, COLS), jnp.float32),
+            jax.ShapeDtypeStruct((3 * FEAT, 128), jnp.float32),
         ],
         scratch_shapes=[
             pltpu.VMEM((len(SHIFTS), ROWS + 2 * MARGIN, PLANES, COLS), jnp.bfloat16),
             pltpu.VMEM((8, PLANES, FEAT, COLS), jnp.bfloat16),
+            pltpu.VMEM((COMP * FEAT, FEAT + 16), jnp.float32),
+            pltpu.VMEM((COMP, 8, COLS), jnp.float32),
         ],
         compiler_params=pltpu.CompilerParams(
             dimension_semantics=("arbitrary",), vmem_limit_bytes=50 * 2**20
         ),
         name="mixture_step",
     )(padded, filt, scale, lhs, prior)
-
-
-def parameters(log_weights, means, prec_factor):
-    lowered = prec_factor.astype(jnp.bfloat16)
-    offsets = jnp.einsum(
-        "kij,ki->kj", lowered.astype(jnp.float32), means, precision=lax.Precision.HIGHEST
-    )
-    log_diag = jnp.sum(jnp.log(jnp.diagonal(prec_factor, axis1=1, axis2=2)), axis=1)
-    log_prior = jax.nn.log_softmax(log_weights) + log_diag - 0.5 * FEAT * math.log(2.0 * math.pi)
-    columns = jnp.transpose(lowered.reshape(3, 2, FEAT, FEAT), (0, 3, 1, 2))
-    eye = jnp.eye(4, dtype=jnp.bfloat16)
-    stacked = columns[:, :, :, None, None, :] * eye[None, None, None, :, :, None]
-    stacked = stacked.reshape(COMP * FEAT * 4, 4 * FEAT)
-    rest = -jnp.transpose(offsets.reshape(3, 2, FEAT), (0, 2, 1))
-    terms = []
-    for _ in range(3):
-        term = lax.reduce_precision(rest, 8, 7)
-        terms.append(term)
-        rest = rest - term
-    tail = jnp.stack(terms + [jnp.zeros_like(rest)] * 13, axis=-1).astype(jnp.bfloat16)
-    tail = jnp.broadcast_to(tail[:, :, :, None, :], (3, FEAT, 2, 4, 16)).reshape(-1, 16)
-    lhs = jnp.concatenate([stacked, tail], axis=1)
-    prior = jnp.broadcast_to(log_prior.reshape(3, 2, 1, 1), (3, 2, 4, COLS)).reshape(3, 8, COLS)
-    return lhs, prior
 
 
 def padded_2(cells, axis, dim, width):
@@ -243,23 +345,11 @@
 
 
 def shards(volume, log_weights, means, prec_factor):
-    lhs, prior = parameters(log_weights, means, prec_factor)
+    lhs, prior = prepare(log_weights, means, prec_factor)
     cells = padded_2(volume, "narrow", 2, MARGIN)
     cells = padded_2(cells, "wide", 1, MARGIN)
-    cells = jnp.transpose(cells, (1, 0, 2))
-    cells = jnp.pad(cells, ((0, 0), (0, 0), (0, 96)))
-    responsibility, sec, cnt = local_step(cells, lhs, prior)
-    counts = jnp.sum(cnt, axis=(1, 2))
-    flat = jnp.concatenate([sec[: FEAT + 1].reshape(-1), counts, jnp.zeros((218,), jnp.float32)])
-    flat = device_sum(flat.reshape(112, 128)).reshape(-1)
-    size = FEAT * COMP * FEAT
-    second = jnp.transpose(flat[:size].reshape(FEAT, COMP, FEAT), (1, 2, 0))
-    first = flat[size : size + COMP * FEAT].reshape(COMP, FEAT)
-    counts = flat[size + COMP * FEAT : size + COMP * FEAT + COMP]
-    new_weights = counts / jnp.sum(counts)
-    new_means = first / counts[:, None]
-    new_cov = second / counts[:, None, None] - new_means[:, :, None] * new_means[:, None, :]
-    return (responsibility, new_weights, new_means, new_cov)
+    responsibility, moments = local_step(jnp.transpose(cells, (1, 0, 2)), lhs, prior)
+    return (responsibility,) + finish(device_sum(moments))
 
 
 def solution(mesh):

time: 184 us -> 114 us (0.62)
  Pallas kernels: 122 us -> 58.4 us
  waiting for transfers between devices: 13 us -> 25.5 us
  local copies, waits for them, and re-layouts: 10 us -> 1.29 us
  other arithmetic: 6.12 us -> 1.23 us
  starting transfers between devices: 30.5 us -> 26.3 us
    pallas_call x1, Pallas kernels: 122 us -> 53.8 us  [local_step(): pl.pallas_call(kernel, grid=(ROWS // 8,), in_specs=[full(*padded.shape),...]
    pallas_call x0 -> x2, Pallas kernels: none -> 4.57 us  [the longest x1 2.65 us: prepare(): pl.pallas_call(prepare_kernel, in_specs=vmem_specs(4), out_specs=vmem_spe...]
    ppermute x6, waiting for transfers between devices: 6.29 us -> 10.4 us  [device_sum(): got.append(lax.ppermute(part, 'wide', perm))]
    ppermute x2, waiting for transfers between devices: 0.01 us -> 4.08 us  [padded_2(): before = lax.ppermute(tail, axis, [(i, i + 1) for i in range(ends)])]
    ppermute x2, waiting for transfers between devices: 2.67 us -> 5.54 us  [padded_2(): after = lax.ppermute(head, axis, [(i + 1, i) for i in range(ends)])]
    ppermute x3, starting transfers between devices: 7.24 us -> 4.89 us  [device_sum(): lax.ppermute(part, 'narrow', [(i, (i + d) % 4) for i in range(4)])]
    unnamed x15 -> x9, local copies, waits for them, and re-layouts: 3.45 us -> 1.15 us
    gather x1 -> x0, local copies, waits for them, and re-layouts: 2.09 us -> none  [parameters(): jnp.diagonal(prec_factor, axis1=1, axis2=2)]
  transfers between devices with their start and end apart: 14 -> 14, of which waited for: 7 -> 12; matrix products, arithmetic and copies ran while one was open for 5% -> 0% of each run, Pallas kernels for 0% -> 2%
where the time goes in v2:
time: 114 us; the launch traced here: 113 us
  Pallas kernels  58.4 us (51%)
  starting transfers between devices  26.3 us (23%)
  waiting for transfers between devices  25.5 us (22%)
  local copies, waits for them, and re-layouts  1.29 us (1%)
  other arithmetic  1.23 us (1%)
    pallas_call x1, Pallas kernels, local_step(): pl.pallas_call(kernel, grid=(ROWS // 8,), in_specs=[full(*padded.shape),...  53.8 us
    ppermute x6, waiting for transfers between devices, device_sum(): got.append(lax.ppermute(part, 'wide', perm))  10.4 us
    ppermute x6, starting transfers between devices, device_sum(): got.append(lax.ppermute(part, 'wide', perm))  9.93 us
    ppermute x2, waiting for transfers between devices, padded_2(): after = lax.ppermute(head, axis, [(i + 1, i) for i in range(ends)])  5.54 us
    ppermute x2, starting transfers between devices, padded_2(): before = lax.ppermute(tail, axis, [(i, i + 1) for i in range(ends)])  5.22 us
    ppermute x3, starting transfers between devices, device_sum(): lax.ppermute(part, 'narrow', [(i, (i + d) % 4) for i in range(4)])  4.89 us
    ppermute x3, waiting for transfers between devices, device_sum(): lax.ppermute(part, 'narrow', [(i, (i + d) % 4) for i in range(4)])  4.55 us
    ppermute x2, waiting for transfers between devices, padded_2(): before = lax.ppermute(tail, axis, [(i, i + 1) for i in range(ends)])  4.08 us
  transfers between devices with their start and end apart: 14, of which 12 were waited for; matrix products, arithmetic and copies ran while one was open for 0% of the time, Pallas kernels for 2%

profile of v2, /device:TPU:0, one launch (start us, length us, event | category | flops | bytes accessed | tf_op | source)
XLA Modules:
  0.0 113.4 jit_solution(8135380225227932816)
XLA Ops:
  0.6 1.1 copy.11
  1.9 3.9 %collective-permute-start = (bf16[16,64,16]{2,0,1:T(8,128)(2,1)S(1)}, bf16[16,64,16]{2,0,1:T(8,128)(2,1)S(1)}, u32[]{:S(2)}, u32[]{:S(2)}) collective-permute-start(bf16[16,64,16]{2,0,1:T(8,128)(2,1)S(1)} %get-tuple-element.20), channel_id=1, source_target_pairs={{0,1},{1,2},{2,3},{4,5},{5,6},{6,7},{8,9},{9,10},{10,11},{12,13},{... | collective-permute-start | bytes 98312 | tf_op jit(solution)/shard_map/ppermute | solution.py:316
  5.9 1.4 %collective-permute-start.1 = (bf16[16,64,16]{2,0,1:T(8,128)(2,1)S(1)}, bf16[16,64,16]{2,0,1:T(8,128)(2,1)S(1)}, u32[]{:S(2)}, u32[]{:S(2)}) collective-permute-start(bf16[16,64,16]{2,0,1:T(8,128)(2,1)S(1)} %get-tuple-element.21), channel_id=1, source_target_pairs={{1,0},{2,1},{3,2},{5,4},{6,5},{7,6},{9,8},{10,9},{11,10},{13,12},{... | collective-permute-start | bytes 98312 | tf_op jit(solution)/shard_map/ppermute | solution.py:317
  7.3 4.1 %collective-permute-done = bf16[16,64,16]{2,0,1:T(8,128)(2,1)S(1)} collective-permute-done((bf16[16,64,16]{2,0,1:T(8,128)(2,1)S(1)}, bf16[16,64,16]{2,0,1:T(8,128)(2,1)S(1)}, u32[]{:S(2)}, u32[]{:S(2)}) %collective-permute-start) | collective-permute-done | bytes 32800 | tf_op jit(solution)/shard_map/ppermute | solution.py:316
  11.4 4.5 %collective-permute-done.1 = bf16[16,64,16]{2,0,1:T(8,128)(2,1)S(1)} collective-permute-done((bf16[16,64,16]{2,0,1:T(8,128)(2,1)S(1)}, bf16[16,64,16]{2,0,1:T(8,128)(2,1)S(1)}, u32[]{:S(2)}, u32[]{:S(2)}) %collective-permute-start.1) | collective-permute-done | bytes 32800 | tf_op jit(solution)/shard_map/ppermute | solution.py:317
  15.8 0.2 pad_maximum_fusion.2
  16.0 1.3 %collective-permute-start.2 = (bf16[16,16,160]{2,0,1:T(8,128)(2,1)S(1)}, bf16[16,16,160]{2,0,1:T(8,128)(2,1)S(1)}, u32[]{:S(2)}, u32[]{:S(2)}) collective-permute-start(bf16[16,16,160]{2,0,1:T(8,128)(2,1)S(1)} %get-tuple-element.18), channel_id=1, source_target_pairs={{0,4},{4,8},{8,12},{12,16},{16,20},{20,24},{24,28},{28,32},{32,36}... | collective-permute-start | bytes 245768 | tf_op jit(solution)/shard_map/ppermute | solution.py:316
  17.3 1.3 %collective-permute-start.3 = (bf16[16,16,160]{2,0,1:T(8,128)(2,1)S(1)}, bf16[16,16,160]{2,0,1:T(8,128)(2,1)S(1)}, u32[]{:S(2)}, u32[]{:S(2)}) collective-permute-start(bf16[16,16,160]{2,0,1:T(8,128)(2,1)S(1)} %get-tuple-element.19), channel_id=1, source_target_pairs={{4,0},{8,4},{12,8},{16,12},{20,16},{24,20},{28,24},{32,28},{36,32}... | collective-permute-start | bytes 245768 | tf_op jit(solution)/shard_map/ppermute | solution.py:317
  18.6 2.6 %prepare.1 = (bf16[1152,208]{1,0:T(8,128)(2,1)}, f32[3,8,128]{2,1,0:T(8,128)}) custom-call(f32[1,6]{1,0:T(1,128)} %bitcast.4, f32[6,48]{1,0:T(8,128)} %mean_ref.1, f32[6,48,48]{2,1,0:T(8,128)} %factor_ref.1, bf16[384,384]{1,0:T(8,128)(2,1)} %constant.6.clone.order_ref), custom_call_target="tpu_custom_call" | custom-call | flops 100000000 | bytes 2000000 | tf_op jit(solution)/shard_map/prepare/pallas_call | solution.py:230
  21.3 1.1 collective-permute-done.3
  22.4 0.3 maximum_bitcast_fusion.vol_ref
  22.8 53.8 %mixture_step.1 = (f32[6,16,64,128]{3,2,1,0:T(8,128)}, f32[144,128]{1,0:T(8,128)S(1)}) custom-call(bf16[96,16,160]{2,1,0:T(8,128)(2,1)S(1)} %maximum_bitcast_fusion.vol_ref, bf16[4,256,400]{2,1,0:T(8,128)(2,1)S(1)} %copy-done, f32[48,128]{1,0:T(8,128)S(1)} %copy-done.2, bf16[1152,208]{1,0:T(8,128)(2,1)S(1)} %copy-done.1, f32[3,8,128]{2,1,0:T(8,128)S(1)} %copy-done.3), custom_call_target="tpu_custom_call" | custom-call | tf_op jit(solution)/shard_map/mixture_step/pallas_call | solution.py:280
  76.6 3.5 %collective-permute-start.4 = (f32[144,128]{1,0:T(8,128)S(1)}, f32[144,128]{1,0:T(8,128)S(1)}, u32[]{:S(2)}, u32[]{:S(2)}) collective-permute-start(f32[144,128]{1,0:T(8,128)S(1)} %get-tuple-element.14), channel_id=1, source_target_pairs={{0,4},{4,0},{8,12},{12,8},{16,20},{20,16},{24,28},{28,24},{32,36},... | collective-permute-start | bytes 221192 | tf_op jit(solution)/shard_map/ppermute | solution.py:330
  80.1 0.9 collective-permute-done.4
  81.1 1.6 %collective-permute-start.7 = (f32[144,128]{1,0:T(8,128)S(1)}, f32[144,128]{1,0:T(8,128)S(1)}, u32[]{:S(2)}, u32[]{:S(2)}) collective-permute-start(f32[144,128]{1,0:T(8,128)S(1)} %add.30), channel_id=1, source_target_pairs={{0,3},{1,0},{2,1},{3,2},{4,7},{5,4},{6,5},{7,6},{8,11},{9,8},{10,9... | collective-permute-start | bytes 221192 | tf_op jit(solution)/shard_map/ppermute | solution.py:332
  82.6 2.3 %collective-permute-start.6 = (f32[144,128]{1,0:T(8,128)S(1)}, f32[144,128]{1,0:T(8,128)S(1)}, u32[]{:S(2)}, u32[]{:S(2)}) collective-permute-start(f32[144,128]{1,0:T(8,128)S(1)} %add.30), channel_id=1, source_target_pairs={{0,2},{1,3},{2,0},{3,1},{4,6},{5,7},{6,4},{7,5},{8,10},{9,11},{10,... | collective-permute-start | bytes 221192 | tf_op jit(solution)/shard_map/ppermute | solution.py:332
  84.9 1.0 collective-permute-start.5
  86.0 3.2 %collective-permute-done.6 = f32[144,128]{1,0:T(8,128)S(1)} collective-permute-done((f32[144,128]{1,0:T(8,128)S(1)}, f32[144,128]{1,0:T(8,128)S(1)}, u32[]{:S(2)}, u32[]{:S(2)}) %collective-permute-start.6) | collective-permute-done | bytes 73760 | tf_op jit(solution)/shard_map/ppermute | solution.py:332
  89.2 1.3 %collective-permute-done.5 = f32[144,128]{1,0:T(8,128)S(1)} collective-permute-done((f32[144,128]{1,0:T(8,128)S(1)}, f32[144,128]{1,0:T(8,128)S(1)}, u32[]{:S(2)}, u32[]{:S(2)}) %collective-permute-start.5) | collective-permute-done | bytes 73760 | tf_op jit(solution)/shard_map/ppermute | solution.py:332
  90.5 4.8 %collective-permute-start.10 = (f32[144,128]{1,0:T(8,128)S(1)}, f32[144,128]{1,0:T(8,128)S(1)}, u32[]{:S(2)}, u32[]{:S(2)}) collective-permute-start(f32[144,128]{1,0:T(8,128)S(1)} %add_add_fusion.2), channel_id=1, source_target_pairs={{0,24},{4,28},{8,0},{12,4},{16,8},{20,12},{24,16},{28,20},{32,56},... | collective-permute-start | bytes 221192 | tf_op jit(solution)/shard_map/ppermute | solution.py:342
  95.3 0.9 collective-permute-start.8
  96.2 1.7 %collective-permute-done.10 = f32[144,128]{1,0:T(8,128)S(1)} collective-permute-done((f32[144,128]{1,0:T(8,128)S(1)}, f32[144,128]{1,0:T(8,128)S(1)}, u32[]{:S(2)}, u32[]{:S(2)}) %collective-permute-start.10) | collective-permute-done | bytes 73760 | tf_op jit(solution)/shard_map/ppermute | solution.py:342
  98.0 3.3 %collective-permute-done.9 = f32[144,128]{1,0:T(8,128)S(1)} collective-permute-done((f32[144,128]{1,0:T(8,128)S(1)}, f32[144,128]{1,0:T(8,128)S(1)}, u32[]{:S(2)}, u32[]{:S(2)}) %collective-permute-start.9) | collective-permute-done | bytes 73760 | tf_op jit(solution)/shard_map/ppermute | solution.py:342
  101.2 0.4 collective-permute-done.8
  101.7 1.0 collective-permute-start.13
  102.6 2.7 %collective-permute-start.12 = (f32[144,128]{1,0:T(8,128)S(1)}, f32[144,128]{1,0:T(8,128)S(1)}, u32[]{:S(2)}, u32[]{:S(2)}) collective-permute-start(f32[144,128]{1,0:T(8,128)S(1)} %add_add_fusion.1), channel_id=1, source_target_pairs={{0,64},{4,68},{8,72},{12,76},{16,80},{20,84},{24,88},{28,92},{32,9... | collective-permute-start | bytes 221192 | tf_op jit(solution)/shard_map/ppermute | solution.py:342
  105.3 0.6 collective-permute-start.11
  105.9 0.2 collective-permute-done.13
  106.1 2.4 %collective-permute-done.12 = f32[144,128]{1,0:T(8,128)S(1)} collective-permute-done((f32[144,128]{1,0:T(8,128)S(1)}, f32[144,128]{1,0:T(8,128)S(1)}, u32[]{:S(2)}, u32[]{:S(2)}) %collective-permute-start.12) | collective-permute-done | bytes 73760 | tf_op jit(solution)/shard_map/ppermute | solution.py:342
  108.5 2.4 %collective-permute-done.11 = f32[144,128]{1,0:T(8,128)S(1)} collective-permute-done((f32[144,128]{1,0:T(8,128)S(1)}, f32[144,128]{1,0:T(8,128)S(1)}, u32[]{:S(2)}, u32[]{:S(2)}) %collective-permute-start.11) | collective-permute-done | bytes 73760 | tf_op jit(solution)/shard_map/ppermute | solution.py:342
  110.9 0.6 add_add_fusion.moment_ref
  111.5 1.9 %finish.1 = (f32[1,6]{1,0:T(1,128)}, f32[6,48]{1,0:T(8,128)}, f32[6,48,48]{2,1,0:T(8,128)}) custom-call(f32[144,128]{1,0:T(8,128)} %add_add_fusion.moment_ref), custom_call_target="tpu_custom_call" | custom-call | tf_op jit(solution)/shard_map/finish/pallas_call | solution.py:262
  (15 shorter events, 0.2 us)
Async XLA Ops:
  1.9 9.5 %collective-permute-start = (bf16[16,64,16]{2,0,1:T(8,128)(2,1)S(1)}, bf16[16,64,16]{2,0,1:T(8,128)(2,1)S(1)}, u32[]{:S(2)}, u32[]{:S(2)}) collective-permute-start(bf16[16,64,16]{2,0,1:T(8,128)(2,1)S(1)} %get-tuple-element.20), channel_id=1, source_target_pairs={{0,1},{1,2},{2,3},{4,5},{5,6},{6,7},{8,9},{9,10},{10,11},{12,13},{... | collective-permute-start | bytes 98312 | tf_op jit(solution)/shard_map/ppermute | solution.py:316
  5.8 16.9 %copy-start = (bf16[4,256,400]{2,1,0:T(8,128)(2,1)S(1)}, bf16[4,256,400]{2,1,0:T(8,128)(2,1)}, u32[]{:S(2)}) copy-start(bf16[4,256,400]{2,1,0:T(8,128)(2,1)} %constant.7.clone.filt_ref) | copy-start | bytes 2457604
  5.8 16.9 %copy-start.2 = (f32[48,128]{1,0:T(8,128)S(1)}, f32[48,128]{1,0:T(8,128)}, u32[]{:S(2)}) copy-start(f32[48,128]{1,0:T(8,128)} %constant.8.clone.scale_ref) | copy-start | bytes 73732
  5.9 10.0 %collective-permute-start.1 = (bf16[16,64,16]{2,0,1:T(8,128)(2,1)S(1)}, bf16[16,64,16]{2,0,1:T(8,128)(2,1)S(1)}, u32[]{:S(2)}, u32[]{:S(2)}) collective-permute-start(bf16[16,64,16]{2,0,1:T(8,128)(2,1)S(1)} %get-tuple-element.21), channel_id=1, source_target_pairs={{1,0},{2,1},{3,2},{5,4},{6,5},{7,6},{9,8},{10,9},{11,10},{13,12},{... | collective-permute-start | bytes 98312 | tf_op jit(solution)/shard_map/ppermute | solution.py:317
  16.0 5.3 %collective-permute-start.2 = (bf16[16,16,160]{2,0,1:T(8,128)(2,1)S(1)}, bf16[16,16,160]{2,0,1:T(8,128)(2,1)S(1)}, u32[]{:S(2)}, u32[]{:S(2)}) collective-permute-start(bf16[16,16,160]{2,0,1:T(8,128)(2,1)S(1)} %get-tuple-element.18), channel_id=1, source_target_pairs={{0,4},{4,8},{8,12},{12,16},{16,20},{20,24},{24,28},{28,32},{32,36}... | collective-permute-start | bytes 245768 | tf_op jit(solution)/shard_map/ppermute | solution.py:316
  17.3 5.0 %collective-permute-start.3 = (bf16[16,16,160]{2,0,1:T(8,128)(2,1)S(1)}, bf16[16,16,160]{2,0,1:T(8,128)(2,1)S(1)}, u32[]{:S(2)}, u32[]{:S(2)}) collective-permute-start(bf16[16,16,160]{2,0,1:T(8,128)(2,1)S(1)} %get-tuple-element.19), channel_id=1, source_target_pairs={{4,0},{8,4},{12,8},{16,12},{20,16},{24,20},{28,24},{32,28},{36,32}... | collective-permute-start | bytes 245768 | tf_op jit(solution)/shard_map/ppermute | solution.py:317
  21.3 1.5 %copy-start.1 = (bf16[1152,208]{1,0:T(8,128)(2,1)S(1)}, bf16[1152,208]{1,0:T(8,128)(2,1)}, u32[]{:S(2)}) copy-start(bf16[1152,208]{1,0:T(8,128)(2,1)} %get-tuple-element.11.lhs_ref) | copy-start | bytes 1437700
  21.3 1.5 %copy-start.3 = (f32[3,8,128]{2,1,0:T(8,128)S(1)}, f32[3,8,128]{2,1,0:T(8,128)}, u32[]{:S(2)}) copy-start(f32[3,8,128]{2,1,0:T(8,128)} %get-tuple-element.12.prior_ref) | copy-start | bytes 36868
  76.6 4.5 %collective-permute-start.4 = (f32[144,128]{1,0:T(8,128)S(1)}, f32[144,128]{1,0:T(8,128)S(1)}, u32[]{:S(2)}, u32[]{:S(2)}) collective-permute-start(f32[144,128]{1,0:T(8,128)S(1)} %get-tuple-element.14), channel_id=1, source_target_pairs={{0,4},{4,0},{8,12},{12,8},{16,20},{20,16},{24,28},{28,24},{32,36},... | collective-permute-start | bytes 221192 | tf_op jit(solution)/shard_map/ppermute | solution.py:330
  81.1 4.9 %collective-permute-start.7 = (f32[144,128]{1,0:T(8,128)S(1)}, f32[144,128]{1,0:T(8,128)S(1)}, u32[]{:S(2)}, u32[]{:S(2)}) collective-permute-start(f32[144,128]{1,0:T(8,128)S(1)} %add.30), channel_id=1, source_target_pairs={{0,3},{1,0},{2,1},{3,2},{4,7},{5,4},{6,5},{7,6},{8,11},{9,8},{10,9... | collective-permute-start | bytes 221192 | tf_op jit(solution)/shard_map/ppermute | solution.py:332
  82.6 6.6 %collective-permute-start.6 = (f32[144,128]{1,0:T(8,128)S(1)}, f32[144,128]{1,0:T(8,128)S(1)}, u32[]{:S(2)}, u32[]{:S(2)}) collective-permute-start(f32[144,128]{1,0:T(8,128)S(1)} %add.30), channel_id=1, source_target_pairs={{0,2},{1,3},{2,0},{3,1},{4,6},{5,7},{6,4},{7,5},{8,10},{9,11},{10,... | collective-permute-start | bytes 221192 | tf_op jit(solution)/shard_map/ppermute | solution.py:332
  84.9 5.6 %collective-permute-start.5 = (f32[144,128]{1,0:T(8,128)S(1)}, f32[144,128]{1,0:T(8,128)S(1)}, u32[]{:S(2)}, u32[]{:S(2)}) collective-permute-start(f32[144,128]{1,0:T(8,128)S(1)} %add.30), channel_id=1, source_target_pairs={{0,1},{1,2},{2,3},{3,0},{4,5},{5,6},{6,7},{7,4},{8,9},{9,10},{10,1... | collective-permute-start | bytes 221192 | tf_op jit(solution)/shard_map/ppermute | solution.py:332
  90.5 7.5 %collective-permute-start.10 = (f32[144,128]{1,0:T(8,128)S(1)}, f32[144,128]{1,0:T(8,128)S(1)}, u32[]{:S(2)}, u32[]{:S(2)}) collective-permute-start(f32[144,128]{1,0:T(8,128)S(1)} %add_add_fusion.2), channel_id=1, source_target_pairs={{0,24},{4,28},{8,0},{12,4},{16,8},{20,12},{24,16},{28,20},{32,56},... | collective-permute-start | bytes 221192 | tf_op jit(solution)/shard_map/ppermute | solution.py:342
  95.3 6.0 %collective-permute-start.9 = (f32[144,128]{1,0:T(8,128)S(1)}, f32[144,128]{1,0:T(8,128)S(1)}, u32[]{:S(2)}, u32[]{:S(2)}) collective-permute-start(f32[144,128]{1,0:T(8,128)S(1)} %add_add_fusion.2), channel_id=1, source_target_pairs={{0,16},{4,20},{8,24},{12,28},{16,0},{20,4},{24,8},{28,12},{32,48},... | collective-permute-start | bytes 221192 | tf_op jit(solution)/shard_map/ppermute | solution.py:342
  95.3 6.4 %collective-permute-start.8 = (f32[144,128]{1,0:T(8,128)S(1)}, f32[144,128]{1,0:T(8,128)S(1)}, u32[]{:S(2)}, u32[]{:S(2)}) collective-permute-start(f32[144,128]{1,0:T(8,128)S(1)} %add_add_fusion.2), channel_id=1, source_target_pairs={{0,8},{4,12},{8,16},{12,20},{16,24},{20,28},{24,0},{28,4},{32,40},... | collective-permute-start | bytes 221192 | tf_op jit(solution)/shard_map/ppermute | solution.py:342
  101.7 4.4 %collective-permute-start.13 = (f32[144,128]{1,0:T(8,128)S(1)}, f32[144,128]{1,0:T(8,128)S(1)}, u32[]{:S(2)}, u32[]{:S(2)}) collective-permute-start(f32[144,128]{1,0:T(8,128)S(1)} %add_add_fusion.1), channel_id=1, source_target_pairs={{0,96},{4,100},{8,104},{12,108},{16,112},{20,116},{24,120},{28,124... | collective-permute-start | bytes 221192 | tf_op jit(solution)/shard_map/ppermute | solution.py:342
  102.6 5.9 %collective-permute-start.12 = (f32[144,128]{1,0:T(8,128)S(1)}, f32[144,128]{1,0:T(8,128)S(1)}, u32[]{:S(2)}, u32[]{:S(2)}) collective-permute-start(f32[144,128]{1,0:T(8,128)S(1)} %add_add_fusion.1), channel_id=1, source_target_pairs={{0,64},{4,68},{8,72},{12,76},{16,80},{20,84},{24,88},{28,92},{32,9... | collective-permute-start | bytes 221192 | tf_op jit(solution)/shard_map/ppermute | solution.py:342
  105.3 5.6 %collective-permute-start.11 = (f32[144,128]{1,0:T(8,128)S(1)}, f32[144,128]{1,0:T(8,128)S(1)}, u32[]{:S(2)}, u32[]{:S(2)}) collective-permute-start(f32[144,128]{1,0:T(8,128)S(1)} %add_add_fusion.1), channel_id=1, source_target_pairs={{0,32},{4,36},{8,40},{12,44},{16,48},{20,52},{24,56},{28,60},{32,6... | collective-permute-start | bytes 221192 | tf_op jit(solution)/shard_map/ppermute | solution.py:342

commit v3 on v2

--- a/solution.py
+++ b/solution.py
@@ -60,7 +60,11 @@
 
 
 def kernel(
-    vol_ref,
+    before_ref,
+    rows_ref,
+    after_ref,
+    left_ref,
+    right_ref,
     filt_ref,
     scale_ref,
     lhs_ref,
@@ -78,13 +82,31 @@
 
     @pl.when(octet == 0)
     def _():
-        def one_row(x, carry):
-            row = vol_ref[x]
-            for n, shift in enumerate(SHIFTS):
-                shifted[n, x] = row[:, MARGIN + shift : MARGIN + shift + COLS]
+        def fill(x, get_row, left, right):
+            for m in range(8):
+                row = get_row(m)
+                for n, shift in enumerate(SHIFTS):
+                    if shift < 0:
+                        edge = left[:, 16 * m + 16 + shift : 16 * m + 16]
+                        moved = jnp.concatenate([edge, row[:, : COLS + shift]], axis=1)
+                    elif shift > 0:
+                        edge = right[:, 16 * m : 16 * m + shift]
+                        moved = jnp.concatenate([row[:, shift:], edge], axis=1)
+                    else:
+                        moved = row
+                    shifted[n, x + m] = moved
+
+        for g in range(2):
+            get_before = lambda m: before_ref[8 * g + m]
+            get_after = lambda m: after_ref[8 * g + m]
+            fill(8 * g, get_before, before_ref[16 + g], before_ref[18 + g])
+            fill(MARGIN + ROWS + 8 * g, get_after, after_ref[16 + g], after_ref[18 + g])
+
+        def one_group(g, carry):
+            fill(MARGIN + 8 * g, lambda m: rows_ref[8 * g + m], left_ref[g], right_ref[g])
             return carry
 
-        lax.fori_loop(0, ROWS + 2 * MARGIN, one_row, 0, unroll=16)
+        lax.fori_loop(0, ROWS // 8, one_group, 0, unroll=2)
         sec_ref[...] = jnp.zeros_like(sec_ref)
         cnt_ref[...] = jnp.zeros_like(cnt_ref)
 
@@ -240,14 +262,15 @@
     )(log_weights.reshape(1, COMP), means, prec_factor, order)
 
 
-def finish_kernel(moment_ref, weight_ref, mean_ref, cov_ref):
+def finish_kernel(a_ref, b_ref, c_ref, d_ref, weight_ref, mean_ref, cov_ref):
     on_diagonal = lax.broadcasted_iota(jnp.int32, (FEAT, FEAT), 0) == lax.broadcasted_iota(
         jnp.int32, (FEAT, FEAT), 1
     )
     lane = lax.broadcasted_iota(jnp.int32, (1, COMP), 1)
     counts = jnp.zeros((1, COMP), jnp.float32)
     for k in range(COMP):
-        both = moment_ref[k // 2 * FEAT : (k // 2 + 1) * FEAT]
+        at = slice(k // 2 * FEAT, (k // 2 + 1) * FEAT)
+        both = (a_ref[at] + b_ref[at]) + (c_ref[at] + d_ref[at])
         block = both[:, k % 2 * 64 : k % 2 * 64 + 64]
         count = block[:1, FEAT + 1 : FEAT + 2]
         column = block[:, FEAT : FEAT + 1] / count
@@ -258,10 +281,10 @@
     weight_ref[...] = counts / jnp.sum(counts, axis=1, keepdims=True)
 
 
-def finish(moments):
+def finish(*parts):
     new_weights, new_means, new_cov = pl.pallas_call(
         finish_kernel,
-        in_specs=vmem_specs(1),
+        in_specs=vmem_specs(4),
         out_specs=vmem_specs(3),
         out_shape=[
             jax.ShapeDtypeStruct((1, COMP), jnp.float32),
@@ -269,11 +292,11 @@
             jax.ShapeDtypeStruct((COMP, FEAT, FEAT), jnp.float32),
         ],
         name="finish",
-    )(moments)
+    )(*parts)
     return new_weights.reshape(COMP), new_means, new_cov
 
 
-def local_step(padded, lhs, prior):
+def local_step(pieces, lhs, prior):
     filt = jnp.asarray(filter_matrix(), jnp.bfloat16)
     scale = jnp.asarray(feature_scale())
     full = lambda *shape: pl.BlockSpec(shape, lambda o: (0,) * len(shape))
@@ -281,7 +304,7 @@
         kernel,
         grid=(ROWS // 8,),
         in_specs=[
-            full(*padded.shape),
+            *[full(*piece.shape) for piece in pieces],
             full(*filt.shape),
             full(*scale.shape),
             full(*lhs.shape),
@@ -305,17 +328,32 @@
             dimension_semantics=("arbitrary",), vmem_limit_bytes=50 * 2**20
         ),
         name="mixture_step",
-    )(padded, filt, scale, lhs, prior)
-
-
-def padded_2(cells, axis, dim, width):
-    count = lax.axis_size(axis)
-    ends = count - 1
-    head = lax.slice_in_dim(cells, 0, width, axis=dim)
-    tail = lax.slice_in_dim(cells, cells.shape[dim] - width, cells.shape[dim], axis=dim)
-    before = lax.ppermute(tail, axis, [(i, i + 1) for i in range(ends)])
-    after = lax.ppermute(head, axis, [(i + 1, i) for i in range(ends)])
-    return jnp.concatenate([before, cells, after], axis=dim)
+    )(*pieces, filt, scale, lhs, prior)
+
+
+def pack_kernel(rows_ref, head_ref, tail_ref):
+    for n in range(ROWS // 8):
+        group = [rows_ref[8 * n + m] for m in range(8)]
+        head_ref[n] = jnp.concatenate([row[:, :MARGIN] for row in group], axis=1)
+        tail_ref[n] = jnp.concatenate([row[:, COLS - MARGIN :] for row in group], axis=1)
+
+
+def pack(rows):
+    shape = jax.ShapeDtypeStruct((ROWS // 8, PLANES, COLS), jnp.bfloat16)
+    return pl.pallas_call(
+        pack_kernel,
+        in_specs=vmem_specs(1),
+        out_specs=vmem_specs(2),
+        out_shape=[shape, shape],
+        name="pack",
+    )(rows)
+
+
+def neighbours(to_next, to_previous, axis):
+    ends = lax.axis_size(axis) - 1
+    before = lax.ppermute(to_next, axis, [(i, i + 1) for i in range(ends)])
+    after = lax.ppermute(to_previous, axis, [(i + 1, i) for i in range(ends)])
+    return before, after
 
 
 def wide_perm(move):
@@ -340,16 +378,22 @@
             else:
                 perm = wide_perm(lambda x, y, c: ((x + d) % 4, y, c))
             got.append(lax.ppermute(part, "wide", perm))
-        part = (part + got[0]) + (got[1] + got[2])
-    return part
+        if axis == 0:
+            part = (part + got[0]) + (got[1] + got[2])
+    return [part] + got
 
 
 def shards(volume, log_weights, means, prec_factor):
+    rows = jnp.transpose(volume, (1, 0, 2))
+    head, tail = pack(rows)
+    left, right = neighbours(tail, head, "narrow")
     lhs, prior = prepare(log_weights, means, prec_factor)
-    cells = padded_2(volume, "narrow", 2, MARGIN)
-    cells = padded_2(cells, "wide", 1, MARGIN)
-    responsibility, moments = local_step(jnp.transpose(cells, (1, 0, 2)), lhs, prior)
-    return (responsibility,) + finish(device_sum(moments))
+    left, right, lhs = lax.optimization_barrier((left, right, lhs))
+    bottom = jnp.concatenate([rows[ROWS - MARGIN :], left[6:], right[6:]], axis=0)
+    top = jnp.concatenate([rows[:MARGIN], left[:2], right[:2]], axis=0)
+    before, after = neighbours(bottom, top, "wide")
+    responsibility, moments = local_step((before, rows, after, left, right), lhs, prior)
+    return (responsibility,) + finish(*device_sum(moments))
 
 
 def solution(mesh):

time: 114 us -> 118 us (1.035)
  local copies, waits for them, and re-layouts: 1.29 us -> 8.03 us
  waiting for transfers between devices: 25.5 us -> 22 us
  Pallas kernels: 58.4 us -> 60.9 us
    unnamed x9 -> x19, local copies, waits for them, and re-layouts: 1.15 us -> 7.14 us
    ppermute x4, waiting for transfers between devices: 9.62 us -> 4.86 us  [the longest x2 4.85 us: neighbours(): after = lax.ppermute(to_previous, axis, [(i + 1, i) for i in range(ends)])]
    pallas_call x2 -> x3, Pallas kernels: 55.8 us -> 58.2 us  [the longest x1 54.4 us: local_step(): pl.pallas_call(kernel, grid=(ROWS // 8,), in_specs=[*[full(*piece.shape)...]
    ppermute x3, waiting for transfers between devices: 4.55 us -> 5.74 us  [device_sum(): lax.ppermute(part, 'narrow', [(i, (i + d) % 4) for i in range(4)])]
  transfers between devices with their start and end apart: 14 -> 14, of which waited for: 12 -> 12; matrix products, arithmetic and copies ran while one was open for 0% -> 1% of each run, Pallas kernels for 2% -> 2%
where the time goes in v3:
time: 118 us
  Pallas kernels  60.9 us (52%)
  starting transfers between devices  25.9 us (22%)
  waiting for transfers between devices  22 us (19%)
  local copies, waits for them, and re-layouts  8.03 us (7%)
    pallas_call x1, Pallas kernels, local_step(): pl.pallas_call(kernel, grid=(ROWS // 8,), in_specs=[*[full(*piece.shape)...  54.4 us
    ppermute x6, waiting for transfers between devices, device_sum(): got.append(lax.ppermute(part, 'wide', perm))  10.5 us
    ppermute x6, starting transfers between devices, device_sum(): got.append(lax.ppermute(part, 'wide', perm))  9.93 us
    unnamed x19, local copies, waits for them, and re-layouts  7.14 us
    ppermute x3, waiting for transfers between devices, device_sum(): lax.ppermute(part, 'narrow', [(i, (i + d) % 4) for i in range(4)])  5.74 us
    ppermute x2, starting transfers between devices, neighbours(): before = lax.ppermute(to_next, axis, [(i, i + 1) for i in range(ends)])  5.19 us
    ppermute x3, starting transfers between devices, device_sum(): lax.ppermute(part, 'narrow', [(i, (i + d) % 4) for i in range(4)])  5.08 us
    ppermute x2, waiting for transfers between devices, neighbours(): after = lax.ppermute(to_previous, axis, [(i + 1, i) for i in range(ends)])  4.85 us
  transfers between devices with their start and end apart: 14, of which 12 were waited for; matrix products, arithmetic and copies ran while one was open for 1% of the time, Pallas kernels for 2%

profile of v3, /device:TPU:0, one launch (start us, length us, event | category | flops | bytes accessed | tf_op | source)
XLA Modules:
  0.0 117.6 jit_solution(1867764365064263577)
XLA Ops:
  0.6 1.8 %copy.13 = bf16[16,64,128]{2,0,1:T(8,128)(2,1)} copy(bf16[16,64,128]{2,1,0:T(8,128)(2,1)} %param.7) | data formatting | bytes 524288 | tf_op args[0]
  2.5 1.8 %pack.1 = (bf16[8,16,128]{2,1,0:T(8,128)(2,1)}, bf16[8,16,128]{2,1,0:T(8,128)(2,1)}) custom-call(bf16[64,16,128]{2,1,0:T(8,128)(2,1)} %bitcast.5), custom_call_target="tpu_custom_call" | custom-call | tf_op jit(solution)/shard_map/pack/pallas_call | solution.py:343
  4.2 3.9 %collective-permute-start = (bf16[8,16,128]{2,1,0:T(8,128)(2,1)}, bf16[8,16,128]{2,1,0:T(8,128)(2,1)S(1)}, u32[]{:S(2)}, u32[]{:S(2)}) collective-permute-start(bf16[8,16,128]{2,1,0:T(8,128)(2,1)} %get-tuple-element.16), channel_id=1, source_target_pairs={{0,1},{1,2},{2,3},{4,5},{5,6},{6,7},{8,9},{9,10},{10,11},{12,13},{... | collective-permute-start | bytes 98312 | tf_op jit(solution)/shard_map/ppermute | solution.py:354
  8.1 1.3 %collective-permute-start.1 = (bf16[8,16,128]{2,1,0:T(8,128)(2,1)}, bf16[8,16,128]{2,1,0:T(8,128)(2,1)S(1)}, u32[]{:S(2)}, u32[]{:S(2)}) collective-permute-start(bf16[8,16,128]{2,1,0:T(8,128)(2,1)} %get-tuple-element.17), channel_id=1, source_target_pairs={{1,0},{2,1},{3,2},{5,4},{6,5},{7,6},{9,8},{10,9},{11,10},{13,12},{... | collective-permute-start | bytes 98312 | tf_op jit(solution)/shard_map/ppermute | solution.py:355
  9.4 0.9 fusion
  10.3 2.6 %prepare.1 = (bf16[1152,208]{1,0:T(8,128)(2,1)}, f32[3,8,128]{2,1,0:T(8,128)}) custom-call(f32[1,6]{1,0:T(1,128)} %bitcast.8, f32[6,48]{1,0:T(8,128)} %mean_ref.1, f32[6,48,48]{2,1,0:T(8,128)} %factor_ref.1, bf16[384,384]{1,0:T(8,128)(2,1)} %constant.6.clone.order_ref), custom_call_target="tpu_custom_call" | custom-call | flops 100000000 | bytes 2000000 | tf_op jit(solution)/shard_map/prepare/pallas_call | solution.py:252
  13.0 1.2 %collective-permute-done.1.right_ref = bf16[8,16,128]{2,1,0:T(8,128)(2,1)S(1)} collective-permute-done((bf16[8,16,128]{2,1,0:T(8,128)(2,1)}, bf16[8,16,128]{2,1,0:T(8,128)(2,1)S(1)}, u32[]{:S(2)}, u32[]{:S(2)}) %collective-permute-start.1) | collective-permute-done | bytes 32800 | tf_op jit(solution)/shard_map/ppermute | solution.py:355
  14.2 1.3 %collective-permute-start.2 = (bf16[20,16,128]{2,1,0:T(8,128)(2,1)S(1)}, bf16[20,16,128]{2,1,0:T(8,128)(2,1)S(1)}, u32[]{:S(2)}, u32[]{:S(2)}) collective-permute-start(bf16[20,16,128]{2,1,0:T(8,128)(2,1)S(1)} %pad_maximum_fusion), channel_id=1, source_target_pairs={{0,4},{4,8},{8,12},{12,16},{16,20},{20,24},{24,28},{28,32},{32,36}... | collective-permute-start | bytes 245768 | tf_op jit(solution)/shard_map/ppermute | solution.py:354
  15.5 1.3 %collective-permute-start.3 = (bf16[20,16,128]{2,1,0:T(8,128)(2,1)S(1)}, bf16[20,16,128]{2,1,0:T(8,128)(2,1)S(1)}, u32[]{:S(2)}, u32[]{:S(2)}) collective-permute-start(bf16[20,16,128]{2,1,0:T(8,128)(2,1)S(1)} %pad_maximum_fusion.1), channel_id=1, source_target_pairs={{4,0},{8,4},{12,8},{16,12},{20,16},{24,20},{28,24},{32,28},{36,32}... | collective-permute-start | bytes 245768 | tf_op jit(solution)/shard_map/ppermute | solution.py:355
  16.8 3.7 %collective-permute-done.3.after_ref = bf16[20,16,128]{2,1,0:T(8,128)(2,1)S(1)} collective-permute-done((bf16[20,16,128]{2,1,0:T(8,128)(2,1)S(1)}, bf16[20,16,128]{2,1,0:T(8,128)(2,1)S(1)}, u32[]{:S(2)}, u32[]{:S(2)}) %collective-permute-start.3) | collective-permute-done | bytes 81952 | tf_op jit(solution)/shard_map/ppermute | solution.py:355
  20.5 0.9 copy-done
  21.4 1.2 %copy-done.1 = bf16[4,256,400]{2,1,0:T(8,128)(2,1)S(1)} copy-done((bf16[4,256,400]{2,1,0:T(8,128)(2,1)S(1)}, bf16[4,256,400]{2,1,0:T(8,128)(2,1)}, u32[]{:S(2)}) %copy-start.1) | copy-done | bytes 819224
  22.7 1.1 copy-done.2
  23.7 0.7 copy-done.3
  24.5 0.7 copy-done.4
  25.2 54.4 %mixture_step.1 = (f32[6,16,64,128]{3,2,1,0:T(8,128)}, f32[144,128]{1,0:T(8,128)S(1)}) custom-call(bf16[20,16,128]{2,1,0:T(8,128)(2,1)S(1)} %collective-permute-done.2.before_ref, bf16[64,16,128]{2,1,0:T(8,128)(2,1)S(1)} %bitcast.7, bf16[20,16,128]{2,1,0:T(8,128)(2,1)S(1)} %collective-permute-done.3.after_ref, ...), custom_call_target="tpu_custom_call" | custom-call | tf_op jit(solution)/shard_map/mixture_step/pallas_call | solution.py:303
  79.6 3.1 %collective-permute-start.4 = (f32[144,128]{1,0:T(8,128)S(1)}, f32[144,128]{1,0:T(8,128)S(1)}, u32[]{:S(2)}, u32[]{:S(2)}) collective-permute-start(f32[144,128]{1,0:T(8,128)S(1)} %get-tuple-element.24), channel_id=1, source_target_pairs={{0,4},{4,0},{8,12},{12,8},{16,20},{20,16},{24,28},{28,24},{32,36},... | collective-permute-start | bytes 221192 | tf_op jit(solution)/shard_map/ppermute | solution.py:368
  82.7 0.9 collective-permute-done.4
  83.6 3.7 %collective-permute-start.7 = (f32[144,128]{1,0:T(8,128)S(1)}, f32[144,128]{1,0:T(8,128)S(1)}, u32[]{:S(2)}, u32[]{:S(2)}) collective-permute-start(f32[144,128]{1,0:T(8,128)S(1)} %add.21), channel_id=1, source_target_pairs={{0,3},{1,0},{2,1},{3,2},{4,7},{5,4},{6,5},{7,6},{8,11},{9,8},{10,9... | collective-permute-start | bytes 221192 | tf_op jit(solution)/shard_map/ppermute | solution.py:370
  87.7 1.0 collective-permute-start.5
  88.7 2.3 %collective-permute-done.7 = f32[144,128]{1,0:T(8,128)S(1)} collective-permute-done((f32[144,128]{1,0:T(8,128)S(1)}, f32[144,128]{1,0:T(8,128)S(1)}, u32[]{:S(2)}, u32[]{:S(2)}) %collective-permute-start.7) | collective-permute-done | bytes 73760 | tf_op jit(solution)/shard_map/ppermute | solution.py:370
  90.9 2.9 %collective-permute-done.6 = f32[144,128]{1,0:T(8,128)S(1)} collective-permute-done((f32[144,128]{1,0:T(8,128)S(1)}, f32[144,128]{1,0:T(8,128)S(1)}, u32[]{:S(2)}, u32[]{:S(2)}) %collective-permute-start.6) | collective-permute-done | bytes 73760 | tf_op jit(solution)/shard_map/ppermute | solution.py:370
  94.4 4.8 %collective-permute-start.10 = (f32[144,128]{1,0:T(8,128)S(1)}, f32[144,128]{1,0:T(8,128)S(1)}, u32[]{:S(2)}, u32[]{:S(2)}) collective-permute-start(f32[144,128]{1,0:T(8,128)S(1)} %add_add_fusion.1), channel_id=1, source_target_pairs={{0,24},{4,28},{8,0},{12,4},{16,8},{20,12},{24,16},{28,20},{32,56},... | collective-permute-start | bytes 221192 | tf_op jit(solution)/shard_map/ppermute | solution.py:380
  99.2 0.9 collective-permute-start.8
  100.2 2.1 %collective-permute-done.10 = f32[144,128]{1,0:T(8,128)S(1)} collective-permute-done((f32[144,128]{1,0:T(8,128)S(1)}, f32[144,128]{1,0:T(8,128)S(1)}, u32[]{:S(2)}, u32[]{:S(2)}) %collective-permute-start.10) | collective-permute-done | bytes 73760 | tf_op jit(solution)/shard_map/ppermute | solution.py:380
  102.3 2.9 %collective-permute-done.9 = f32[144,128]{1,0:T(8,128)S(1)} collective-permute-done((f32[144,128]{1,0:T(8,128)S(1)}, f32[144,128]{1,0:T(8,128)S(1)}, u32[]{:S(2)}, u32[]{:S(2)}) %collective-permute-start.9) | collective-permute-done | bytes 73760 | tf_op jit(solution)/shard_map/ppermute | solution.py:380
  105.7 0.9 collective-permute-start.13
  106.6 2.8 %collective-permute-start.12 = (f32[144,128]{1,0:T(8,128)S(1)}, f32[144,128]{1,0:T(8,128)S(1)}, u32[]{:S(2)}, u32[]{:S(2)}) collective-permute-start(f32[144,128]{1,0:T(8,128)S(1)} %add_add_fusion.a_ref), channel_id=1, source_target_pairs={{0,64},{4,68},{8,72},{12,76},{16,80},{20,84},{24,88},{28,92},{32,9... | collective-permute-start | bytes 221192 | tf_op jit(solution)/shard_map/ppermute | solution.py:380
  110.4 2.2 %collective-permute-done.12.c_ref = f32[144,128]{1,0:T(8,128)S(1)} collective-permute-done((f32[144,128]{1,0:T(8,128)S(1)}, f32[144,128]{1,0:T(8,128)S(1)}, u32[]{:S(2)}, u32[]{:S(2)}) %collective-permute-start.12) | collective-permute-done | bytes 73760 | tf_op jit(solution)/shard_map/ppermute | solution.py:380
  112.5 2.4 %collective-permute-done.11.b_ref = f32[144,128]{1,0:T(8,128)S(1)} collective-permute-done((f32[144,128]{1,0:T(8,128)S(1)}, f32[144,128]{1,0:T(8,128)S(1)}, u32[]{:S(2)}, u32[]{:S(2)}) %collective-permute-start.11) | collective-permute-done | bytes 73760 | tf_op jit(solution)/shard_map/ppermute | solution.py:380
  114.9 0.6 copy-done.8
  115.5 2.0 %finish.1 = (f32[1,6]{1,0:T(1,128)}, f32[6,48]{1,0:T(8,128)}, f32[6,48,48]{2,1,0:T(8,128)}) custom-call(f32[144,128]{1,0:T(8,128)} %copy-done.5, f32[144,128]{1,0:T(8,128)} %copy-done.8, f32[144,128]{1,0:T(8,128)} %copy-done.7, f32[144,128]{1,0:T(8,128)} %copy-done.6), custom_call_target="tpu_custom_call" | custom-call | tf_op jit(solution)/shard_map/finish/pallas_call | solution.py:285
  (26 shorter events, 2.6 us)
Async XLA Ops:
  4.2 8.7 %collective-permute-start = (bf16[8,16,128]{2,1,0:T(8,128)(2,1)}, bf16[8,16,128]{2,1,0:T(8,128)(2,1)S(1)}, u32[]{:S(2)}, u32[]{:S(2)}) collective-permute-start(bf16[8,16,128]{2,1,0:T(8,128)(2,1)} %get-tuple-element.16), channel_id=1, source_target_pairs={{0,1},{1,2},{2,3},{4,5},{5,6},{6,7},{8,9},{9,10},{10,11},{12,13},{... | collective-permute-start | bytes 98312 | tf_op jit(solution)/shard_map/ppermute | solution.py:354
  8.1 6.0 %collective-permute-start.1 = (bf16[8,16,128]{2,1,0:T(8,128)(2,1)}, bf16[8,16,128]{2,1,0:T(8,128)(2,1)S(1)}, u32[]{:S(2)}, u32[]{:S(2)}) collective-permute-start(bf16[8,16,128]{2,1,0:T(8,128)(2,1)} %get-tuple-element.17), channel_id=1, source_target_pairs={{1,0},{2,1},{3,2},{5,4},{6,5},{7,6},{9,8},{10,9},{11,10},{13,12},{... | collective-permute-start | bytes 98312 | tf_op jit(solution)/shard_map/ppermute | solution.py:355
  14.2 2.6 %collective-permute-start.2 = (bf16[20,16,128]{2,1,0:T(8,128)(2,1)S(1)}, bf16[20,16,128]{2,1,0:T(8,128)(2,1)S(1)}, u32[]{:S(2)}, u32[]{:S(2)}) collective-permute-start(bf16[20,16,128]{2,1,0:T(8,128)(2,1)S(1)} %pad_maximum_fusion), channel_id=1, source_target_pairs={{0,4},{4,8},{8,12},{12,16},{16,20},{20,24},{24,28},{28,32},{32,36}... | collective-permute-start | bytes 245768 | tf_op jit(solution)/shard_map/ppermute | solution.py:354
  15.5 5.0 %collective-permute-start.3 = (bf16[20,16,128]{2,1,0:T(8,128)(2,1)S(1)}, bf16[20,16,128]{2,1,0:T(8,128)(2,1)S(1)}, u32[]{:S(2)}, u32[]{:S(2)}) collective-permute-start(bf16[20,16,128]{2,1,0:T(8,128)(2,1)S(1)} %pad_maximum_fusion.1), channel_id=1, source_target_pairs={{4,0},{8,4},{12,8},{16,12},{20,16},{24,20},{28,24},{32,28},{36,32}... | collective-permute-start | bytes 245768 | tf_op jit(solution)/shard_map/ppermute | solution.py:355
  20.5 1.0 copy-start
  21.4 1.2 %copy-start.1 = (bf16[4,256,400]{2,1,0:T(8,128)(2,1)S(1)}, bf16[4,256,400]{2,1,0:T(8,128)(2,1)}, u32[]{:S(2)}) copy-start(bf16[4,256,400]{2,1,0:T(8,128)(2,1)} %constant.7.clone.filt_ref) | copy-start | bytes 2457604
  22.6 1.1 copy-start.2
  23.7 0.7 copy-start.3
  24.5 0.7 copy-start.4
  79.6 4.0 %collective-permute-start.4 = (f32[144,128]{1,0:T(8,128)S(1)}, f32[144,128]{1,0:T(8,128)S(1)}, u32[]{:S(2)}, u32[]{:S(2)}) collective-permute-start(f32[144,128]{1,0:T(8,128)S(1)} %get-tuple-element.24), channel_id=1, source_target_pairs={{0,4},{4,0},{8,12},{12,8},{16,20},{20,16},{24,28},{28,24},{32,36},... | collective-permute-start | bytes 221192 | tf_op jit(solution)/shard_map/ppermute | solution.py:368
  83.6 7.3 %collective-permute-start.7 = (f32[144,128]{1,0:T(8,128)S(1)}, f32[144,128]{1,0:T(8,128)S(1)}, u32[]{:S(2)}, u32[]{:S(2)}) collective-permute-start(f32[144,128]{1,0:T(8,128)S(1)} %add.21), channel_id=1, source_target_pairs={{0,3},{1,0},{2,1},{3,2},{4,7},{5,4},{6,5},{7,6},{8,11},{9,8},{10,9... | collective-permute-start | bytes 221192 | tf_op jit(solution)/shard_map/ppermute | solution.py:370
  87.3 6.5 %collective-permute-start.6 = (f32[144,128]{1,0:T(8,128)S(1)}, f32[144,128]{1,0:T(8,128)S(1)}, u32[]{:S(2)}, u32[]{:S(2)}) collective-permute-start(f32[144,128]{1,0:T(8,128)S(1)} %add.21), channel_id=1, source_target_pairs={{0,2},{1,3},{2,0},{3,1},{4,6},{5,7},{6,4},{7,5},{8,10},{9,11},{10,... | collective-permute-start | bytes 221192 | tf_op jit(solution)/shard_map/ppermute | solution.py:370
  87.7 6.8 %collective-permute-start.5 = (f32[144,128]{1,0:T(8,128)S(1)}, f32[144,128]{1,0:T(8,128)S(1)}, u32[]{:S(2)}, u32[]{:S(2)}) collective-permute-start(f32[144,128]{1,0:T(8,128)S(1)} %add.21), channel_id=1, source_target_pairs={{0,1},{1,2},{2,3},{3,0},{4,5},{5,6},{6,7},{7,4},{8,9},{9,10},{10,1... | collective-permute-start | bytes 221192 | tf_op jit(solution)/shard_map/ppermute | solution.py:370
  94.4 7.8 %collective-permute-start.10 = (f32[144,128]{1,0:T(8,128)S(1)}, f32[144,128]{1,0:T(8,128)S(1)}, u32[]{:S(2)}, u32[]{:S(2)}) collective-permute-start(f32[144,128]{1,0:T(8,128)S(1)} %add_add_fusion.1), channel_id=1, source_target_pairs={{0,24},{4,28},{8,0},{12,4},{16,8},{20,12},{24,16},{28,20},{32,56},... | collective-permute-start | bytes 221192 | tf_op jit(solution)/shard_map/ppermute | solution.py:380
  99.2 6.0 %collective-permute-start.9 = (f32[144,128]{1,0:T(8,128)S(1)}, f32[144,128]{1,0:T(8,128)S(1)}, u32[]{:S(2)}, u32[]{:S(2)}) collective-permute-start(f32[144,128]{1,0:T(8,128)S(1)} %add_add_fusion.1), channel_id=1, source_target_pairs={{0,16},{4,20},{8,24},{12,28},{16,0},{20,4},{24,8},{28,12},{32,48},... | collective-permute-start | bytes 221192 | tf_op jit(solution)/shard_map/ppermute | solution.py:380
  99.2 6.5 %collective-permute-start.8 = (f32[144,128]{1,0:T(8,128)S(1)}, f32[144,128]{1,0:T(8,128)S(1)}, u32[]{:S(2)}, u32[]{:S(2)}) collective-permute-start(f32[144,128]{1,0:T(8,128)S(1)} %add_add_fusion.1), channel_id=1, source_target_pairs={{0,8},{4,12},{8,16},{12,20},{16,24},{20,28},{24,0},{28,4},{32,40},... | collective-permute-start | bytes 221192 | tf_op jit(solution)/shard_map/ppermute | solution.py:380
  105.7 9.2 %copy-start.5 = (f32[144,128]{1,0:T(8,128)}, f32[144,128]{1,0:T(8,128)S(1)}, u32[]{:S(2)}) copy-start(f32[144,128]{1,0:T(8,128)S(1)} %add_add_fusion.a_ref) | copy-start | bytes 221188
  105.7 4.7 %collective-permute-start.13 = (f32[144,128]{1,0:T(8,128)S(1)}, f32[144,128]{1,0:T(8,128)S(1)}, u32[]{:S(2)}, u32[]{:S(2)}) collective-permute-start(f32[144,128]{1,0:T(8,128)S(1)} %add_add_fusion.a_ref), channel_id=1, source_target_pairs={{0,96},{4,100},{8,104},{12,108},{16,112},{20,116},{24,120},{28,124... | collective-permute-start | bytes 221192 | tf_op jit(solution)/shard_map/ppermute | solution.py:380
  106.6 6.0 %collective-permute-start.12 = (f32[144,128]{1,0:T(8,128)S(1)}, f32[144,128]{1,0:T(8,128)S(1)}, u32[]{:S(2)}, u32[]{:S(2)}) collective-permute-start(f32[144,128]{1,0:T(8,128)S(1)} %add_add_fusion.a_ref), channel_id=1, source_target_pairs={{0,64},{4,68},{8,72},{12,76},{16,80},{20,84},{24,88},{28,92},{32,9... | collective-permute-start | bytes 221192 | tf_op jit(solution)/shard_map/ppermute | solution.py:380
  109.3 5.6 %collective-permute-start.11 = (f32[144,128]{1,0:T(8,128)S(1)}, f32[144,128]{1,0:T(8,128)S(1)}, u32[]{:S(2)}, u32[]{:S(2)}) collective-permute-start(f32[144,128]{1,0:T(8,128)S(1)} %add_add_fusion.a_ref), channel_id=1, source_target_pairs={{0,32},{4,36},{8,40},{12,44},{16,48},{20,52},{24,56},{28,60},{32,6... | collective-permute-start | bytes 221192 | tf_op jit(solution)/shard_map/ppermute | solution.py:380
  110.4 4.5 %copy-start.6 = (f32[144,128]{1,0:T(8,128)}, f32[144,128]{1,0:T(8,128)S(1)}, u32[]{:S(2)}) copy-start(f32[144,128]{1,0:T(8,128)S(1)} %collective-permute-done.13.d_ref) | copy-start | bytes 221188
  112.5 2.4 %copy-start.7 = (f32[144,128]{1,0:T(8,128)}, f32[144,128]{1,0:T(8,128)S(1)}, u32[]{:S(2)}) copy-start(f32[144,128]{1,0:T(8,128)S(1)} %collective-permute-done.12.c_ref) | copy-start | bytes 221188
  114.9 0.6 copy-start.8

commit v4 on v3

--- a/solution.py
+++ b/solution.py
@@ -33,30 +33,24 @@
 
 
 def filter_matrix():
-    out = np.zeros((4, PLANES, 16, 5, 5, PLANES), np.float32)
+    out = np.zeros((4, 12 * PLANES, 5, 5, PLANES), np.float32)
     for s, d in enumerate(DILATIONS):
-        base = 4 * (s % 2)
         for j, (oz, ox, oy) in enumerate(ORDER_TRIPLES):
             plane_taps = np.outer(BASE_TAPS[ox], BASE_TAPS[oy])
             for c in range(5):
                 for z in range(PLANES):
+                    if s % 2 == 0:
+                        main, slot, other = j, z % 2, j - 8
+                    else:
+                        main, slot, other = j - 4, 1 - z % 2, j
+                    if 0 <= main < 8:
+                        row = 8 * z + main
+                    else:
+                        row = 8 * PLANES + z // 2 * 8 + slot * 4 + other
                     src = z + (c - 2) * d
                     if 0 <= src < PLANES:
-                        out[s, z, base + j, :, :, src] += BASE_TAPS[oz][c] * plane_taps
-    return out.reshape(4, PLANES * 16, 25 * PLANES)
-
-
-def feature_scale():
-    rows = [1.0 / math.sqrt(TAP_NORMS[a] * TAP_NORMS[b] * TAP_NORMS[c]) for a, b, c in ORDER_TRIPLES]
-    return np.tile(np.array(rows * 4, np.float32)[:, None], (1, COLS))
-
-
-def interleave_matrix():
-    out = np.zeros((FEAT, 8, 8, FEAT), np.float32)
-    for j in range(FEAT):
-        for c in range(8):
-            out[j, c, c, j] = 1.0
-    return out.reshape(8 * FEAT, 8 * FEAT)
+                        out[s, row, :, :, src] += BASE_TAPS[oz][c] * plane_taps
+    return out.reshape(4, 12 * PLANES, 25 * PLANES)
 
 
 def kernel(
@@ -65,7 +59,7 @@
     after_ref,
     left_ref,
     right_ref,
-    filt_ref,
+    filt_in,
     scale_ref,
     lhs_ref,
     prior_ref,
@@ -75,6 +69,8 @@
     feats,
     sec_ref,
     cnt_ref,
+    filt_ref,
+    semaphore,
 ):
     octet = pl.program_id(0)
     one_tile = jnp.where(lax.broadcasted_iota(jnp.int32, (16, COLS), 0) < 3, 1.0, 0.0)
@@ -82,6 +78,9 @@
 
     @pl.when(octet == 0)
     def _():
+        taps_copy = pltpu.make_async_copy(filt_in, filt_ref, semaphore)
+        taps_copy.start()
+
         def fill(x, get_row, left, right):
             for m in range(8):
                 row = get_row(m)
@@ -109,6 +108,7 @@
         lax.fori_loop(0, ROWS // 8, one_group, 0, unroll=2)
         sec_ref[...] = jnp.zeros_like(sec_ref)
         cnt_ref[...] = jnp.zeros_like(cnt_ref)
+        taps_copy.wait()
 
     def one_pair(pair, carry):
         x = octet * 8 + pair * 2
@@ -124,9 +124,18 @@
                 sides.append(jnp.concatenate(tiles, axis=0))
             rhs = jnp.concatenate(sides, axis=1)
             out = jnp.dot(filt_ref[s], rhs, preferred_element_type=jnp.float32)
-            blocks.append(out.reshape(PLANES, 16, 2 * COLS))
-        a, b, c, d = blocks
-        rows = [a[:, :8], a[:, 8:] + b[:, :8], b[:, 8:], c[:, :8], c[:, 8:] + d[:, :8], d[:, 8:]]
+            blocks.append(out)
+        low = lax.broadcasted_iota(jnp.int32, (PLANES // 2, 8, 2 * COLS), 1) < 4
+        rows = []
+        for first, second in (blocks[:2], blocks[2:]):
+            rows.append(first[: 8 * PLANES].reshape(PLANES, 8, 2 * COLS))
+            one = first[8 * PLANES :].reshape(PLANES // 2, 8, 2 * COLS)
+            two = second[8 * PLANES :].reshape(PLANES // 2, 8, 2 * COLS)
+            even = jnp.where(low, one, two)
+            odd = jnp.where(low, two, one)
+            odd = jnp.concatenate([odd[:, 4:], odd[:, :4]], axis=1)
+            rows.append(jnp.stack([even, odd], axis=1).reshape(PLANES, 8, 2 * COLS))
+            rows.append(second[: 8 * PLANES].reshape(PLANES, 8, 2 * COLS))
         whole = jnp.concatenate(rows, axis=1)
         for e in range(2):
             part = whole[:, :, e * COLS : (e + 1) * COLS] * scale_ref[...][None]
@@ -208,7 +217,7 @@
             moment_ref[m * FEAT : (m + 1) * FEAT] = both
 
 
-def prepare_kernel(weight_ref, mean_ref, factor_ref, order_ref, lhs_ref, prior_ref):
+def prepare_kernel(weight_ref, mean_ref, factor_ref, lhs_ref, prior_ref, scale_ref):
     logits = weight_ref[...]
     top = jnp.max(logits, axis=1, keepdims=True)
     log_total = jnp.log(jnp.sum(jnp.exp(logits - top), axis=1, keepdims=True)) + top
@@ -217,7 +226,15 @@
     )
     lane = lax.broadcasted_iota(jnp.int32, (FEAT, 256), 1)
     half = lax.broadcasted_iota(jnp.int32, (8, COLS), 0) < 4
-    order = order_ref[...]
+    to_row = lax.broadcasted_iota(jnp.int32, (8 * FEAT, 8 * FEAT), 0)
+    from_row = lax.broadcasted_iota(jnp.int32, (8 * FEAT, 8 * FEAT), 1)
+    wanted = (to_row & 7) * FEAT + (to_row >> 3)
+    order = jnp.where(wanted == from_row, 1.0, 0.0).astype(jnp.bfloat16)
+    feature = lax.broadcasted_iota(jnp.int32, (FEAT, COLS), 0)
+    for j, (oz, ox, oy) in enumerate(ORDER_TRIPLES):
+        value = 1.0 / math.sqrt(TAP_NORMS[oz] * TAP_NORMS[ox] * TAP_NORMS[oy])
+        scale = jnp.full((FEAT, COLS), value, jnp.float32) if j == 0 else jnp.where(lax.rem(feature, len(ORDER_TRIPLES)) == j, value, scale)
+    scale_ref[...] = scale
     for g in range(3):
         rows, priors = [], []
         for h in range(2):
@@ -248,18 +265,19 @@
 
 
 def prepare(log_weights, means, prec_factor):
-    order = jnp.asarray(interleave_matrix(), jnp.bfloat16)
     return pl.pallas_call(
         prepare_kernel,
-        in_specs=vmem_specs(4),
-        out_specs=vmem_specs(2),
+        in_specs=vmem_specs(3),
+        out_specs=vmem_specs(3),
         out_shape=[
             jax.ShapeDtypeStruct((COMP * FEAT * 4, DEEP), jnp.bfloat16),
             jax.ShapeDtypeStruct((3, 8, COLS), jnp.float32),
+            jax.ShapeDtypeStruct((FEAT, COLS), jnp.float32),
         ],
         cost_estimate=pl.CostEstimate(flops=10**8, bytes_accessed=2 * 10**6, transcendentals=2 * 10**4),
+        compiler_params=pltpu.CompilerParams(vmem_limit_bytes=8 * 2**20),
         name="prepare",
-    )(log_weights.reshape(1, COMP), means, prec_factor, order)
+    )(log_weights.reshape(1, COMP), means, prec_factor)
 
 
 def finish_kernel(a_ref, b_ref, c_ref, d_ref, weight_ref, mean_ref, cov_ref):
@@ -291,21 +309,21 @@
             jax.ShapeDtypeStruct((COMP, FEAT), jnp.float32),
             jax.ShapeDtypeStruct((COMP, FEAT, FEAT), jnp.float32),
         ],
+        compiler_params=pltpu.CompilerParams(vmem_limit_bytes=8 * 2**20),
         name="finish",
     )(*parts)
     return new_weights.reshape(COMP), new_means, new_cov
 
 
-def local_step(pieces, lhs, prior):
+def local_step(pieces, lhs, prior, scale):
     filt = jnp.asarray(filter_matrix(), jnp.bfloat16)
-    scale = jnp.asarray(feature_scale())
     full = lambda *shape: pl.BlockSpec(shape, lambda o: (0,) * len(shape))
     return pl.pallas_call(
         kernel,
         grid=(ROWS // 8,),
         in_specs=[
             *[full(*piece.shape) for piece in pieces],
-            full(*filt.shape),
+            pl.BlockSpec(memory_space=pltpu.HBM),
             full(*scale.shape),
             full(*lhs.shape),
             full(*prior.shape),
@@ -323,9 +341,11 @@
             pltpu.VMEM((8, PLANES, FEAT, COLS), jnp.bfloat16),
             pltpu.VMEM((COMP * FEAT, FEAT + 16), jnp.float32),
             pltpu.VMEM((COMP, 8, COLS), jnp.float32),
+            pltpu.VMEM(filt.shape, filt.dtype),
+            pltpu.SemaphoreType.DMA,
         ],
         compiler_params=pltpu.CompilerParams(
-            dimension_semantics=("arbitrary",), vmem_limit_bytes=50 * 2**20
+            dimension_semantics=("arbitrary",), vmem_limit_bytes=32 * 2**20
         ),
         name="mixture_step",
     )(*pieces, filt, scale, lhs, prior)
@@ -345,6 +365,7 @@
         in_specs=vmem_specs(1),
         out_specs=vmem_specs(2),
         out_shape=[shape, shape],
+        compiler_params=pltpu.CompilerParams(vmem_limit_bytes=8 * 2**20),
         name="pack",
     )(rows)
 
@@ -387,12 +408,11 @@
     rows = jnp.transpose(volume, (1, 0, 2))
     head, tail = pack(rows)
     left, right = neighbours(tail, head, "narrow")
-    lhs, prior = prepare(log_weights, means, prec_factor)
-    left, right, lhs = lax.optimization_barrier((left, right, lhs))
+    lhs, prior, scale = prepare(log_weights, means, prec_factor)
     bottom = jnp.concatenate([rows[ROWS - MARGIN :], left[6:], right[6:]], axis=0)
     top = jnp.concatenate([rows[:MARGIN], left[:2], right[:2]], axis=0)
     before, after = neighbours(bottom, top, "wide")
-    responsibility, moments = local_step((before, rows, after, left, right), lhs, prior)
+    responsibility, moments = local_step((before, rows, after, left, right), lhs, prior, scale)
     return (responsibility,) + finish(*device_sum(moments))
 
 

time: 118 us -> 107 us (0.907)
  Pallas kernels: 60.9 us -> 54.5 us
  local copies, waits for them, and re-layouts: 8.03 us -> 4.52 us
    unnamed x19 -> x9, local copies, waits for them, and re-layouts: 7.14 us -> 4.5 us
    pallas_call x1, Pallas kernels: 54.4 us -> 52.4 us  [local_step(): pl.pallas_call(kernel, grid=(ROWS // 8,), in_specs=[*[full(*piece.shape)...]
    pallas_call x1, Pallas kernels: 2.65 us -> 0.81 us  [prepare(): pl.pallas_call(prepare_kernel, in_specs=vmem_specs(3), out_specs=vmem_spe...]
    pallas_call x1, Pallas kernels: 1.76 us -> 0.18 us  [pack(): pl.pallas_call(pack_kernel, in_specs=vmem_specs(1), out_specs=vmem_specs(...]
  transfers between devices with their start and end apart: 14 -> 14, of which waited for: 12 -> 12; matrix products, arithmetic and copies ran while one was open for 1% -> 0% of each run, Pallas kernels for 2% -> 1%
where the time goes in v4:
time: 107 us
  Pallas kernels  54.5 us (51%)
  starting transfers between devices  26 us (24%)
  waiting for transfers between devices  21 us (20%)
  local copies, waits for them, and re-layouts  4.52 us (4%)
    pallas_call x1, Pallas kernels, local_step(): pl.pallas_call(kernel, grid=(ROWS // 8,), in_specs=[*[full(*piece.shape)...  52.4 us
    ppermute x6, waiting for transfers between devices, device_sum(): got.append(lax.ppermute(part, 'wide', perm))  10.4 us
    ppermute x6, starting transfers between devices, device_sum(): got.append(lax.ppermute(part, 'wide', perm))  9.93 us
    ppermute x2, starting transfers between devices, neighbours(): before = lax.ppermute(to_next, axis, [(i, i + 1) for i in range(ends)])  5.2 us
    ppermute x3, starting transfers between devices, device_sum(): lax.ppermute(part, 'narrow', [(i, (i + d) % 4) for i in range(4)])  5.07 us
    ppermute x2, waiting for transfers between devices, neighbours(): after = lax.ppermute(to_previous, axis, [(i + 1, i) for i in range(ends)])  4.82 us
    ppermute x3, waiting for transfers between devices, device_sum(): lax.ppermute(part, 'narrow', [(i, (i + d) % 4) for i in range(4)])  4.61 us
    unnamed x9, local copies, waits for them, and re-layouts  4.5 us
  transfers between devices with their start and end apart: 14, of which 12 were waited for; matrix products, arithmetic and copies ran while one was open for 0% of the time, Pallas kernels for 1%

profile of v4, /device:TPU:0, one launch (start us, length us, event | category | flops | bytes accessed | tf_op | source)
XLA Modules:
  0.0 106.7 jit_solution(4426836979053519601)
XLA Ops:
  0.6 1.1 %copy.11 = bf16[16,64,128]{2,0,1:T(8,128)(2,1)S(1)} copy(bf16[16,64,128]{2,1,0:T(8,128)(2,1)} %param.5) | data formatting | bytes 524288 | tf_op args[0]
  1.9 3.9 %collective-permute-start = (bf16[8,16,128]{2,1,0:T(8,128)(2,1)S(1)}, bf16[8,16,128]{2,1,0:T(8,128)(2,1)S(1)}, u32[]{:S(2)}, u32[]{:S(2)}) collective-permute-start(bf16[8,16,128]{2,1,0:T(8,128)(2,1)S(1)} %get-tuple-element.14), channel_id=1, source_target_pairs={{0,1},{1,2},{2,3},{4,5},{5,6},{6,7},{8,9},{9,10},{10,11},{12,13},{... | collective-permute-start | bytes 98312 | tf_op jit(solution)/shard_map/ppermute | solution.py:375
  5.9 1.3 %collective-permute-start.1 = (bf16[8,16,128]{2,1,0:T(8,128)(2,1)S(1)}, bf16[8,16,128]{2,1,0:T(8,128)(2,1)S(1)}, u32[]{:S(2)}, u32[]{:S(2)}) collective-permute-start(bf16[8,16,128]{2,1,0:T(8,128)(2,1)S(1)} %get-tuple-element.15), channel_id=1, source_target_pairs={{1,0},{2,1},{3,2},{5,4},{6,5},{7,6},{9,8},{10,9},{11,10},{13,12},{... | collective-permute-start | bytes 98312 | tf_op jit(solution)/shard_map/ppermute | solution.py:376
  7.2 0.3 collective-permute-done.left_ref
  7.4 4.2 %collective-permute-done.1.right_ref = bf16[8,16,128]{2,1,0:T(8,128)(2,1)S(1)} collective-permute-done((bf16[8,16,128]{2,1,0:T(8,128)(2,1)S(1)}, bf16[8,16,128]{2,1,0:T(8,128)(2,1)S(1)}, u32[]{:S(2)}, u32[]{:S(2)}) %collective-permute-start.1) | collective-permute-done | bytes 32800 | tf_op jit(solution)/shard_map/ppermute | solution.py:376
  11.7 1.3 %collective-permute-start.2 = (bf16[20,16,128]{2,1,0:T(8,128)(2,1)S(1)}, bf16[20,16,128]{2,1,0:T(8,128)(2,1)S(1)}, u32[]{:S(2)}, u32[]{:S(2)}) collective-permute-start(bf16[20,16,128]{2,1,0:T(8,128)(2,1)S(1)} %pad_maximum_fusion), channel_id=1, source_target_pairs={{0,4},{4,8},{8,12},{12,16},{16,20},{20,24},{24,28},{28,32},{32,36}... | collective-permute-start | bytes 245768 | tf_op jit(solution)/shard_map/ppermute | solution.py:375
  13.0 1.3 %collective-permute-start.3 = (bf16[20,16,128]{2,1,0:T(8,128)(2,1)S(1)}, bf16[20,16,128]{2,1,0:T(8,128)(2,1)S(1)}, u32[]{:S(2)}, u32[]{:S(2)}) collective-permute-start(bf16[20,16,128]{2,1,0:T(8,128)(2,1)S(1)} %pad_maximum_fusion.1), channel_id=1, source_target_pairs={{4,0},{8,4},{12,8},{16,12},{20,16},{24,20},{28,24},{32,28},{36,32}... | collective-permute-start | bytes 245768 | tf_op jit(solution)/shard_map/ppermute | solution.py:376
  14.3 0.9 copy-done.1
  15.2 0.7 copy-done.2
  15.9 0.7 copy-done.3
  16.6 0.8 prepare.1
  17.4 0.6 collective-permute-done.3.after_ref
  18.0 1.1 %copy-done = bf16[4,192,400]{2,1,0:T(8,128)(2,1)S(1)} copy-done((bf16[4,192,400]{2,1,0:T(8,128)(2,1)S(1)}, bf16[4,192,400]{2,1,0:T(8,128)(2,1)}, u32[]{:S(2)}) %copy-start) | copy-done | bytes 614424
  19.1 52.4 %mixture_step.1 = (f32[6,16,64,128]{3,2,1,0:T(8,128)}, f32[144,128]{1,0:T(8,128)S(1)}) custom-call(bf16[20,16,128]{2,1,0:T(8,128)(2,1)S(1)} %collective-permute-done.2.before_ref, bf16[64,16,128]{2,1,0:T(8,128)(2,1)S(1)} %bitcast.7, bf16[20,16,128]{2,1,0:T(8,128)(2,1)S(1)} %collective-permute-done.3.after_ref, ...), custom_call_target="tpu_custom_call" | custom-call | tf_op jit(solution)/shard_map/mixture_step/pallas_call | solution.py:321
  71.6 3.2 %collective-permute-start.4 = (f32[144,128]{1,0:T(8,128)S(1)}, f32[144,128]{1,0:T(8,128)S(1)}, u32[]{:S(2)}, u32[]{:S(2)}) collective-permute-start(f32[144,128]{1,0:T(8,128)S(1)} %get-tuple-element.20), channel_id=1, source_target_pairs={{0,4},{4,0},{8,12},{12,8},{16,20},{20,16},{24,28},{28,24},{32,36},... | collective-permute-start | bytes 221192 | tf_op jit(solution)/shard_map/ppermute | solution.py:389
  74.7 0.9 collective-permute-done.4
  75.7 1.9 %collective-permute-start.7 = (f32[144,128]{1,0:T(8,128)S(1)}, f32[144,128]{1,0:T(8,128)S(1)}, u32[]{:S(2)}, u32[]{:S(2)}) collective-permute-start(f32[144,128]{1,0:T(8,128)S(1)} %add.21), channel_id=1, source_target_pairs={{0,3},{1,0},{2,1},{3,2},{4,7},{5,4},{6,5},{7,6},{8,11},{9,8},{10,9... | collective-permute-start | bytes 221192 | tf_op jit(solution)/shard_map/ppermute | solution.py:391
  77.6 2.2 %collective-permute-start.6 = (f32[144,128]{1,0:T(8,128)S(1)}, f32[144,128]{1,0:T(8,128)S(1)}, u32[]{:S(2)}, u32[]{:S(2)}) collective-permute-start(f32[144,128]{1,0:T(8,128)S(1)} %add.21), channel_id=1, source_target_pairs={{0,2},{1,3},{2,0},{3,1},{4,6},{5,7},{6,4},{7,5},{8,10},{9,11},{10,... | collective-permute-start | bytes 221192 | tf_op jit(solution)/shard_map/ppermute | solution.py:391
  79.7 1.0 collective-permute-start.5
  80.7 3.5 %collective-permute-done.6 = f32[144,128]{1,0:T(8,128)S(1)} collective-permute-done((f32[144,128]{1,0:T(8,128)S(1)}, f32[144,128]{1,0:T(8,128)S(1)}, u32[]{:S(2)}, u32[]{:S(2)}) %collective-permute-start.6) | collective-permute-done | bytes 73760 | tf_op jit(solution)/shard_map/ppermute | solution.py:391
  84.2 1.1 %collective-permute-done.5 = f32[144,128]{1,0:T(8,128)S(1)} collective-permute-done((f32[144,128]{1,0:T(8,128)S(1)}, f32[144,128]{1,0:T(8,128)S(1)}, u32[]{:S(2)}, u32[]{:S(2)}) %collective-permute-start.5) | collective-permute-done | bytes 73760 | tf_op jit(solution)/shard_map/ppermute | solution.py:391
  85.4 4.8 %collective-permute-start.10 = (f32[144,128]{1,0:T(8,128)S(1)}, f32[144,128]{1,0:T(8,128)S(1)}, u32[]{:S(2)}, u32[]{:S(2)}) collective-permute-start(f32[144,128]{1,0:T(8,128)S(1)} %add_add_fusion.1), channel_id=1, source_target_pairs={{0,24},{4,28},{8,0},{12,4},{16,8},{20,12},{24,16},{28,20},{32,56},... | collective-permute-start | bytes 221192 | tf_op jit(solution)/shard_map/ppermute | solution.py:401
  90.1 0.9 collective-permute-start.8
  91.1 1.7 %collective-permute-done.10 = f32[144,128]{1,0:T(8,128)S(1)} collective-permute-done((f32[144,128]{1,0:T(8,128)S(1)}, f32[144,128]{1,0:T(8,128)S(1)}, u32[]{:S(2)}, u32[]{:S(2)}) %collective-permute-start.10) | collective-permute-done | bytes 73760 | tf_op jit(solution)/shard_map/ppermute | solution.py:401
  92.8 3.2 %collective-permute-done.9 = f32[144,128]{1,0:T(8,128)S(1)} collective-permute-done((f32[144,128]{1,0:T(8,128)S(1)}, f32[144,128]{1,0:T(8,128)S(1)}, u32[]{:S(2)}, u32[]{:S(2)}) %collective-permute-start.9) | collective-permute-done | bytes 73760 | tf_op jit(solution)/shard_map/ppermute | solution.py:401
  96.0 0.4 collective-permute-done.8
  96.5 1.0 collective-permute-start.13
  97.5 2.6 %collective-permute-start.12 = (f32[144,128]{1,0:T(8,128)S(1)}, f32[144,128]{1,0:T(8,128)S(1)}, u32[]{:S(2)}, u32[]{:S(2)}) collective-permute-start(f32[144,128]{1,0:T(8,128)S(1)} %add_add_fusion.a_ref), channel_id=1, source_target_pairs={{0,64},{4,68},{8,72},{12,76},{16,80},{20,84},{24,88},{28,92},{32,9... | collective-permute-start | bytes 221192 | tf_op jit(solution)/shard_map/ppermute | solution.py:401
  100.1 0.6 collective-permute-start.11
  100.9 2.5 %collective-permute-done.12.c_ref = f32[144,128]{1,0:T(8,128)S(1)} collective-permute-done((f32[144,128]{1,0:T(8,128)S(1)}, f32[144,128]{1,0:T(8,128)S(1)}, u32[]{:S(2)}, u32[]{:S(2)}) %collective-permute-start.12) | collective-permute-done | bytes 73760 | tf_op jit(solution)/shard_map/ppermute | solution.py:401
  103.4 2.3 %collective-permute-done.11.b_ref = f32[144,128]{1,0:T(8,128)S(1)} collective-permute-done((f32[144,128]{1,0:T(8,128)S(1)}, f32[144,128]{1,0:T(8,128)S(1)}, u32[]{:S(2)}, u32[]{:S(2)}) %collective-permute-start.11) | collective-permute-done | bytes 73760 | tf_op jit(solution)/shard_map/ppermute | solution.py:401
  105.7 1.0 finish.1
  (17 shorter events, 0.5 us)
Async XLA Ops:
  1.9 5.5 %collective-permute-start = (bf16[8,16,128]{2,1,0:T(8,128)(2,1)S(1)}, bf16[8,16,128]{2,1,0:T(8,128)(2,1)S(1)}, u32[]{:S(2)}, u32[]{:S(2)}) collective-permute-start(bf16[8,16,128]{2,1,0:T(8,128)(2,1)S(1)} %get-tuple-element.14), channel_id=1, source_target_pairs={{0,1},{1,2},{2,3},{4,5},{5,6},{6,7},{8,9},{9,10},{10,11},{12,13},{... | collective-permute-start | bytes 98312 | tf_op jit(solution)/shard_map/ppermute | solution.py:375
  5.9 5.8 %collective-permute-start.1 = (bf16[8,16,128]{2,1,0:T(8,128)(2,1)S(1)}, bf16[8,16,128]{2,1,0:T(8,128)(2,1)S(1)}, u32[]{:S(2)}, u32[]{:S(2)}) collective-permute-start(bf16[8,16,128]{2,1,0:T(8,128)(2,1)S(1)} %get-tuple-element.15), channel_id=1, source_target_pairs={{1,0},{2,1},{3,2},{5,4},{6,5},{7,6},{9,8},{10,9},{11,10},{13,12},{... | collective-permute-start | bytes 98312 | tf_op jit(solution)/shard_map/ppermute | solution.py:376
  11.7 5.7 %collective-permute-start.2 = (bf16[20,16,128]{2,1,0:T(8,128)(2,1)S(1)}, bf16[20,16,128]{2,1,0:T(8,128)(2,1)S(1)}, u32[]{:S(2)}, u32[]{:S(2)}) collective-permute-start(bf16[20,16,128]{2,1,0:T(8,128)(2,1)S(1)} %pad_maximum_fusion), channel_id=1, source_target_pairs={{0,4},{4,8},{8,12},{12,16},{16,20},{20,24},{24,28},{28,32},{32,36}... | collective-permute-start | bytes 245768 | tf_op jit(solution)/shard_map/ppermute | solution.py:375
  13.0 5.0 %collective-permute-start.3 = (bf16[20,16,128]{2,1,0:T(8,128)(2,1)S(1)}, bf16[20,16,128]{2,1,0:T(8,128)(2,1)S(1)}, u32[]{:S(2)}, u32[]{:S(2)}) collective-permute-start(bf16[20,16,128]{2,1,0:T(8,128)(2,1)S(1)} %pad_maximum_fusion.1), channel_id=1, source_target_pairs={{4,0},{8,4},{12,8},{16,12},{20,16},{24,20},{28,24},{32,28},{36,32}... | collective-permute-start | bytes 245768 | tf_op jit(solution)/shard_map/ppermute | solution.py:376
  14.3 0.9 copy-start.1
  15.2 0.7 copy-start.2
  15.9 0.7 copy-start.3
  18.0 1.1 %copy-start = (bf16[4,192,400]{2,1,0:T(8,128)(2,1)S(1)}, bf16[4,192,400]{2,1,0:T(8,128)(2,1)}, u32[]{:S(2)}) copy-start(bf16[4,192,400]{2,1,0:T(8,128)(2,1)} %constant.2.clone.filt_in) | copy-start | bytes 1843204
  71.6 4.1 %collective-permute-start.4 = (f32[144,128]{1,0:T(8,128)S(1)}, f32[144,128]{1,0:T(8,128)S(1)}, u32[]{:S(2)}, u32[]{:S(2)}) collective-permute-start(f32[144,128]{1,0:T(8,128)S(1)} %get-tuple-element.20), channel_id=1, source_target_pairs={{0,4},{4,0},{8,12},{12,8},{16,20},{20,16},{24,28},{28,24},{32,36},... | collective-permute-start | bytes 221192 | tf_op jit(solution)/shard_map/ppermute | solution.py:389
  75.7 5.1 %collective-permute-start.7 = (f32[144,128]{1,0:T(8,128)S(1)}, f32[144,128]{1,0:T(8,128)S(1)}, u32[]{:S(2)}, u32[]{:S(2)}) collective-permute-start(f32[144,128]{1,0:T(8,128)S(1)} %add.21), channel_id=1, source_target_pairs={{0,3},{1,0},{2,1},{3,2},{4,7},{5,4},{6,5},{7,6},{8,11},{9,8},{10,9... | collective-permute-start | bytes 221192 | tf_op jit(solution)/shard_map/ppermute | solution.py:391
  77.6 6.7 %collective-permute-start.6 = (f32[144,128]{1,0:T(8,128)S(1)}, f32[144,128]{1,0:T(8,128)S(1)}, u32[]{:S(2)}, u32[]{:S(2)}) collective-permute-start(f32[144,128]{1,0:T(8,128)S(1)} %add.21), channel_id=1, source_target_pairs={{0,2},{1,3},{2,0},{3,1},{4,6},{5,7},{6,4},{7,5},{8,10},{9,11},{10,... | collective-permute-start | bytes 221192 | tf_op jit(solution)/shard_map/ppermute | solution.py:391
  79.7 5.6 %collective-permute-start.5 = (f32[144,128]{1,0:T(8,128)S(1)}, f32[144,128]{1,0:T(8,128)S(1)}, u32[]{:S(2)}, u32[]{:S(2)}) collective-permute-start(f32[144,128]{1,0:T(8,128)S(1)} %add.21), channel_id=1, source_target_pairs={{0,1},{1,2},{2,3},{3,0},{4,5},{5,6},{6,7},{7,4},{8,9},{9,10},{10,1... | collective-permute-start | bytes 221192 | tf_op jit(solution)/shard_map/ppermute | solution.py:391
  85.4 7.4 %collective-permute-start.10 = (f32[144,128]{1,0:T(8,128)S(1)}, f32[144,128]{1,0:T(8,128)S(1)}, u32[]{:S(2)}, u32[]{:S(2)}) collective-permute-start(f32[144,128]{1,0:T(8,128)S(1)} %add_add_fusion.1), channel_id=1, source_target_pairs={{0,24},{4,28},{8,0},{12,4},{16,8},{20,12},{24,16},{28,20},{32,56},... | collective-permute-start | bytes 221192 | tf_op jit(solution)/shard_map/ppermute | solution.py:401
  90.1 5.9 %collective-permute-start.9 = (f32[144,128]{1,0:T(8,128)S(1)}, f32[144,128]{1,0:T(8,128)S(1)}, u32[]{:S(2)}, u32[]{:S(2)}) collective-permute-start(f32[144,128]{1,0:T(8,128)S(1)} %add_add_fusion.1), channel_id=1, source_target_pairs={{0,16},{4,20},{8,24},{12,28},{16,0},{20,4},{24,8},{28,12},{32,48},... | collective-permute-start | bytes 221192 | tf_op jit(solution)/shard_map/ppermute | solution.py:401
  90.1 6.4 %collective-permute-start.8 = (f32[144,128]{1,0:T(8,128)S(1)}, f32[144,128]{1,0:T(8,128)S(1)}, u32[]{:S(2)}, u32[]{:S(2)}) collective-permute-start(f32[144,128]{1,0:T(8,128)S(1)} %add_add_fusion.1), channel_id=1, source_target_pairs={{0,8},{4,12},{8,16},{12,20},{16,24},{20,28},{24,0},{28,4},{32,40},... | collective-permute-start | bytes 221192 | tf_op jit(solution)/shard_map/ppermute | solution.py:401
  96.5 4.4 %collective-permute-start.13 = (f32[144,128]{1,0:T(8,128)S(1)}, f32[144,128]{1,0:T(8,128)S(1)}, u32[]{:S(2)}, u32[]{:S(2)}) collective-permute-start(f32[144,128]{1,0:T(8,128)S(1)} %add_add_fusion.a_ref), channel_id=1, source_target_pairs={{0,96},{4,100},{8,104},{12,108},{16,112},{20,116},{24,120},{28,124... | collective-permute-start | bytes 221192 | tf_op jit(solution)/shard_map/ppermute | solution.py:401
  97.5 5.9 %collective-permute-start.12 = (f32[144,128]{1,0:T(8,128)S(1)}, f32[144,128]{1,0:T(8,128)S(1)}, u32[]{:S(2)}, u32[]{:S(2)}) collective-permute-start(f32[144,128]{1,0:T(8,128)S(1)} %add_add_fusion.a_ref), channel_id=1, source_target_pairs={{0,64},{4,68},{8,72},{12,76},{16,80},{20,84},{24,88},{28,92},{32,9... | collective-permute-start | bytes 221192 | tf_op jit(solution)/shard_map/ppermute | solution.py:401
  100.1 5.6 %collective-permute-start.11 = (f32[144,128]{1,0:T(8,128)S(1)}, f32[144,128]{1,0:T(8,128)S(1)}, u32[]{:S(2)}, u32[]{:S(2)}) collective-permute-start(f32[144,128]{1,0:T(8,128)S(1)} %add_add_fusion.a_ref), channel_id=1, source_target_pairs={{0,32},{4,36},{8,40},{12,44},{16,48},{20,52},{24,56},{28,60},{32,6... | collective-permute-start | bytes 221192 | tf_op jit(solution)/shard_map/ppermute | solution.py:401

commit v5 on v4

--- a/solution.py
+++ b/solution.py
@@ -208,13 +208,22 @@
 
     @pl.when(octet == pl.num_programs(0) - 1)
     def _():
-        lane = lax.broadcasted_iota(jnp.int32, (FEAT, 128), 1)
+        half = FEAT // 2
+        row = lax.broadcasted_iota(jnp.int32, (half, 64), 0)
+        lane = lax.broadcasted_iota(jnp.int32, (half, 64), 1)
+        packed = []
+        for k in range(COMP):
+            upper = sec_ref[k * FEAT : k * FEAT + half]
+            lower = sec_ref[k * FEAT + half : (k + 1) * FEAT]
+            first = lower[:, FEAT : FEAT + 1]
+            diagonal = jnp.sum(jnp.where(lane == row + half, lower, 0.0), axis=1, keepdims=True)
+            block = jnp.where(lane < row, jnp.concatenate([lower[:, half:], lower[:, :half]], axis=1), upper)
+            block = jnp.where(lane == FEAT + 1, first, block)
+            block = jnp.where(lane == FEAT + 2, diagonal, block)
+            packed.append(jnp.where(lane == FEAT + 3, jnp.sum(cnt_ref[k]), block))
         for m in range(3):
-            first, second = [sec_ref[k * FEAT : (k + 1) * FEAT] for k in (2 * m, 2 * m + 1)]
-            both = jnp.concatenate([first, second], axis=1)
-            both = jnp.where(lane == FEAT + 1, jnp.sum(cnt_ref[2 * m]), both)
-            both = jnp.where(lane == 64 + FEAT + 1, jnp.sum(cnt_ref[2 * m + 1]), both)
-            moment_ref[m * FEAT : (m + 1) * FEAT] = both
+            both = jnp.concatenate(packed[2 * m : 2 * m + 2], axis=1)
+            moment_ref[m * half : (m + 1) * half] = both
 
 
 def prepare_kernel(weight_ref, mean_ref, factor_ref, lhs_ref, prior_ref, scale_ref):
@@ -280,21 +289,35 @@
     )(log_weights.reshape(1, COMP), means, prec_factor)
 
 
+def pick(block, column):
+    lane = lax.broadcasted_iota(jnp.int32, block.shape, 1)
+    return jnp.sum(jnp.where(lane == column, block, 0.0), axis=1, keepdims=True)
+
+
 def finish_kernel(a_ref, b_ref, c_ref, d_ref, weight_ref, mean_ref, cov_ref):
-    on_diagonal = lax.broadcasted_iota(jnp.int32, (FEAT, FEAT), 0) == lax.broadcasted_iota(
-        jnp.int32, (FEAT, FEAT), 1
-    )
+    half = FEAT // 2
+    row = lax.broadcasted_iota(jnp.int32, (FEAT, FEAT), 0)
+    col = lax.broadcasted_iota(jnp.int32, (FEAT, FEAT), 1)
+    stored = ((row < half) & (col >= row)) | ((row >= half) & (col >= half) & (col < row))
     lane = lax.broadcasted_iota(jnp.int32, (1, COMP), 1)
     counts = jnp.zeros((1, COMP), jnp.float32)
     for k in range(COMP):
-        at = slice(k // 2 * FEAT, (k // 2 + 1) * FEAT)
+        at = slice(k // 2 * half, (k // 2 + 1) * half)
         both = (a_ref[at] + b_ref[at]) + (c_ref[at] + d_ref[at])
-        block = both[:, k % 2 * 64 : k % 2 * 64 + 64]
-        count = block[:1, FEAT + 1 : FEAT + 2]
-        column = block[:, FEAT : FEAT + 1] / count
-        row = jnp.sum(jnp.where(on_diagonal, column, 0.0), axis=0, keepdims=True)
-        cov_ref[k] = block[:, :FEAT] / count - column * row
-        mean_ref[k : k + 1] = row
+        block = both if k % 2 == 0 else pltpu.roll(both, 64, 1)
+        upper = block[:, :FEAT]
+        lower = pltpu.roll(block, half, 1)[:, :FEAT]
+        second = jnp.concatenate([upper, lower], axis=0)
+        second = jnp.where(stored, second, second.T)
+        diagonal = pick(block, FEAT + 2)
+        diagonal = jnp.concatenate([diagonal, diagonal], axis=0)
+        second = jnp.where((row == col) & (row >= half), diagonal, second)
+        first = jnp.concatenate([pick(block, FEAT), pick(block, FEAT + 1)], axis=0)
+        count = pick(block, FEAT + 3)[:1]
+        column = first / count
+        across = jnp.sum(jnp.where(row == col, column, 0.0), axis=0, keepdims=True)
+        cov_ref[k] = second / count - column * across
+        mean_ref[k : k + 1] = across
         counts = jnp.where(lane == k, count, counts)
     weight_ref[...] = counts / jnp.sum(counts, axis=1, keepdims=True)
 
@@ -330,11 +353,11 @@
         ],
         out_specs=[
             pl.BlockSpec((COMP, PLANES, 8, COLS), lambda o: (0, 0, o, 0)),
-            full(3 * FEAT, 128),
+            full(3 * FEAT // 2, 128),
         ],
         out_shape=[
             jax.ShapeDtypeStruct((COMP, PLANES, ROWS, COLS), jnp.float32),
-            jax.ShapeDtypeStruct((3 * FEAT, 128), jnp.float32),
+            jax.ShapeDtypeStruct((3 * FEAT // 2, 128), jnp.float32),
         ],
         scratch_shapes=[
             pltpu.VMEM((len(SHIFTS), ROWS + 2 * MARGIN, PLANES, COLS), jnp.bfloat16),

time: 107 us -> 106 us (level)
  waiting for transfers between devices: 21 us -> 19.3 us
    ppermute x6, waiting for transfers between devices: 10.4 us -> 9.19 us  [device_sum(): got.append(lax.ppermute(part, 'wide', perm))]
  transfers between devices with their start and end apart: 14 -> 14, of which waited for: 12 -> 10; matrix products, arithmetic and copies ran while one was open for 0% -> 0% of each run, Pallas kernels for 1% -> 1%
where the time goes in v5:
time: 106 us; the launch traced here: 105 us
  Pallas kernels  55 us (52%)
  starting transfers between devices  25.9 us (24%)
  waiting for transfers between devices  19.3 us (18%)
  local copies, waits for them, and re-layouts  4.52 us (4%)
    pallas_call x1, Pallas kernels, local_step(): pl.pallas_call(kernel, grid=(ROWS // 8,), in_specs=[*[full(*piece.shape)...  52.6 us
    ppermute x6, starting transfers between devices, device_sum(): got.append(lax.ppermute(part, 'wide', perm))  9.93 us
    ppermute x6, waiting for transfers between devices, device_sum(): got.append(lax.ppermute(part, 'wide', perm))  9.19 us
    ppermute x2, starting transfers between devices, neighbours(): before = lax.ppermute(to_next, axis, [(i, i + 1) for i in range(ends)])  5.2 us
    ppermute x3, starting transfers between devices, device_sum(): lax.ppermute(part, 'narrow', [(i, (i + d) % 4) for i in range(4)])  5 us
    ppermute x2, waiting for transfers between devices, neighbours(): after = lax.ppermute(to_previous, axis, [(i + 1, i) for i in range(ends)])  4.82 us
    unnamed x9, local copies, waits for them, and re-layouts  4.5 us
    ppermute x3, waiting for transfers between devices, device_sum(): lax.ppermute(part, 'narrow', [(i, (i + d) % 4) for i in range(4)])  4.16 us
  transfers between devices with their start and end apart: 14, of which 10 were waited for; matrix products, arithmetic and copies ran while one was open for 0% of the time, Pallas kernels for 1%

profile of v5, /device:TPU:0, one launch (start us, length us, event | category | flops | bytes accessed | tf_op | source)
XLA Modules:
  0.0 105.5 jit_solution(16789911885121610093)
XLA Ops:
  0.6 1.1 %copy.11 = bf16[16,64,128]{2,0,1:T(8,128)(2,1)S(1)} copy(bf16[16,64,128]{2,1,0:T(8,128)(2,1)} %param.5) | data formatting | bytes 524288 | tf_op args[0]
  1.8 0.2 pack.1
  1.9 3.9 %collective-permute-start = (bf16[8,16,128]{2,1,0:T(8,128)(2,1)S(1)}, bf16[8,16,128]{2,1,0:T(8,128)(2,1)S(1)}, u32[]{:S(2)}, u32[]{:S(2)}) collective-permute-start(bf16[8,16,128]{2,1,0:T(8,128)(2,1)S(1)} %get-tuple-element.14), channel_id=1, source_target_pairs={{0,1},{1,2},{2,3},{4,5},{5,6},{6,7},{8,9},{9,10},{10,11},{12,13},{... | collective-permute-start | bytes 98312 | tf_op jit(solution)/shard_map/ppermute | solution.py:398
  5.9 1.3 %collective-permute-start.1 = (bf16[8,16,128]{2,1,0:T(8,128)(2,1)S(1)}, bf16[8,16,128]{2,1,0:T(8,128)(2,1)S(1)}, u32[]{:S(2)}, u32[]{:S(2)}) collective-permute-start(bf16[8,16,128]{2,1,0:T(8,128)(2,1)S(1)} %get-tuple-element.15), channel_id=1, source_target_pairs={{1,0},{2,1},{3,2},{5,4},{6,5},{7,6},{9,8},{10,9},{11,10},{13,12},{... | collective-permute-start | bytes 98312 | tf_op jit(solution)/shard_map/ppermute | solution.py:399
  7.2 0.3 collective-permute-done.left_ref
  7.4 4.2 %collective-permute-done.1.right_ref = bf16[8,16,128]{2,1,0:T(8,128)(2,1)S(1)} collective-permute-done((bf16[8,16,128]{2,1,0:T(8,128)(2,1)S(1)}, bf16[8,16,128]{2,1,0:T(8,128)(2,1)S(1)}, u32[]{:S(2)}, u32[]{:S(2)}) %collective-permute-start.1) | collective-permute-done | bytes 32800 | tf_op jit(solution)/shard_map/ppermute | solution.py:399
  11.7 1.3 %collective-permute-start.2 = (bf16[20,16,128]{2,1,0:T(8,128)(2,1)S(1)}, bf16[20,16,128]{2,1,0:T(8,128)(2,1)S(1)}, u32[]{:S(2)}, u32[]{:S(2)}) collective-permute-start(bf16[20,16,128]{2,1,0:T(8,128)(2,1)S(1)} %pad_maximum_fusion), channel_id=1, source_target_pairs={{0,4},{4,8},{8,12},{12,16},{16,20},{20,24},{24,28},{28,32},{32,36}... | collective-permute-start | bytes 245768 | tf_op jit(solution)/shard_map/ppermute | solution.py:398
  13.0 1.3 %collective-permute-start.3 = (bf16[20,16,128]{2,1,0:T(8,128)(2,1)S(1)}, bf16[20,16,128]{2,1,0:T(8,128)(2,1)S(1)}, u32[]{:S(2)}, u32[]{:S(2)}) collective-permute-start(bf16[20,16,128]{2,1,0:T(8,128)(2,1)S(1)} %pad_maximum_fusion.1), channel_id=1, source_target_pairs={{4,0},{8,4},{12,8},{16,12},{20,16},{24,20},{28,24},{32,28},{36,32}... | collective-permute-start | bytes 245768 | tf_op jit(solution)/shard_map/ppermute | solution.py:399
  14.3 0.9 copy-done.1
  15.2 0.7 copy-done.2
  15.9 0.7 copy-done.3
  16.6 0.8 prepare.1
  17.4 0.6 collective-permute-done.3.after_ref
  18.0 1.1 %copy-done = bf16[4,192,400]{2,1,0:T(8,128)(2,1)S(1)} copy-done((bf16[4,192,400]{2,1,0:T(8,128)(2,1)S(1)}, bf16[4,192,400]{2,1,0:T(8,128)(2,1)}, u32[]{:S(2)}) %copy-start) | copy-done | bytes 614424
  19.1 52.6 %mixture_step.1 = (f32[6,16,64,128]{3,2,1,0:T(8,128)}, f32[72,128]{1,0:T(8,128)S(1)}) custom-call(bf16[20,16,128]{2,1,0:T(8,128)(2,1)S(1)} %collective-permute-done.2.before_ref, bf16[64,16,128]{2,1,0:T(8,128)(2,1)S(1)} %bitcast.7, bf16[20,16,128]{2,1,0:T(8,128)(2,1)S(1)} %collective-permute-done.3.after_ref, ...), custom_call_target="tpu_custom_call" | custom-call | tf_op jit(solution)/shard_map/mixture_step/pallas_call | solution.py:344
  71.8 3.2 %collective-permute-start.4 = (f32[72,128]{1,0:T(8,128)S(1)}, f32[72,128]{1,0:T(8,128)S(1)}, u32[]{:S(2)}, u32[]{:S(2)}) collective-permute-start(f32[72,128]{1,0:T(8,128)S(1)} %get-tuple-element.20), channel_id=1, source_target_pairs={{0,4},{4,0},{8,12},{12,8},{16,20},{20,16},{24,28},{28,24},{32,36},... | collective-permute-start | bytes 110600 | tf_op jit(solution)/shard_map/ppermute | solution.py:412
  75.0 0.9 collective-permute-done.4
  75.8 1.8 %collective-permute-start.7 = (f32[72,128]{1,0:T(8,128)S(1)}, f32[72,128]{1,0:T(8,128)S(1)}, u32[]{:S(2)}, u32[]{:S(2)}) collective-permute-start(f32[72,128]{1,0:T(8,128)S(1)} %add.21), channel_id=1, source_target_pairs={{0,3},{1,0},{2,1},{3,2},{4,7},{5,4},{6,5},{7,6},{8,11},{9,8},{10,9... | collective-permute-start | bytes 110600 | tf_op jit(solution)/shard_map/ppermute | solution.py:414
  77.7 2.2 %collective-permute-start.6 = (f32[72,128]{1,0:T(8,128)S(1)}, f32[72,128]{1,0:T(8,128)S(1)}, u32[]{:S(2)}, u32[]{:S(2)}) collective-permute-start(f32[72,128]{1,0:T(8,128)S(1)} %add.21), channel_id=1, source_target_pairs={{0,2},{1,3},{2,0},{3,1},{4,6},{5,7},{6,4},{7,5},{8,10},{9,11},{10,... | collective-permute-start | bytes 110600 | tf_op jit(solution)/shard_map/ppermute | solution.py:414
  79.8 1.0 collective-permute-start.5
  80.8 2.6 %collective-permute-done.6 = f32[72,128]{1,0:T(8,128)S(1)} collective-permute-done((f32[72,128]{1,0:T(8,128)S(1)}, f32[72,128]{1,0:T(8,128)S(1)}, u32[]{:S(2)}, u32[]{:S(2)}) %collective-permute-start.6) | collective-permute-done | bytes 36896 | tf_op jit(solution)/shard_map/ppermute | solution.py:414
  83.4 1.6 %collective-permute-done.5 = f32[72,128]{1,0:T(8,128)S(1)} collective-permute-done((f32[72,128]{1,0:T(8,128)S(1)}, f32[72,128]{1,0:T(8,128)S(1)}, u32[]{:S(2)}, u32[]{:S(2)}) %collective-permute-start.5) | collective-permute-done | bytes 36896 | tf_op jit(solution)/shard_map/ppermute | solution.py:414
  85.0 4.8 %collective-permute-start.10 = (f32[72,128]{1,0:T(8,128)S(1)}, f32[72,128]{1,0:T(8,128)S(1)}, u32[]{:S(2)}, u32[]{:S(2)}) collective-permute-start(f32[72,128]{1,0:T(8,128)S(1)} %add_add_fusion.1), channel_id=1, source_target_pairs={{0,24},{4,28},{8,0},{12,4},{16,8},{20,12},{24,16},{28,20},{32,56},... | collective-permute-start | bytes 110600 | tf_op jit(solution)/shard_map/ppermute | solution.py:424
  89.8 0.9 collective-permute-start.8
  90.7 0.7 collective-permute-done.10
  91.4 3.9 %collective-permute-done.9 = f32[72,128]{1,0:T(8,128)S(1)} collective-permute-done((f32[72,128]{1,0:T(8,128)S(1)}, f32[72,128]{1,0:T(8,128)S(1)}, u32[]{:S(2)}, u32[]{:S(2)}) %collective-permute-start.9) | collective-permute-done | bytes 36896 | tf_op jit(solution)/shard_map/ppermute | solution.py:424
  95.4 1.4 %collective-permute-start.13 = (f32[72,128]{1,0:T(8,128)S(1)}, f32[72,128]{1,0:T(8,128)S(1)}, u32[]{:S(2)}, u32[]{:S(2)}) collective-permute-start(f32[72,128]{1,0:T(8,128)S(1)} %add_add_fusion.a_ref), channel_id=1, source_target_pairs={{0,96},{4,100},{8,104},{12,108},{16,112},{20,116},{24,120},{28,124... | collective-permute-start | bytes 110600 | tf_op jit(solution)/shard_map/ppermute | solution.py:424
  96.7 2.3 %collective-permute-start.12 = (f32[72,128]{1,0:T(8,128)S(1)}, f32[72,128]{1,0:T(8,128)S(1)}, u32[]{:S(2)}, u32[]{:S(2)}) collective-permute-start(f32[72,128]{1,0:T(8,128)S(1)} %add_add_fusion.a_ref), channel_id=1, source_target_pairs={{0,64},{4,68},{8,72},{12,76},{16,80},{20,84},{24,88},{28,92},{32,9... | collective-permute-start | bytes 110600 | tf_op jit(solution)/shard_map/ppermute | solution.py:424
  99.0 0.6 collective-permute-start.11
  99.6 2.6 %collective-permute-done.12.c_ref = f32[72,128]{1,0:T(8,128)S(1)} collective-permute-done((f32[72,128]{1,0:T(8,128)S(1)}, f32[72,128]{1,0:T(8,128)S(1)}, u32[]{:S(2)}, u32[]{:S(2)}) %collective-permute-start.12) | collective-permute-done | bytes 36896 | tf_op jit(solution)/shard_map/ppermute | solution.py:424
  102.2 2.0 %collective-permute-done.11.b_ref = f32[72,128]{1,0:T(8,128)S(1)} collective-permute-done((f32[72,128]{1,0:T(8,128)S(1)}, f32[72,128]{1,0:T(8,128)S(1)}, u32[]{:S(2)}, u32[]{:S(2)}) %collective-permute-start.11) | collective-permute-done | bytes 36896 | tf_op jit(solution)/shard_map/ppermute | solution.py:424
  104.1 1.3 %finish.1 = (f32[1,6]{1,0:T(1,128)}, f32[6,48]{1,0:T(8,128)}, f32[6,48,48]{2,1,0:T(8,128)}) custom-call(f32[72,128]{1,0:T(8,128)S(1)} %add_add_fusion.a_ref, f32[72,128]{1,0:T(8,128)S(1)} %collective-permute-done.11.b_ref, f32[72,128]{1,0:T(8,128)S(1)} %collective-permute-done.12.c_ref, f32[72,128]{1,0:T(8,128)S(1)} %collective-permute-done.13.d_ref), custom_call_target="tpu_custom_call" | custom-call | tf_op jit(solution)/shard_map/finish/pallas_call | solution.py:326
  (17 shorter events, 0.1 us)
Async XLA Ops:
  1.9 5.5 %collective-permute-start = (bf16[8,16,128]{2,1,0:T(8,128)(2,1)S(1)}, bf16[8,16,128]{2,1,0:T(8,128)(2,1)S(1)}, u32[]{:S(2)}, u32[]{:S(2)}) collective-permute-start(bf16[8,16,128]{2,1,0:T(8,128)(2,1)S(1)} %get-tuple-element.14), channel_id=1, source_target_pairs={{0,1},{1,2},{2,3},{4,5},{5,6},{6,7},{8,9},{9,10},{10,11},{12,13},{... | collective-permute-start | bytes 98312 | tf_op jit(solution)/shard_map/ppermute | solution.py:398
  5.9 5.8 %collective-permute-start.1 = (bf16[8,16,128]{2,1,0:T(8,128)(2,1)S(1)}, bf16[8,16,128]{2,1,0:T(8,128)(2,1)S(1)}, u32[]{:S(2)}, u32[]{:S(2)}) collective-permute-start(bf16[8,16,128]{2,1,0:T(8,128)(2,1)S(1)} %get-tuple-element.15), channel_id=1, source_target_pairs={{1,0},{2,1},{3,2},{5,4},{6,5},{7,6},{9,8},{10,9},{11,10},{13,12},{... | collective-permute-start | bytes 98312 | tf_op jit(solution)/shard_map/ppermute | solution.py:399
  11.7 5.7 %collective-permute-start.2 = (bf16[20,16,128]{2,1,0:T(8,128)(2,1)S(1)}, bf16[20,16,128]{2,1,0:T(8,128)(2,1)S(1)}, u32[]{:S(2)}, u32[]{:S(2)}) collective-permute-start(bf16[20,16,128]{2,1,0:T(8,128)(2,1)S(1)} %pad_maximum_fusion), channel_id=1, source_target_pairs={{0,4},{4,8},{8,12},{12,16},{16,20},{20,24},{24,28},{28,32},{32,36}... | collective-permute-start | bytes 245768 | tf_op jit(solution)/shard_map/ppermute | solution.py:398
  13.0 5.0 %collective-permute-start.3 = (bf16[20,16,128]{2,1,0:T(8,128)(2,1)S(1)}, bf16[20,16,128]{2,1,0:T(8,128)(2,1)S(1)}, u32[]{:S(2)}, u32[]{:S(2)}) collective-permute-start(bf16[20,16,128]{2,1,0:T(8,128)(2,1)S(1)} %pad_maximum_fusion.1), channel_id=1, source_target_pairs={{4,0},{8,4},{12,8},{16,12},{20,16},{24,20},{28,24},{32,28},{36,32}... | collective-permute-start | bytes 245768 | tf_op jit(solution)/shard_map/ppermute | solution.py:399
  14.3 0.9 copy-start.1
  15.2 0.7 copy-start.2
  15.9 0.7 copy-start.3
  18.0 1.1 %copy-start = (bf16[4,192,400]{2,1,0:T(8,128)(2,1)S(1)}, bf16[4,192,400]{2,1,0:T(8,128)(2,1)}, u32[]{:S(2)}) copy-start(bf16[4,192,400]{2,1,0:T(8,128)(2,1)} %constant.2.clone.filt_in) | copy-start | bytes 1843204
  71.8 4.0 %collective-permute-start.4 = (f32[72,128]{1,0:T(8,128)S(1)}, f32[72,128]{1,0:T(8,128)S(1)}, u32[]{:S(2)}, u32[]{:S(2)}) collective-permute-start(f32[72,128]{1,0:T(8,128)S(1)} %get-tuple-element.20), channel_id=1, source_target_pairs={{0,4},{4,0},{8,12},{12,8},{16,20},{20,16},{24,28},{28,24},{32,36},... | collective-permute-start | bytes 110600 | tf_op jit(solution)/shard_map/ppermute | solution.py:412
  75.8 5.0 %collective-permute-start.7 = (f32[72,128]{1,0:T(8,128)S(1)}, f32[72,128]{1,0:T(8,128)S(1)}, u32[]{:S(2)}, u32[]{:S(2)}) collective-permute-start(f32[72,128]{1,0:T(8,128)S(1)} %add.21), channel_id=1, source_target_pairs={{0,3},{1,0},{2,1},{3,2},{4,7},{5,4},{6,5},{7,6},{8,11},{9,8},{10,9... | collective-permute-start | bytes 110600 | tf_op jit(solution)/shard_map/ppermute | solution.py:414
  77.7 5.7 %collective-permute-start.6 = (f32[72,128]{1,0:T(8,128)S(1)}, f32[72,128]{1,0:T(8,128)S(1)}, u32[]{:S(2)}, u32[]{:S(2)}) collective-permute-start(f32[72,128]{1,0:T(8,128)S(1)} %add.21), channel_id=1, source_target_pairs={{0,2},{1,3},{2,0},{3,1},{4,6},{5,7},{6,4},{7,5},{8,10},{9,11},{10,... | collective-permute-start | bytes 110600 | tf_op jit(solution)/shard_map/ppermute | solution.py:414
  79.8 5.2 %collective-permute-start.5 = (f32[72,128]{1,0:T(8,128)S(1)}, f32[72,128]{1,0:T(8,128)S(1)}, u32[]{:S(2)}, u32[]{:S(2)}) collective-permute-start(f32[72,128]{1,0:T(8,128)S(1)} %add.21), channel_id=1, source_target_pairs={{0,1},{1,2},{2,3},{3,0},{4,5},{5,6},{6,7},{7,4},{8,9},{9,10},{10,1... | collective-permute-start | bytes 110600 | tf_op jit(solution)/shard_map/ppermute | solution.py:414
  85.0 6.4 %collective-permute-start.10 = (f32[72,128]{1,0:T(8,128)S(1)}, f32[72,128]{1,0:T(8,128)S(1)}, u32[]{:S(2)}, u32[]{:S(2)}) collective-permute-start(f32[72,128]{1,0:T(8,128)S(1)} %add_add_fusion.1), channel_id=1, source_target_pairs={{0,24},{4,28},{8,0},{12,4},{16,8},{20,12},{24,16},{28,20},{32,56},... | collective-permute-start | bytes 110600 | tf_op jit(solution)/shard_map/ppermute | solution.py:424
  89.8 5.6 %collective-permute-start.9 = (f32[72,128]{1,0:T(8,128)S(1)}, f32[72,128]{1,0:T(8,128)S(1)}, u32[]{:S(2)}, u32[]{:S(2)}) collective-permute-start(f32[72,128]{1,0:T(8,128)S(1)} %add_add_fusion.1), channel_id=1, source_target_pairs={{0,16},{4,20},{8,24},{12,28},{16,0},{20,4},{24,8},{28,12},{32,48},... | collective-permute-start | bytes 110600 | tf_op jit(solution)/shard_map/ppermute | solution.py:424
  89.8 5.6 %collective-permute-start.8 = (f32[72,128]{1,0:T(8,128)S(1)}, f32[72,128]{1,0:T(8,128)S(1)}, u32[]{:S(2)}, u32[]{:S(2)}) collective-permute-start(f32[72,128]{1,0:T(8,128)S(1)} %add_add_fusion.1), channel_id=1, source_target_pairs={{0,8},{4,12},{8,16},{12,20},{16,24},{20,28},{24,0},{28,4},{32,40},... | collective-permute-start | bytes 110600 | tf_op jit(solution)/shard_map/ppermute | solution.py:424
  95.4 4.2 %collective-permute-start.13 = (f32[72,128]{1,0:T(8,128)S(1)}, f32[72,128]{1,0:T(8,128)S(1)}, u32[]{:S(2)}, u32[]{:S(2)}) collective-permute-start(f32[72,128]{1,0:T(8,128)S(1)} %add_add_fusion.a_ref), channel_id=1, source_target_pairs={{0,96},{4,100},{8,104},{12,108},{16,112},{20,116},{24,120},{28,124... | collective-permute-start | bytes 110600 | tf_op jit(solution)/shard_map/ppermute | solution.py:424
  96.7 5.5 %collective-permute-start.12 = (f32[72,128]{1,0:T(8,128)S(1)}, f32[72,128]{1,0:T(8,128)S(1)}, u32[]{:S(2)}, u32[]{:S(2)}) collective-permute-start(f32[72,128]{1,0:T(8,128)S(1)} %add_add_fusion.a_ref), channel_id=1, source_target_pairs={{0,64},{4,68},{8,72},{12,76},{16,80},{20,84},{24,88},{28,92},{32,9... | collective-permute-start | bytes 110600 | tf_op jit(solution)/shard_map/ppermute | solution.py:424
  99.0 5.2 %collective-permute-start.11 = (f32[72,128]{1,0:T(8,128)S(1)}, f32[72,128]{1,0:T(8,128)S(1)}, u32[]{:S(2)}, u32[]{:S(2)}) collective-permute-start(f32[72,128]{1,0:T(8,128)S(1)} %add_add_fusion.a_ref), channel_id=1, source_target_pairs={{0,32},{4,36},{8,40},{12,44},{16,48},{20,52},{24,56},{28,60},{32,6... | collective-permute-start | bytes 110600 | tf_op jit(solution)/shard_map/ppermute | solution.py:424

commit v6 on v5

--- a/solution.py
+++ b/solution.py
@@ -409,11 +409,13 @@
 
 
 def device_sum(part):
-    part = part + lax.ppermute(part, "wide", wide_perm(lambda x, y, c: (x, y, 1 - c)))
-    narrow = [
-        lax.ppermute(part, "narrow", [(i, (i + d) % 4) for i in range(4)]) for d in (1, 2, 3)
-    ]
-    part = ((part + narrow[0]) + (narrow[1] + narrow[2]))
+    got = []
+    for c in range(2):
+        for d in range(4):
+            if c + d:
+                perm = [(4 * w + n, 4 * (w ^ c) + (n + d) % 4) for w in range(32) for n in range(4)]
+                got.append(lax.ppermute(part, ("wide", "narrow"), perm))
+    part = (part + got[0]) + (got[1] + got[2]) + ((got[3] + got[4]) + (got[5] + got[6]))
     for axis in range(2):
         got = []
         for d in (1, 2, 3):

time: 106 us -> 108 us (1.019)
  starting transfers between devices: 25.9 us -> 28.4 us
    ppermute x4 -> x7, starting transfers between devices: 8.17 us -> 10.7 us  [device_sum(): got.append(lax.ppermute(part, ('wide', 'narrow'), perm))]
    ppermute x4 -> x7, waiting for transfers between devices: 5.02 us -> 4.93 us  [device_sum(): got.append(lax.ppermute(part, ('wide', 'narrow'), perm))]
  transfers between devices with their start and end apart: 14 -> 17, of which waited for: 10 -> 12; matrix products, arithmetic and copies ran while one was open for 0% -> 0% of each run, Pallas kernels for 1% -> 1%
where the time goes in v6:
time: 108 us
  Pallas kernels  55 us (51%)
  starting transfers between devices  28.4 us (26%)
  waiting for transfers between devices  19.2 us (18%)
  local copies, waits for them, and re-layouts  4.52 us (4%)
    pallas_call x1, Pallas kernels, local_step(): pl.pallas_call(kernel, grid=(ROWS // 8,), in_specs=[*[full(*piece.shape)...  52.6 us
    ppermute x7, starting transfers between devices, device_sum(): got.append(lax.ppermute(part, ('wide', 'narrow'), perm))  10.7 us
    ppermute x6, starting transfers between devices, device_sum(): got.append(lax.ppermute(part, 'wide', perm))  9.94 us
    ppermute x6, waiting for transfers between devices, device_sum(): got.append(lax.ppermute(part, 'wide', perm))  9.19 us
    ppermute x2, starting transfers between devices, neighbours(): before = lax.ppermute(to_next, axis, [(i, i + 1) for i in range(ends)])  5.2 us
    ppermute x7, waiting for transfers between devices, device_sum(): got.append(lax.ppermute(part, ('wide', 'narrow'), perm))  4.93 us
    ppermute x2, waiting for transfers between devices, neighbours(): after = lax.ppermute(to_previous, axis, [(i + 1, i) for i in range(ends)])  4.82 us
    unnamed x9, local copies, waits for them, and re-layouts  4.5 us
  transfers between devices with their start and end apart: 17, of which 12 were waited for; matrix products, arithmetic and copies ran while one was open for 0% of the time, Pallas kernels for 1%

profile of v6, /device:TPU:0, one launch (start us, length us, event | category | flops | bytes accessed | tf_op | source)
XLA Modules:
  0.0 107.9 jit_solution(7294858059354681641)
XLA Ops:
  0.6 1.1 %copy.11 = bf16[16,64,128]{2,0,1:T(8,128)(2,1)S(1)} copy(bf16[16,64,128]{2,1,0:T(8,128)(2,1)} %param.5) | data formatting | bytes 524288 | tf_op args[0]
  1.9 3.9 %collective-permute-start = (bf16[8,16,128]{2,1,0:T(8,128)(2,1)S(1)}, bf16[8,16,128]{2,1,0:T(8,128)(2,1)S(1)}, u32[]{:S(2)}, u32[]{:S(2)}) collective-permute-start(bf16[8,16,128]{2,1,0:T(8,128)(2,1)S(1)} %get-tuple-element.14), channel_id=1, source_target_pairs={{0,1},{1,2},{2,3},{4,5},{5,6},{6,7},{8,9},{9,10},{10,11},{12,13},{... | collective-permute-start | bytes 98312 | tf_op jit(solution)/shard_map/ppermute | solution.py:398
  5.9 1.3 %collective-permute-start.1 = (bf16[8,16,128]{2,1,0:T(8,128)(2,1)S(1)}, bf16[8,16,128]{2,1,0:T(8,128)(2,1)S(1)}, u32[]{:S(2)}, u32[]{:S(2)}) collective-permute-start(bf16[8,16,128]{2,1,0:T(8,128)(2,1)S(1)} %get-tuple-element.15), channel_id=1, source_target_pairs={{1,0},{2,1},{3,2},{5,4},{6,5},{7,6},{9,8},{10,9},{11,10},{13,12},{... | collective-permute-start | bytes 98312 | tf_op jit(solution)/shard_map/ppermute | solution.py:399
  7.4 4.2 %collective-permute-done.1.right_ref = bf16[8,16,128]{2,1,0:T(8,128)(2,1)S(1)} collective-permute-done((bf16[8,16,128]{2,1,0:T(8,128)(2,1)S(1)}, bf16[8,16,128]{2,1,0:T(8,128)(2,1)S(1)}, u32[]{:S(2)}, u32[]{:S(2)}) %collective-permute-start.1) | collective-permute-done | bytes 32800 | tf_op jit(solution)/shard_map/ppermute | solution.py:399
  11.7 1.3 %collective-permute-start.2 = (bf16[20,16,128]{2,1,0:T(8,128)(2,1)S(1)}, bf16[20,16,128]{2,1,0:T(8,128)(2,1)S(1)}, u32[]{:S(2)}, u32[]{:S(2)}) collective-permute-start(bf16[20,16,128]{2,1,0:T(8,128)(2,1)S(1)} %pad_maximum_fusion), channel_id=1, source_target_pairs={{0,4},{4,8},{8,12},{12,16},{16,20},{20,24},{24,28},{28,32},{32,36}... | collective-permute-start | bytes 245768 | tf_op jit(solution)/shard_map/ppermute | solution.py:398
  13.0 1.3 %collective-permute-start.3 = (bf16[20,16,128]{2,1,0:T(8,128)(2,1)S(1)}, bf16[20,16,128]{2,1,0:T(8,128)(2,1)S(1)}, u32[]{:S(2)}, u32[]{:S(2)}) collective-permute-start(bf16[20,16,128]{2,1,0:T(8,128)(2,1)S(1)} %pad_maximum_fusion.1), channel_id=1, source_target_pairs={{4,0},{8,4},{12,8},{16,12},{20,16},{24,20},{28,24},{32,28},{36,32}... | collective-permute-start | bytes 245768 | tf_op jit(solution)/shard_map/ppermute | solution.py:399
  14.3 0.9 copy-done.1
  15.2 0.7 copy-done.2
  15.9 0.7 copy-done.3
  16.6 0.8 prepare.1
  17.4 0.6 collective-permute-done.3.after_ref
  18.0 1.1 %copy-done = bf16[4,192,400]{2,1,0:T(8,128)(2,1)S(1)} copy-done((bf16[4,192,400]{2,1,0:T(8,128)(2,1)S(1)}, bf16[4,192,400]{2,1,0:T(8,128)(2,1)}, u32[]{:S(2)}) %copy-start) | copy-done | bytes 614424
  19.1 52.6 %mixture_step.1 = (f32[6,16,64,128]{3,2,1,0:T(8,128)}, f32[72,128]{1,0:T(8,128)S(1)}) custom-call(bf16[20,16,128]{2,1,0:T(8,128)(2,1)S(1)} %collective-permute-done.2.before_ref, bf16[64,16,128]{2,1,0:T(8,128)(2,1)S(1)} %bitcast.7, bf16[20,16,128]{2,1,0:T(8,128)(2,1)S(1)} %collective-permute-done.3.after_ref, ...), custom_call_target="tpu_custom_call" | custom-call | tf_op jit(solution)/shard_map/mixture_step/pallas_call | solution.py:344
  71.8 4.6 %collective-permute-start.10 = (f32[72,128]{1,0:T(8,128)S(1)}, f32[72,128]{1,0:T(8,128)S(1)}, u32[]{:S(2)}, u32[]{:S(2)}) collective-permute-start(f32[72,128]{1,0:T(8,128)S(1)} %get-tuple-element.20), channel_id=1, source_target_pairs={{0,7},{1,4},{2,5},{3,6},{4,3},{5,0},{6,1},{7,2},{8,15},{9,12},{10,... | collective-permute-start | bytes 110600 | tf_op jit(solution)/shard_map/ppermute | solution.py:417
  76.4 1.8 %collective-permute-start.9 = (f32[72,128]{1,0:T(8,128)S(1)}, f32[72,128]{1,0:T(8,128)S(1)}, u32[]{:S(2)}, u32[]{:S(2)}) collective-permute-start(f32[72,128]{1,0:T(8,128)S(1)} %get-tuple-element.20), channel_id=1, source_target_pairs={{0,6},{1,7},{2,4},{3,5},{4,2},{5,3},{6,0},{7,1},{8,14},{9,15},{10,... | collective-permute-start | bytes 110600 | tf_op jit(solution)/shard_map/ppermute | solution.py:417
  78.2 1.0 collective-permute-start.8
  79.3 2.3 %collective-permute-start.6 = (f32[72,128]{1,0:T(8,128)S(1)}, f32[72,128]{1,0:T(8,128)S(1)}, u32[]{:S(2)}, u32[]{:S(2)}) collective-permute-start(f32[72,128]{1,0:T(8,128)S(1)} %get-tuple-element.20), channel_id=1, source_target_pairs={{0,3},{1,0},{2,1},{3,2},{4,7},{5,4},{6,5},{7,6},{8,11},{9,8},{10,9... | collective-permute-start | bytes 110600 | tf_op jit(solution)/shard_map/ppermute | solution.py:417
  81.7 0.7 collective-permute-start.4
  82.5 0.3 collective-permute-done.8
  82.8 0.9 collective-permute-done.6
  83.7 3.3 %collective-permute-done.5 = f32[72,128]{1,0:T(8,128)S(1)} collective-permute-done((f32[72,128]{1,0:T(8,128)S(1)}, f32[72,128]{1,0:T(8,128)S(1)}, u32[]{:S(2)}, u32[]{:S(2)}) %collective-permute-start.5) | collective-permute-done | bytes 36896 | tf_op jit(solution)/shard_map/ppermute | solution.py:417
  87.1 0.3 collective-permute-done.4
  87.4 4.8 %collective-permute-start.13 = (f32[72,128]{1,0:T(8,128)S(1)}, f32[72,128]{1,0:T(8,128)S(1)}, u32[]{:S(2)}, u32[]{:S(2)}) collective-permute-start(f32[72,128]{1,0:T(8,128)S(1)} %add_add_fusion.1), channel_id=1, source_target_pairs={{0,24},{4,28},{8,0},{12,4},{16,8},{20,12},{24,16},{28,20},{32,56},... | collective-permute-start | bytes 110600 | tf_op jit(solution)/shard_map/ppermute | solution.py:426
  92.2 0.9 collective-permute-start.11
  93.1 0.7 collective-permute-done.13
  93.8 3.9 %collective-permute-done.12 = f32[72,128]{1,0:T(8,128)S(1)} collective-permute-done((f32[72,128]{1,0:T(8,128)S(1)}, f32[72,128]{1,0:T(8,128)S(1)}, u32[]{:S(2)}, u32[]{:S(2)}) %collective-permute-start.12) | collective-permute-done | bytes 36896 | tf_op jit(solution)/shard_map/ppermute | solution.py:426
  97.8 1.4 %collective-permute-start.16 = (f32[72,128]{1,0:T(8,128)S(1)}, f32[72,128]{1,0:T(8,128)S(1)}, u32[]{:S(2)}, u32[]{:S(2)}) collective-permute-start(f32[72,128]{1,0:T(8,128)S(1)} %add_add_fusion.a_ref), channel_id=1, source_target_pairs={{0,96},{4,100},{8,104},{12,108},{16,112},{20,116},{24,120},{28,124... | collective-permute-start | bytes 110600 | tf_op jit(solution)/shard_map/ppermute | solution.py:426
  99.2 2.2 %collective-permute-start.15 = (f32[72,128]{1,0:T(8,128)S(1)}, f32[72,128]{1,0:T(8,128)S(1)}, u32[]{:S(2)}, u32[]{:S(2)}) collective-permute-start(f32[72,128]{1,0:T(8,128)S(1)} %add_add_fusion.a_ref), channel_id=1, source_target_pairs={{0,64},{4,68},{8,72},{12,76},{16,80},{20,84},{24,88},{28,92},{32,9... | collective-permute-start | bytes 110600 | tf_op jit(solution)/shard_map/ppermute | solution.py:426
  101.4 0.6 collective-permute-start.14
  102.0 2.6 %collective-permute-done.15.c_ref = f32[72,128]{1,0:T(8,128)S(1)} collective-permute-done((f32[72,128]{1,0:T(8,128)S(1)}, f32[72,128]{1,0:T(8,128)S(1)}, u32[]{:S(2)}, u32[]{:S(2)}) %collective-permute-start.15) | collective-permute-done | bytes 36896 | tf_op jit(solution)/shard_map/ppermute | solution.py:426
  104.6 2.0 %collective-permute-done.14.b_ref = f32[72,128]{1,0:T(8,128)S(1)} collective-permute-done((f32[72,128]{1,0:T(8,128)S(1)}, f32[72,128]{1,0:T(8,128)S(1)}, u32[]{:S(2)}, u32[]{:S(2)}) %collective-permute-start.14) | collective-permute-done | bytes 36896 | tf_op jit(solution)/shard_map/ppermute | solution.py:426
  106.6 1.3 %finish.1 = (f32[1,6]{1,0:T(1,128)}, f32[6,48]{1,0:T(8,128)}, f32[6,48,48]{2,1,0:T(8,128)}) custom-call(f32[72,128]{1,0:T(8,128)S(1)} %add_add_fusion.a_ref, f32[72,128]{1,0:T(8,128)S(1)} %collective-permute-done.14.b_ref, f32[72,128]{1,0:T(8,128)S(1)} %collective-permute-done.15.c_ref, f32[72,128]{1,0:T(8,128)S(1)} %collective-permute-done.16.d_ref), custom_call_target="tpu_custom_call" | custom-call | tf_op jit(solution)/shard_map/finish/pallas_call | solution.py:326
  (22 shorter events, 0.8 us)
Async XLA Ops:
  1.9 5.5 %collective-permute-start = (bf16[8,16,128]{2,1,0:T(8,128)(2,1)S(1)}, bf16[8,16,128]{2,1,0:T(8,128)(2,1)S(1)}, u32[]{:S(2)}, u32[]{:S(2)}) collective-permute-start(bf16[8,16,128]{2,1,0:T(8,128)(2,1)S(1)} %get-tuple-element.14), channel_id=1, source_target_pairs={{0,1},{1,2},{2,3},{4,5},{5,6},{6,7},{8,9},{9,10},{10,11},{12,13},{... | collective-permute-start | bytes 98312 | tf_op jit(solution)/shard_map/ppermute | solution.py:398
  5.9 5.8 %collective-permute-start.1 = (bf16[8,16,128]{2,1,0:T(8,128)(2,1)S(1)}, bf16[8,16,128]{2,1,0:T(8,128)(2,1)S(1)}, u32[]{:S(2)}, u32[]{:S(2)}) collective-permute-start(bf16[8,16,128]{2,1,0:T(8,128)(2,1)S(1)} %get-tuple-element.15), channel_id=1, source_target_pairs={{1,0},{2,1},{3,2},{5,4},{6,5},{7,6},{9,8},{10,9},{11,10},{13,12},{... | collective-permute-start | bytes 98312 | tf_op jit(solution)/shard_map/ppermute | solution.py:399
  11.7 5.7 %collective-permute-start.2 = (bf16[20,16,128]{2,1,0:T(8,128)(2,1)S(1)}, bf16[20,16,128]{2,1,0:T(8,128)(2,1)S(1)}, u32[]{:S(2)}, u32[]{:S(2)}) collective-permute-start(bf16[20,16,128]{2,1,0:T(8,128)(2,1)S(1)} %pad_maximum_fusion), channel_id=1, source_target_pairs={{0,4},{4,8},{8,12},{12,16},{16,20},{20,24},{24,28},{28,32},{32,36}... | collective-permute-start | bytes 245768 | tf_op jit(solution)/shard_map/ppermute | solution.py:398
  13.0 5.0 %collective-permute-start.3 = (bf16[20,16,128]{2,1,0:T(8,128)(2,1)S(1)}, bf16[20,16,128]{2,1,0:T(8,128)(2,1)S(1)}, u32[]{:S(2)}, u32[]{:S(2)}) collective-permute-start(bf16[20,16,128]{2,1,0:T(8,128)(2,1)S(1)} %pad_maximum_fusion.1), channel_id=1, source_target_pairs={{4,0},{8,4},{12,8},{16,12},{20,16},{24,20},{28,24},{32,28},{36,32}... | collective-permute-start | bytes 245768 | tf_op jit(solution)/shard_map/ppermute | solution.py:399
  14.3 0.9 copy-start.1
  15.2 0.7 copy-start.2
  15.9 0.7 copy-start.3
  18.0 1.1 %copy-start = (bf16[4,192,400]{2,1,0:T(8,128)(2,1)S(1)}, bf16[4,192,400]{2,1,0:T(8,128)(2,1)}, u32[]{:S(2)}) copy-start(bf16[4,192,400]{2,1,0:T(8,128)(2,1)} %constant.2.clone.filt_in) | copy-start | bytes 1843204
  71.8 9.8 %collective-permute-start.10 = (f32[72,128]{1,0:T(8,128)S(1)}, f32[72,128]{1,0:T(8,128)S(1)}, u32[]{:S(2)}, u32[]{:S(2)}) collective-permute-start(f32[72,128]{1,0:T(8,128)S(1)} %get-tuple-element.20), channel_id=1, source_target_pairs={{0,7},{1,4},{2,5},{3,6},{4,3},{5,0},{6,1},{7,2},{8,15},{9,12},{10,... | collective-permute-start | bytes 110600 | tf_op jit(solution)/shard_map/ppermute | solution.py:417
  76.4 5.4 %collective-permute-start.9 = (f32[72,128]{1,0:T(8,128)S(1)}, f32[72,128]{1,0:T(8,128)S(1)}, u32[]{:S(2)}, u32[]{:S(2)}) collective-permute-start(f32[72,128]{1,0:T(8,128)S(1)} %get-tuple-element.20), channel_id=1, source_target_pairs={{0,6},{1,7},{2,4},{3,5},{4,2},{5,3},{6,0},{7,1},{8,14},{9,15},{10,... | collective-permute-start | bytes 110600 | tf_op jit(solution)/shard_map/ppermute | solution.py:417
  78.2 4.6 %collective-permute-start.8 = (f32[72,128]{1,0:T(8,128)S(1)}, f32[72,128]{1,0:T(8,128)S(1)}, u32[]{:S(2)}, u32[]{:S(2)}) collective-permute-start(f32[72,128]{1,0:T(8,128)S(1)} %get-tuple-element.20), channel_id=1, source_target_pairs={{0,5},{1,6},{2,7},{3,4},{4,1},{5,2},{6,3},{7,0},{8,13},{9,14},{10,... | collective-permute-start | bytes 110600 | tf_op jit(solution)/shard_map/ppermute | solution.py:417
  79.3 3.5 %collective-permute-start.7 = (f32[72,128]{1,0:T(8,128)S(1)}, f32[72,128]{1,0:T(8,128)S(1)}, u32[]{:S(2)}, u32[]{:S(2)}) collective-permute-start(f32[72,128]{1,0:T(8,128)S(1)} %get-tuple-element.20), channel_id=1, source_target_pairs={{0,4},{1,5},{2,6},{3,7},{4,0},{5,1},{6,2},{7,3},{8,12},{9,13},{10,... | collective-permute-start | bytes 110600 | tf_op jit(solution)/shard_map/ppermute | solution.py:417
  79.3 4.5 %collective-permute-start.6 = (f32[72,128]{1,0:T(8,128)S(1)}, f32[72,128]{1,0:T(8,128)S(1)}, u32[]{:S(2)}, u32[]{:S(2)}) collective-permute-start(f32[72,128]{1,0:T(8,128)S(1)} %get-tuple-element.20), channel_id=1, source_target_pairs={{0,3},{1,0},{2,1},{3,2},{4,7},{5,4},{6,5},{7,6},{8,11},{9,8},{10,9... | collective-permute-start | bytes 110600 | tf_op jit(solution)/shard_map/ppermute | solution.py:417
  81.6 5.5 %collective-permute-start.5 = (f32[72,128]{1,0:T(8,128)S(1)}, f32[72,128]{1,0:T(8,128)S(1)}, u32[]{:S(2)}, u32[]{:S(2)}) collective-permute-start(f32[72,128]{1,0:T(8,128)S(1)} %get-tuple-element.20), channel_id=1, source_target_pairs={{0,2},{1,3},{2,0},{3,1},{4,6},{5,7},{6,4},{7,5},{8,10},{9,11},{10,... | collective-permute-start | bytes 110600 | tf_op jit(solution)/shard_map/ppermute | solution.py:417
  81.7 5.7 %collective-permute-start.4 = (f32[72,128]{1,0:T(8,128)S(1)}, f32[72,128]{1,0:T(8,128)S(1)}, u32[]{:S(2)}, u32[]{:S(2)}) collective-permute-start(f32[72,128]{1,0:T(8,128)S(1)} %get-tuple-element.20), channel_id=1, source_target_pairs={{0,1},{1,2},{2,3},{3,0},{4,5},{5,6},{6,7},{7,4},{8,9},{9,10},{10,1... | collective-permute-start | bytes 110600 | tf_op jit(solution)/shard_map/ppermute | solution.py:417
  87.4 6.4 %collective-permute-start.13 = (f32[72,128]{1,0:T(8,128)S(1)}, f32[72,128]{1,0:T(8,128)S(1)}, u32[]{:S(2)}, u32[]{:S(2)}) collective-permute-start(f32[72,128]{1,0:T(8,128)S(1)} %add_add_fusion.1), channel_id=1, source_target_pairs={{0,24},{4,28},{8,0},{12,4},{16,8},{20,12},{24,16},{28,20},{32,56},... | collective-permute-start | bytes 110600 | tf_op jit(solution)/shard_map/ppermute | solution.py:426
  92.2 5.5 %collective-permute-start.12 = (f32[72,128]{1,0:T(8,128)S(1)}, f32[72,128]{1,0:T(8,128)S(1)}, u32[]{:S(2)}, u32[]{:S(2)}) collective-permute-start(f32[72,128]{1,0:T(8,128)S(1)} %add_add_fusion.1), channel_id=1, source_target_pairs={{0,16},{4,20},{8,24},{12,28},{16,0},{20,4},{24,8},{28,12},{32,48},... | collective-permute-start | bytes 110600 | tf_op jit(solution)/shard_map/ppermute | solution.py:426
  92.2 5.6 %collective-permute-start.11 = (f32[72,128]{1,0:T(8,128)S(1)}, f32[72,128]{1,0:T(8,128)S(1)}, u32[]{:S(2)}, u32[]{:S(2)}) collective-permute-start(f32[72,128]{1,0:T(8,128)S(1)} %add_add_fusion.1), channel_id=1, source_target_pairs={{0,8},{4,12},{8,16},{12,20},{16,24},{20,28},{24,0},{28,4},{32,40},... | collective-permute-start | bytes 110600 | tf_op jit(solution)/shard_map/ppermute | solution.py:426
  97.8 4.2 %collective-permute-start.16 = (f32[72,128]{1,0:T(8,128)S(1)}, f32[72,128]{1,0:T(8,128)S(1)}, u32[]{:S(2)}, u32[]{:S(2)}) collective-permute-start(f32[72,128]{1,0:T(8,128)S(1)} %add_add_fusion.a_ref), channel_id=1, source_target_pairs={{0,96},{4,100},{8,104},{12,108},{16,112},{20,116},{24,120},{28,124... | collective-permute-start | bytes 110600 | tf_op jit(solution)/shard_map/ppermute | solution.py:426
  99.2 5.5 %collective-permute-start.15 = (f32[72,128]{1,0:T(8,128)S(1)}, f32[72,128]{1,0:T(8,128)S(1)}, u32[]{:S(2)}, u32[]{:S(2)}) collective-permute-start(f32[72,128]{1,0:T(8,128)S(1)} %add_add_fusion.a_ref), channel_id=1, source_target_pairs={{0,64},{4,68},{8,72},{12,76},{16,80},{20,84},{24,88},{28,92},{32,9... | collective-permute-start | bytes 110600 | tf_op jit(solution)/shard_map/ppermute | solution.py:426
  101.4 5.2 %collective-permute-start.14 = (f32[72,128]{1,0:T(8,128)S(1)}, f32[72,128]{1,0:T(8,128)S(1)}, u32[]{:S(2)}, u32[]{:S(2)}) collective-permute-start(f32[72,128]{1,0:T(8,128)S(1)} %add_add_fusion.a_ref), channel_id=1, source_target_pairs={{0,32},{4,36},{8,40},{12,44},{16,48},{20,52},{24,56},{28,60},{32,6... | collective-permute-start | bytes 110600 | tf_op jit(solution)/shard_map/ppermute | solution.py:426
